TPU v7x, 512 devices: a whole 4x8x8 slice. The times are simulated.
512 devices in a mesh: segment: 2 (over core), rows: 128 (over z, y_lo, x), mp: 2 (over y_hi).
Axes of the slice: x: 4, y: 8 (y_hi: 2, y_lo: 4; y = y_hi * 4 + y_lo), z: 8, core: 2. Of those that a mesh axis runs over, the one named last changes fastest.
Arguments:
- start_state: bfloat16 [8192, 2048], P('rows', 'mp'), may hold values from -6 to 6
- expert_ids: int32 [3, 8192, 8], P(None, 'rows'), may hold values from 0 to 127, all different within a row; in each aligned block of 64 rows (0 to 63, 64 to 127, ..., all dimensions but the last counted through in order) at most 8 rows name the same one
- norm_gain: float32 [2048], P('mp'), may hold values from 0.1 to 1.9
- w_router: bfloat16 [2048, 128], P('mp'), may hold values from -0.125 to 0.125
- w_gate: bfloat16 [128, 2048, 384], P('rows', None, 'mp'), may hold values from -0.125 to 0.125
- w_up: bfloat16 [128, 2048, 384], P('rows', None, 'mp'), may hold values from -0.125 to 0.125
- w_down: bfloat16 [128, 384, 2048], P('rows', 'mp'), may hold values from -0.3125 to 0.3125
- w_in: bfloat16 [2048, 1024], P(None, 'mp'), may hold values from -0.125 to 0.125
- trans_taps: float32 [4, 1024], P(None, 'mp'), may hold values from -4 to 4
- dw_kernels: float32 [2, 7, 1024], P(None, None, 'mp'), may hold values from -2.5 to 2.5
- ln_gain: float32 [2, 1024], P(None, 'mp'), may hold values from 0.1 to 1.9
- ln_bias: float32 [2, 1024], P(None, 'mp'), may hold values from -3 to 3
- w_out: float32 [1024], P('mp'), may hold values from -0.1875 to 0.1875
Outputs:
- talker_state: bfloat16 [8192, 2048], P('rows', 'mp')
- audio: float32 [2, 3, 16384], P('segment', None, 'rows')
Inputs may be any that keep to these rules, and one draw needn't show every extreme that they name: `expert_ids`: each frame names 8 different experts. In each pass no expert is named by more than 8 rows of one aligned block of 64 rows, and in some blocks one is named by exactly 8.
All inputs are finite; a program needn't handle non-finite values.
Results may differ from a plain program's by a relative error of at most 0.014.
Values may be sent and summed in bfloat16 or wider, within the bound.
No kernel may reach another device: no remote copies, remote signals or barrier semaphores. Data moves between devices by JAX's collectives and lax.ppermute only.
A program may use at most 64 MiB of HBM per device.

v0:
```python
import jax
import jax.numpy as jnp
from jax import lax
from jax.sharding import PartitionSpec as P

D = 2048
C = 1024


def passed_along(block, axis, distance):
    devices = range(lax.axis_size(axis))
    route = [(i - distance, i) for i in devices if i - distance in devices]
    return lax.ppermute(block, axis, route)


def upsample(frames, before, taps):
    current = frames.astype(jnp.float32)
    earlier = jnp.concatenate([before.astype(jnp.float32), current[:-1]], axis=0)
    even_rows = taps[0] * current + taps[2] * earlier
    odd_rows = taps[1] * current + taps[3] * earlier
    return (
        jnp.stack([even_rows, odd_rows], axis=1).reshape(-1, frames.shape[1]).astype(jnp.bfloat16)
    )


def mix_layer(padded, signal, kernel_taps, gain, shift_bias, dilation):
    length = signal.shape[0]
    reach = (kernel_taps.shape[0] - 1) * dilation
    mixed = jnp.zeros(signal.shape, jnp.float32)
    for tap_index in range(kernel_taps.shape[0]):
        start_row = reach - tap_index * dilation
        mixed = mixed + kernel_taps[tap_index] * padded[start_row : start_row + length]
    totals = lax.psum((jnp.sum(mixed, axis=1), jnp.sum(mixed * mixed, axis=1)), "mp")
    center = totals[0] / C
    spread = totals[1] / C - center * center
    normed = (mixed - center[:, None]) * lax.rsqrt(spread + 1e-06)[:, None]
    return (signal.astype(jnp.float32) + normed * gain + shift_bias).astype(jnp.bfloat16)


def on_device(
    start_state,
    expert_ids,
    norm_gain,
    w_router,
    w_gate,
    w_up,
    w_down,
    w_in,
    trans_taps,
    dw_kernels,
    ln_gain,
    ln_bias,
    w_out,
):
    row_count = start_state.shape[0]
    experts = w_router.shape[1]
    topk_count = expert_ids.shape[2]
    step_count = expert_ids.shape[0]
    layers = dw_kernels.shape[0]
    kernel = dw_kernels.shape[1]
    capacity = min(row_count, max(2, 2 * row_count * topk_count // experts))
    pair_count = row_count * topk_count
    slot_count = experts * capacity
    talker = lax.axis_index("segment") == 0
    hidden = start_state
    arrived = jnp.zeros_like(start_state)
    carried = arrived
    sounds = []
    for tick_index in range(step_count + 1):
        if tick_index > 0:
            full_rows = lax.all_gather(carried, "mp", axis=1, tiled=True)
            projected = jnp.dot(full_rows, w_in, preferred_element_type=jnp.float32).astype(
                jnp.bfloat16
            )
            before = passed_along(projected[-1:], "rows", 1)
            signal = upsample(projected, before, trans_taps)
            for layer_index in range(layers):
                dilation = 3**layer_index
                reach = (kernel - 1) * dilation
                rim_rows = passed_along(signal[-reach:], "rows", 1)
                padded = jnp.concatenate([rim_rows, signal], axis=0).astype(jnp.float32)
                signal = mix_layer(
                    padded,
                    signal,
                    dw_kernels[layer_index],
                    ln_gain[layer_index],
                    ln_bias[layer_index],
                    dilation,
                )
            rendered = lax.psum(jnp.sum(signal.astype(jnp.float32) * w_out, axis=1), "mp")
            sounds.append(jnp.where(talker, jnp.zeros_like(rendered), rendered))
        if tick_index < step_count:
            step_ids = expert_ids[tick_index]
            hidden_f = hidden.astype(jnp.float32)
            squares = lax.psum(jnp.sum(hidden_f * hidden_f, axis=1), "mp")
            normed = (hidden_f * lax.rsqrt(squares / D + 1e-06)[:, None] * norm_gain).astype(
                jnp.bfloat16
            )
            logits = lax.psum(
                jnp.dot(normed, w_router, preferred_element_type=jnp.float32).astype(jnp.bfloat16),
                "mp",
            ).astype(jnp.float32)
            picked = step_ids[:, :, None] == jnp.arange(experts, dtype=jnp.int32)[None, None, :]
            chosen = jnp.sum(jnp.where(picked, logits[:, None, :], 0.0), axis=2)
            squashed = jax.nn.sigmoid(chosen)
            weights = squashed / jnp.sum(squashed, axis=1, keepdims=True)
            flat_ids = step_ids.reshape(pair_count)
            one_hot = (flat_ids[:, None] == jnp.arange(experts, dtype=jnp.int32)[None, :]).astype(
                jnp.int32
            )
            earlier = jnp.cumsum(one_hot, axis=0) - one_hot
            position = jnp.sum(earlier * one_hot, axis=1)
            target = flat_ids * capacity + position
            placed = (target[:, None] == jnp.arange(slot_count, dtype=jnp.int32)[None, :]).reshape(
                row_count, topk_count, slot_count
            )
            dispatch = jnp.any(placed, axis=1).astype(jnp.bfloat16)
            combine_map = jnp.sum(jnp.where(placed, weights[:, :, None], 0.0), axis=1)
            outgoing = jnp.einsum("rs,rd->sd", dispatch, normed, preferred_element_type=jnp.float32)
            outgoing = outgoing.astype(jnp.bfloat16).reshape(experts, capacity, normed.shape[1])
            received = lax.all_gather(
                lax.all_to_all(outgoing, "rows", split_axis=0, concat_axis=0, tiled=True),
                "mp",
                axis=2,
                tiled=True,
            )
            sources = received.shape[0]
            count = received.shape[1]
            flat = received.reshape(sources * count, received.shape[2])
            gate_val = jnp.dot(flat, w_gate[0], preferred_element_type=jnp.float32)
            up_val = jnp.dot(flat, w_up[0], preferred_element_type=jnp.float32)
            active = (jax.nn.silu(gate_val) * up_val).astype(jnp.bfloat16)
            partial_out = jnp.dot(active, w_down[0], preferred_element_type=jnp.float32)
            summed = lax.psum_scatter(
                partial_out.astype(jnp.bfloat16), "mp", scatter_dimension=1, tiled=True
            ).astype(jnp.float32)
            returned = summed.astype(jnp.bfloat16).reshape(sources, count, summed.shape[1])
            arrived_back = lax.all_to_all(returned, "rows", split_axis=0, concat_axis=0, tiled=True)
            mixed = jnp.dot(
                combine_map,
                arrived_back.reshape(slot_count, arrived_back.shape[2]).astype(jnp.float32),
                precision=lax.Precision.HIGHEST,
            )
            fresh = (hidden_f + mixed).astype(jnp.bfloat16)
            hidden = jnp.where(talker, fresh, hidden)
            arrived = passed_along(hidden, "segment", 1)
            carried = arrived
    talker_state = jnp.where(talker, hidden, arrived)
    audio = jnp.stack(sounds, axis=0)[None]
    return (talker_state, audio)


def solution(mesh):
    return jax.shard_map(
        on_device,
        mesh=mesh,
        in_specs=(
            P("rows", "mp"),
            P(None, "rows", None),
            P("mp"),
            P("mp", None),
            P("rows", None, "mp"),
            P("rows", None, "mp"),
            P("rows", "mp", None),
            P(None, "mp"),
            P(None, "mp"),
            P(None, None, "mp"),
            P(None, "mp"),
            P(None, "mp"),
            P("mp"),
        ),
        out_specs=(P("rows", "mp"), P("segment", None, "rows")),
        check_vma=False,
    )
```

profile of v0, /device:TPU:256, one launch (start us, length us, event | category | flops | bytes accessed | tf_op | source)
XLA Modules:
  0.0 1238.4 jit_solution(10877478065674280957)
XLA Ops:
  10.0 8.8 psum.147
  19.6 62.2 %all_to_all.30 = bf16[128,8,1024]{2,1,0:T(8,128)(2,1)} all-to-all(bf16[128,8,1024]{2,1,0:T(8,128)(2,1)S(1)} %convert_bitcast_fusion.2), channel_id=1, replica_groups=mesh['segment'=2,'rows'=128,'mp'=2] {'rows'}, dimensions={0} | all-to-all | bytes 4194304 | tf_op jit(solution)/shard_map/all_to_all | solution.py:122
  82.0 114.9 %all-gather.4.cloned.1.call-done = bf16[128,8,2048]{2,1,0:T(8,128)(2,1)} async-done(((bf16[128,8,1024]{2,1,0:T(8,128)(2,1)}), bf16[128,8,2048]{2,1,0:T(8,128)(2,1)}) %all-gather.4.cloned.1.call-update) | async-done | bytes 4194320 | tf_op jit(solution)/shard_map/all_gather | solution.py:121
  209.3 108.5 %reduce-scatter.4.cloned.1.call-done = bf16[1024,1024]{1,0:T(8,128)(2,1)} async-done(((bf16[1024,2048]{1,0:T(8,128)(2,1)}), bf16[1024,1024]{1,0:T(8,128)(2,1)}) %reduce-scatter.4.cloned.1.call-update) | async-done | bytes 2097168 | tf_op jit(solution)/shard_map/reduce_scatter | solution.py:134
  317.8 11.9 all-to-all-start.1
  330.3 40.1 %psum.148 = bf16[64,128]{1,0:T(8,128)(2,1)S(1)} all-reduce(bf16[64,128]{1,0:T(8,128)(2,1)S(1)} %convolution_convert_fusion.8), channel_id=1, replica_groups=mesh['segment'=2,'rows'=128,'mp'=2] {'mp'}, use_global_device_ids=true, to_apply=%region_5.6 | all-reduce | flops 8192 | bytes 32768 | tf_op jit(solution)/shard_map/psum | solution.py:99
  381.7 8.8 psum.149
  391.3 59.5 %all_to_all.31 = bf16[128,8,1024]{2,1,0:T(8,128)(2,1)} all-to-all(bf16[128,8,1024]{2,1,0:T(8,128)(2,1)S(1)} %convert_bitcast_fusion.1), channel_id=1, replica_groups=mesh['segment'=2,'rows'=128,'mp'=2] {'rows'}, dimensions={0} | all-to-all | bytes 4194304 | tf_op jit(solution)/shard_map/all_to_all | solution.py:122
  450.9 114.7 %all-gather.6.cloned.1.call-done = bf16[128,8,2048]{2,1,0:T(8,128)(2,1)} async-done(((bf16[128,8,1024]{2,1,0:T(8,128)(2,1)}), bf16[128,8,2048]{2,1,0:T(8,128)(2,1)}) %all-gather.6.cloned.1.call-update) | async-done | bytes 4194320 | tf_op jit(solution)/shard_map/all_gather | solution.py:121
  578.1 108.5 %reduce-scatter.6.cloned.1.call-done = bf16[1024,1024]{1,0:T(8,128)(2,1)} async-done(((bf16[1024,2048]{1,0:T(8,128)(2,1)}), bf16[1024,1024]{1,0:T(8,128)(2,1)}) %reduce-scatter.6.cloned.1.call-update) | async-done | bytes 2097168 | tf_op jit(solution)/shard_map/reduce_scatter | solution.py:134
  686.6 11.7 all-to-all-start.3
  700.6 38.2 %psum.150 = bf16[64,128]{1,0:T(8,128)(2,1)S(1)} all-reduce(bf16[64,128]{1,0:T(8,128)(2,1)S(1)} %convolution_convert_fusion.7), channel_id=1, replica_groups=mesh['segment'=2,'rows'=128,'mp'=2] {'mp'}, use_global_device_ids=true, to_apply=%region_16.17 | all-reduce | flops 8192 | bytes 32768 | tf_op jit(solution)/shard_map/psum | solution.py:99
  750.3 8.8 psum.151
  759.9 59.5 %all_to_all.32 = bf16[128,8,1024]{2,1,0:T(8,128)(2,1)} all-to-all(bf16[128,8,1024]{2,1,0:T(8,128)(2,1)S(1)} %convert_bitcast_fusion), channel_id=1, replica_groups=mesh['segment'=2,'rows'=128,'mp'=2] {'rows'}, dimensions={0} | all-to-all | bytes 4194304 | tf_op jit(solution)/shard_map/all_to_all | solution.py:122
  819.5 114.7 %all-gather.8.cloned.1.call-done = bf16[128,8,2048]{2,1,0:T(8,128)(2,1)} async-done(((bf16[128,8,1024]{2,1,0:T(8,128)(2,1)}), bf16[128,8,2048]{2,1,0:T(8,128)(2,1)}) %all-gather.8.cloned.1.call-update) | async-done | bytes 4194320 | tf_op jit(solution)/shard_map/all_gather | solution.py:121
  946.7 108.5 %reduce-scatter.8.cloned.1.call-done = bf16[1024,1024]{1,0:T(8,128)(2,1)} async-done(((bf16[1024,2048]{1,0:T(8,128)(2,1)}), bf16[1024,1024]{1,0:T(8,128)(2,1)}) %reduce-scatter.8.cloned.1.call-update) | async-done | bytes 2097168 | tf_op jit(solution)/shard_map/reduce_scatter | solution.py:134
  1055.2 11.9 all-to-all-start.5
  1070.1 37.6 %all_gather.21 = bf16[64,2048]{1,0:T(8,128)(2,1)S(1)} all-gather(bf16[64,1024]{1,0:T(8,128)(2,1)S(1)} %collective-permute-done.1), channel_id=1, replica_groups=mesh['segment'=2,'rows'=128,'mp'=2] {'mp'}, dimensions={1}, use_global_device_ids=true | all-gather | bytes 393216 | tf_op jit(solution)/shard_map/all_gather | solution.py:71
  1113.4 13.8 %psum.152 = bf16[64,128]{1,0:T(8,128)(2,1)S(1)} all-reduce(bf16[64,128]{1,0:T(8,128)(2,1)S(1)} %convolution_convert_fusion.6), channel_id=1, replica_groups=mesh['segment'=2,'rows'=128,'mp'=2] {'mp'}, use_global_device_ids=true, to_apply=%region_27.28 | all-reduce | flops 8192 | bytes 32768 | tf_op jit(solution)/shard_map/psum | solution.py:99
  1128.4 9.6 all_gather.22
  1146.8 9.6 all_gather.23
  1185.6 8.8 all-reduce.2
  1212.4 8.9 all-reduce.1
  1221.7 8.8 all-reduce
  (246 shorter events, 134.1 us)
Async XLA Ops:
  7.2 1100.5 %copy-start = (bf16[2048,512]{1,0:T(8,128)(2,1)S(1)}, bf16[2048,512]{1,0:T(8,128)(2,1)}, u32[]{:S(2)}) copy-start(bf16[2048,512]{1,0:T(8,128)(2,1)} %param.20) | copy-start | bytes 6291460
  7.2 189.7 %all-gather.4.cloned.1.call-start = ((), (), s32[]{:S(2)}) async-start(), calls=%async_computation.9 | async-start | bytes 6291456 | tf_op jit(solution)/shard_map/all_gather | solution.py:121
  81.9 235.9 %reduce-scatter.4.cloned.1.call-start = ((), (), s32[]{:S(2)}) async-start(), calls=%async_computation.10 | async-start | bytes 6291456 | tf_op jit(solution)/shard_map/reduce_scatter | solution.py:134
  317.8 60.9 %all-to-all-start.1 = ((bf16[128,8,1024]{2,1,0:T(8,128)(2,1)}), bf16[128,8,1024]{2,1,0:T(8,128)(2,1)}, u32[]{:S(2)}, u32[]{:S(2)}) async-start(bf16[128,8,1024]{2,1,0:T(8,128)(2,1)} %bitcast.200), calls=%async_computation.2 | async-start | bytes 4194304 | tf_op jit(solution)/shard_map/all_to_all | solution.py:138
  329.7 235.9 %all-gather.6.cloned.1.call-start = ((), (), s32[]{:S(2)}) async-start(), calls=%async_computation.11 | async-start | bytes 6291456 | tf_op jit(solution)/shard_map/all_gather | solution.py:121
  450.9 235.7 %reduce-scatter.6.cloned.1.call-start = ((), (), s32[]{:S(2)}) async-start(), calls=%async_computation.12 | async-start | bytes 6291456 | tf_op jit(solution)/shard_map/reduce_scatter | solution.py:134
  686.6 60.8 %all-to-all-start.3 = ((bf16[128,8,1024]{2,1,0:T(8,128)(2,1)}), bf16[128,8,1024]{2,1,0:T(8,128)(2,1)}, u32[]{:S(2)}, u32[]{:S(2)}) async-start(bf16[128,8,1024]{2,1,0:T(8,128)(2,1)} %bitcast.201), calls=%async_computation.5 | async-start | bytes 4194304 | tf_op jit(solution)/shard_map/all_to_all | solution.py:138
  698.3 235.9 %all-gather.8.cloned.1.call-start = ((), (), s32[]{:S(2)}) async-start(), calls=%async_computation.13 | async-start | bytes 6291456 | tf_op jit(solution)/shard_map/all_gather | solution.py:121
  819.5 235.7 %reduce-scatter.8.cloned.1.call-start = ((), (), s32[]{:S(2)}) async-start(), calls=%async_computation.14 | async-start | bytes 6291456 | tf_op jit(solution)/shard_map/reduce_scatter | solution.py:134
  1055.2 82.7 %all-to-all-start.5 = ((bf16[128,8,1024]{2,1,0:T(8,128)(2,1)}), bf16[128,8,1024]{2,1,0:T(8,128)(2,1)}, u32[]{:S(2)}, u32[]{:S(2)}) async-start(bf16[128,8,1024]{2,1,0:T(8,128)(2,1)} %bitcast.199), calls=%async_computation.8 | async-start | bytes 4194304 | tf_op jit(solution)/shard_map/all_to_all | solution.py:138
  1067.8 112.5 %copy-start.15 = (f32[1,1,512]{2,0,1:T(1,128)}, f32[1,1,512]{2,0,1:T(1,128)S(1)}, u32[]{:S(2)}) copy-start(f32[1,1,512]{2,0,1:T(1,128)S(1)} %get-tuple-element.61) | copy-start | bytes 6148
  1067.8 112.5 %copy-start.17 = (f32[1,1,512]{2,0,1:T(1,128)}, f32[1,1,512]{2,0,1:T(1,128)S(1)}, u32[]{:S(2)}) copy-start(f32[1,1,512]{2,0,1:T(1,128)S(1)} %get-tuple-element.62) | copy-start | bytes 6148
  1067.8 2.3 collective-permute-start.1
  1108.2 51.6 %collective-permute-start.2 = (bf16[1,512]{1,0:T(2,128)(2,1)S(1)}, bf16[1,512]{1,0:T(2,128)(2,1)S(1)}, u32[]{:S(2)}, u32[]{:S(2)}) collective-permute-start(bf16[1,512]{1,0:T(2,128)(2,1)S(1)} %slice.433), channel_id=1, source_target_pairs={{0,2},{2,4},{4,6},{6,8},{8,10},{10,12},{12,14},{14,16},{16,18},{18... | collective-permute-start | bytes 3080 | tf_op jit(solution)/shard_map/ppermute | solution.py:13
  1111.6 16.8 %collective-permute-start.5 = (bf16[64,1024]{1,0:T(8,128)(2,1)S(1)}, bf16[64,1024]{1,0:T(8,128)(2,1)S(1)}, u32[]{:S(2)}, u32[]{:S(2)}) collective-permute-start(bf16[64,1024]{1,0:T(8,128)(2,1)S(1)} %get-tuple-element.99), channel_id=1, source_target_pairs={{0,256},{1,257},{2,258},{3,259},{4,260},{5,261},{6,262},{7,263},{8... | collective-permute-start | bytes 393224 | tf_op jit(solution)/shard_map/ppermute | solution.py:13
  1140.8 6.0 collective-permute-start
  1142.6 17.2 %collective-permute-start.6 = (bf16[1,512]{1,0:T(2,128)(2,1)S(1)}, bf16[1,512]{1,0:T(2,128)(2,1)S(1)}, u32[]{:S(2)}, u32[]{:S(2)}) collective-permute-start(bf16[1,512]{1,0:T(2,128)(2,1)S(1)} %slice.452), channel_id=1, source_target_pairs={{0,2},{2,4},{4,6},{6,8},{8,10},{10,12},{12,14},{14,16},{16,18},{18... | collective-permute-start | bytes 3080 | tf_op jit(solution)/shard_map/ppermute | solution.py:13
  1156.8 11.5 collective-permute-start.9
  1168.6 11.6 collective-permute-start.7
  1170.8 11.6 collective-permute-start.3
  1173.0 11.6 collective-permute-start.10
  1195.7 11.7 collective-permute-start.11
  1198.3 11.7 collective-permute-start.8
  1200.3 11.7 collective-permute-start.4
  (26 other events, 771.0 us)
Sparse Core Ops, SparseCore 0:
  82.0 114.7 all-gather.3
  209.4 108.3 reduce-scatter.3
  451.0 114.5 all-gather.5
  578.2 108.3 reduce-scatter.5
  819.6 114.5 all-gather.7
  946.8 108.3 reduce-scatter.7
where the time goes:
time: 1250 us; the launch traced here: 1240 us
  waiting for transfers between devices  708 us (57%)
  blocking collectives  383 us (31%)
  starting transfers between devices  61.4 us (5%)
  matrix products  50.4 us (4%)
  between operations  15.7 us (1%)
  other arithmetic  13.4 us (1%)
    all_gather x3, waiting for transfers between devices, on_device(): lax.all_gather(lax.all_to_all(outgoing, 'rows', split_axis=0, concat_axis...  344 us
    reduce_scatter x3, waiting for transfers between devices, on_device(): lax.psum_scatter(partial_out.astype(jnp.bfloat16), 'mp', scatter_dimensio...  326 us
    all_to_all x3, blocking collectives, on_device(): lax.all_to_all(outgoing, 'rows', split_axis=0, concat_axis=0, tiled=True)  181 us
    psum x3, blocking collectives, on_device(): lax.psum(jnp.dot(normed, w_router, preferred_element_type=jnp.float32).as...  92.2 us
    all_gather x3, blocking collectives, on_device(): full_rows = lax.all_gather(carried, 'mp', axis=1, tiled=True)  56.7 us
    all_to_all x3, starting transfers between devices, on_device(): lax.all_to_all(returned, 'rows', split_axis=0, concat_axis=0, tiled=True)  35.4 us
    psum x3, blocking collectives, on_device(): squares = lax.psum(jnp.sum(hidden_f * hidden_f, axis=1), 'mp')  26.5 us
    ppermute x12, starting transfers between devices, passed_along(): return lax.ppermute(block, axis, route)  25.5 us
  transfers between devices with their start and end apart: 21, of which 16 were waited for; matrix products, arithmetic and copies ran while one was open for 1% of the time, Pallas kernels for 0%

commit v1 on v0

v1 whole, which is shorter than its diff:
```python
import jax
import jax.numpy as jnp
from jax import lax
from jax.sharding import PartitionSpec as P

BF16 = jnp.bfloat16
F32 = jnp.float32


def swapped(block, axis):
    return lax.ppermute(block, axis, [(0, 1), (1, 0)])


def passed_along(block):
    count = lax.axis_size("rows")
    return lax.ppermute(block, "rows", [(i, i + 1) for i in range(count - 1)])


def dot(a, b):
    return jnp.dot(a, b, preferred_element_type=F32)


def other_half(weight, axis):
    seg = lax.axis_index("segment")
    share = weight.shape[axis] // 2
    mine = lax.dynamic_slice_in_dim(weight, seg * share, share, axis)
    fetched = swapped(mine, "mp")
    return lax.all_gather(fetched, "segment", axis=axis, tiled=True)


def route(ids, experts, per_device, offset):
    rows = ids.shape[0]
    lanes = jnp.arange(experts, dtype=jnp.int32)
    hot = jnp.any(ids[:, :, None] == lanes[None, None, :], axis=1)
    hot_b = hot.astype(BF16)
    below = (jnp.arange(rows)[:, None] > jnp.arange(rows)[None, :]).astype(BF16)
    slot = dot(below, hot_b)
    code = jnp.where(hot, slot, -1.0).astype(BF16)
    columns = jnp.arange(experts * per_device, dtype=jnp.int32)
    spread = (lanes[:, None] == (columns // per_device)[None, :]).astype(BF16)
    wide = dot(code, spread)
    wanted = (offset + columns % per_device).astype(F32)
    return hot, wide == wanted[None, :], spread


def layer(pieces, taps, gain, bias, dilation, count):
    reach = (taps.shape[0] - 1) * dilation
    mixed = jnp.zeros((count, pieces.shape[1]), F32)
    for j in range(taps.shape[0]):
        start = reach - j * dilation
        mixed = mixed + taps[j] * pieces[start : start + count]
    channels = pieces.shape[1]
    center = jnp.sum(mixed, axis=1, keepdims=True) / channels
    spread = jnp.sum(mixed * mixed, axis=1, keepdims=True) / channels - center * center
    normed = (mixed - center) * lax.rsqrt(spread + 1e-06)
    return (pieces[reach:] + normed * gain + bias).astype(BF16)


def on_device(
    start_state,
    expert_ids,
    norm_gain,
    w_router,
    w_gate,
    w_up,
    w_down,
    w_in,
    trans_taps,
    dw_kernels,
    ln_gain,
    ln_bias,
    w_out,
):
    seg = lax.axis_index("segment")
    mp = lax.axis_index("mp")
    rows, half = start_state.shape
    experts = w_router.shape[1]
    steps, _, topk = expert_ids.shape
    layers, kernel, _ = dw_kernels.shape
    capacity = min(rows, max(2, 2 * rows * topk // experts))
    parts = 4
    per_device = capacity // parts
    slots = experts * per_device
    offset = (mp * 2 + seg) * per_device
    depth = 2 * half
    share = rows // 2

    x = lax.all_gather(start_state, "mp", axis=1, tiled=True)
    gain_pair = lax.all_gather(norm_gain[None], "mp", axis=1, tiled=True)
    small = jnp.concatenate(
        [trans_taps, dw_kernels.reshape(layers * kernel, -1), ln_gain, ln_bias, w_out[None]], axis=0
    )
    small = jnp.concatenate([small, swapped(small, "mp")], axis=1)
    taps = small[:4]
    dw = small[4 : 4 + layers * kernel].reshape(layers, kernel, -1)
    rest = small[4 + layers * kernel :]
    gains, biases, wave = rest[:layers], rest[layers : 2 * layers], rest[2 * layers]

    gate = jnp.concatenate([w_gate[0], other_half(w_gate[0], 0)], axis=1)
    up = jnp.concatenate([w_up[0], other_half(w_up[0], 0)], axis=1)
    down = jnp.concatenate([w_down[0], other_half(w_down[0], 0)], axis=0)
    router_far = other_half(w_router, 0)
    router = jnp.where(
        mp == 0,
        jnp.concatenate([w_router, router_far], axis=0),
        jnp.concatenate([router_far, w_router], axis=0),
    )

    first = lax.axis_index("rows") == 0
    frames_back = 16
    voiced = []
    for step in range(steps):
        hot, placed, spread = route(expert_ids[step], experts, per_device, offset)
        xf = x.astype(F32)
        squares = jnp.sum(xf * xf, axis=1, keepdims=True)
        normed = (xf * lax.rsqrt(squares / depth + 1e-06) * gain_pair).astype(BF16)
        outgoing = lax.dot_general(
            placed.astype(BF16), normed, (((0,), (0,)), ((), ())), preferred_element_type=F32
        ).astype(BF16)
        received = lax.all_to_all(
            outgoing.reshape(experts, per_device, depth), "rows", split_axis=0, concat_axis=0, tiled=True
        )
        logits = dot(normed, router)
        squashed = jnp.where(hot, jax.nn.sigmoid(logits), 0.0)
        weights = squashed / jnp.sum(squashed, axis=1, keepdims=True)
        high = lax.reduce_precision(weights, 8, 7)
        low = weights - high
        pair = jnp.concatenate([high, low], axis=0).astype(BF16)
        both = jnp.concatenate([placed, placed], axis=0)
        combine = jnp.where(both, dot(pair, spread), 0.0).astype(BF16)

        flat = received.reshape(slots, depth)
        active = (jax.nn.silu(dot(flat, gate)) * dot(flat, up)).astype(BF16)
        answer = dot(active, down).astype(BF16)
        back = lax.all_to_all(
            answer.reshape(experts, per_device, depth), "rows", split_axis=0, concat_axis=0, tiled=True
        )
        mixed = dot(combine, back.reshape(slots, depth))
        partial = (mixed[:rows] + mixed[rows:]).astype(BF16)
        chip = lax.all_gather(partial, "segment", axis=0)
        chip = lax.dynamic_slice_in_dim(chip, seg * share, share, 1).astype(F32)
        chip = (chip[0] + chip[1]).astype(BF16)
        total = lax.all_gather(chip, "mp", axis=0).astype(F32)
        mine = lax.dynamic_slice_in_dim(x, seg * share, share, 0).astype(F32)
        fresh = (mine + (total[0] + total[1])).astype(BF16)
        x = lax.all_gather(fresh, "segment", axis=0, tiled=True)

        own = dot(x, w_in).astype(BF16)
        frames = jnp.concatenate([own, swapped(own, "mp")], axis=1)
        earlier = passed_along(frames[-frames_back:])
        frames = jnp.concatenate([earlier, frames], axis=0).astype(F32)
        now, before = frames[1:], frames[:-1]
        even = taps[0] * now + taps[2] * before
        odd = taps[1] * now + taps[3] * before
        signal = jnp.stack([even, odd], axis=1).reshape(-1, frames.shape[1]).astype(BF16)
        length = 2 * rows
        needed = length + sum((kernel - 1) * 3**i for i in range(layers))
        signal = signal[-needed:]
        for i in range(layers):
            needed -= (kernel - 1) * 3**i
            signal = layer(signal.astype(F32), dw[i], gains[i], biases[i], 3**i, needed)
            halo = needed - length
            if halo:
                head = jnp.where(first, jnp.zeros_like(signal[:halo]), signal[:halo])
                signal = jnp.concatenate([head, signal[halo:]], axis=0)
        voiced.append(jnp.sum(signal.astype(F32) * wave, axis=1))
    audio = jnp.stack(voiced, axis=0)
    audio = jnp.where(seg == 0, jnp.zeros_like(audio), audio)[None]
    state = lax.dynamic_slice_in_dim(x, mp * half, half, 1)
    return state, audio


def solution(mesh):
    return jax.shard_map(
        on_device,
        mesh=mesh,
        in_specs=(
            P("rows", "mp"),
            P(None, "rows", None),
            P("mp"),
            P("mp", None),
            P("rows", None, "mp"),
            P("rows", None, "mp"),
            P("rows", "mp", None),
            P(None, "mp"),
            P(None, "mp"),
            P(None, None, "mp"),
            P(None, "mp"),
            P(None, "mp"),
            P("mp"),
        ),
        out_specs=(P("rows", "mp"), P("segment", None, "rows")),
        check_vma=False,
    )
```

time: 1250 us -> 537 us (0.43)
  waiting for transfers between devices: 708 us -> 135 us
  blocking collectives: 383 us -> 158 us
  local copies, waits for them, and re-layouts: 6.04 us -> 86.1 us
  starting transfers between devices: 61.4 us -> 94.8 us
  between operations: 15.7 us -> 1.69 us
    all_gather x3 -> x0, waiting for transfers between devices: 344 us -> none  [on_device(): lax.all_gather(lax.all_to_all(outgoing, 'rows', split_axis=0, concat_axis...]
    reduce_scatter x3 -> x0, waiting for transfers between devices: 326 us -> none  [on_device(): lax.psum_scatter(partial_out.astype(jnp.bfloat16), 'mp', scatter_dimensio...]
    psum x9 -> x0, blocking collectives: 145 us -> none  [the longest x3 92.2 us: on_device(): lax.psum(jnp.dot(normed, w_router, preferred_element_type=jnp.float32).as...]
    all_to_all x3 -> x2, blocking collectives: 181 us -> 77.6 us  [on_device(): lax.all_to_all(outgoing.reshape(experts, per_device, depth), 'rows', spli...]
    ppermute x12 -> x11, waiting for transfers between devices: 25 us -> 103 us  [the longest x8 85.3 us: swapped(): return lax.ppermute(block, axis, [(0, 1), (1, 0)])]
    slice x20 -> x30, local copies, waits for them, and re-layouts: 2.82 us -> 45.6 us  [the longest x21 35.9 us: layer(): mixed = mixed + taps[j] * pieces[start:start + count]]
    all_gather x3 -> x15, blocking collectives: 56.7 us -> 80.3 us  [the longest x3 35.6 us: on_device(): total = lax.all_gather(chip, 'mp', axis=0).astype(F32)]
    reshape x0 -> x13, local copies, waits for them, and re-layouts: none -> 23 us  [the longest x3 7.66 us: on_device(): answer.reshape(experts, per_device, depth)]
  transfers between devices with their start and end apart: 21 -> 15, of which waited for: 16 -> 13; matrix products, arithmetic and copies ran while one was open for 1% -> 4% of each run, Pallas kernels for 0% -> 0%
where the time goes in v1:
time: 537 us; the launch traced here: 527 us
  blocking collectives  158 us (29%)
  waiting for transfers between devices  135 us (25%)
  starting transfers between devices  94.8 us (18%)
  local copies, waits for them, and re-layouts  86.1 us (16%)
  matrix products  39.1 us (7%)
  other arithmetic  11.9 us (2%)
    ppermute x8, waiting for transfers between devices, swapped(): return lax.ppermute(block, axis, [(0, 1), (1, 0)])  85.3 us
    all_to_all x2, blocking collectives, on_device(): lax.all_to_all(outgoing.reshape(experts, per_device, depth), 'rows', spli...  77.6 us
    ppermute x8, starting transfers between devices, swapped(): return lax.ppermute(block, axis, [(0, 1), (1, 0)])  39.7 us
    slice x21, local copies, waits for them, and re-layouts, layer(): mixed = mixed + taps[j] * pieces[start:start + count]  35.9 us
    all_gather x3, blocking collectives, on_device(): total = lax.all_gather(chip, 'mp', axis=0).astype(F32)  35.6 us
    dot_general x18, matrix products, dot(): return jnp.dot(a, b, preferred_element_type=F32)  35.6 us
    all_to_all x3, starting transfers between devices, on_device(): lax.all_to_all(answer.reshape(experts, per_device, depth), 'rows', split_...  33.3 us
    all_to_all x3, waiting for transfers between devices, on_device(): lax.all_to_all(answer.reshape(experts, per_device, depth), 'rows', split_...  27.9 us
  transfers between devices with their start and end apart: 15, of which 13 were waited for; matrix products, arithmetic and copies ran while one was open for 4% of the time, Pallas kernels for 0%

profile of v1, /device:TPU:256, one launch (start us, length us, event | category | flops | bytes accessed | tf_op | source)
XLA Modules:
  0.0 526.7 jit_solution(7923951035629191762)
XLA Ops:
  2.4 10.3 %all_gather.57 = bf16[64,2048]{1,0:T(8,128)(2,1)S(1)} all-gather(bf16[64,1024]{1,0:T(8,128)(2,1)} %param.13), channel_id=1, replica_groups=mesh['segment'=2,'rows'=128,'mp'=2] {'mp'}, dimensions={1}, use_global_device_ids=true | all-gather | bytes 393216 | tf_op jit(solution)/shard_map/all_gather | solution.py:88
  12.7 10.8 %all-gather = f32[2048]{0:T(1024)S(1)} all-gather(f32[1024]{0:T(1024)} %param.15), channel_id=2, replica_groups=mesh['segment'=2,'rows'=128,'mp'=2] {'mp'}, dimensions={0}, use_global_device_ids=true | all-gather | bytes 12288 | tf_op jit(solution)/shard_map/all_gather | solution.py:89
  26.0 14.2 %all-to-all-start = ((bf16[128,2,2048]{2,1,0:T(2,128)(2,1)}), bf16[128,2,2048]{2,1,0:T(2,128)(2,1)S(1)}, u32[]{:S(2)}, u32[]{:S(2)}) async-start(bf16[128,2,2048]{2,1,0:T(2,128)(2,1)} %reshape.287), calls=%async_computation | async-start | bytes 2097152 | tf_op jit(solution)/shard_map/all_to_all | solution.py:120
  42.0 5.1 collective-permute-start.3
  53.8 5.1 collective-permute-start.1
  58.9 36.1 %collective-permute-done.3 = bf16[96,2048]{1,0:T(8,128)(2,1)} collective-permute-done((bf16[96,2048]{1,0:T(8,128)(2,1)}, bf16[96,2048]{1,0:T(8,128)(2,1)}, u32[]{:S(2)}, u32[]{:S(2)}) %collective-permute-start.3) | collective-permute-done | bytes 393248 | tf_op jit(solution)/shard_map/ppermute | solution.py:11
  127.1 10.8 %all-to-all-start.1 = ((bf16[128,2,2048]{2,1,0:T(2,128)(2,1)}), bf16[128,2,2048]{2,1,0:T(2,128)(2,1)S(1)}, u32[]{:S(2)}, u32[]{:S(2)}) async-start(bf16[128,2,2048]{2,1,0:T(2,128)(2,1)} %reshape.289), calls=%async_computation.1 | async-start | bytes 2097152 | tf_op jit(solution)/shard_map/all_to_all | solution.py:135
  139.5 5.1 collective-permute-start
  149.1 12.5 %collective-permute-done = bf16[512,128]{1,0:T(8,128)(2,1)S(1)} collective-permute-done((bf16[512,128]{1,0:T(8,128)(2,1)}, bf16[512,128]{1,0:T(8,128)(2,1)S(1)}, u32[]{:S(2)}, u32[]{:S(2)}) %collective-permute-start) | collective-permute-done | bytes 131104 | tf_op jit(solution)/shard_map/ppermute | solution.py:11
  174.3 12.6 %all_gather.65 = bf16[2,32,2048]{2,1,0:T(8,128)(2,1)S(1)} all-gather(bf16[1,32,2048]{2,1,0:T(8,128)(2,1)S(1)} %fusion.89), channel_id=1, replica_groups=mesh['segment'=2,'rows'=128,'mp'=2] {'mp'}, dimensions={0}, use_global_device_ids=true | all-gather | bytes 393216 | tf_op jit(solution)/shard_map/all_gather | solution.py:143
  192.4 38.6 %all_to_all.30 = bf16[128,2,2048]{2,1,0:T(2,128)(2,1)} all-to-all(bf16[128,2,2048]{2,1,0:T(2,128)(2,1)S(1)} %reshape.291), channel_id=1, replica_groups=mesh['segment'=2,'rows'=128,'mp'=2] {'rows'}, dimensions={0} | all-to-all | bytes 2097152 | tf_op jit(solution)/shard_map/all_to_all | solution.py:120
  242.2 10.8 %all-to-all-start.3 = ((bf16[128,2,2048]{2,1,0:T(2,128)(2,1)}), bf16[128,2,2048]{2,1,0:T(2,128)(2,1)S(1)}, u32[]{:S(2)}, u32[]{:S(2)}) async-start(bf16[128,2,2048]{2,1,0:T(2,128)(2,1)} %reshape.293), calls=%async_computation.3 | async-start | bytes 2097152 | tf_op jit(solution)/shard_map/all_to_all | solution.py:135
  255.3 24.0 %all-to-all-done.3 = bf16[128,2,2048]{2,1,0:T(2,128)(2,1)S(1)} async-done(((bf16[128,2,2048]{2,1,0:T(2,128)(2,1)}), bf16[128,2,2048]{2,1,0:T(2,128)(2,1)S(1)}, u32[]{:S(2)}, u32[]{:S(2)}) %all-to-all-start.3) | async-done | bytes 1048608 | tf_op jit(solution)/shard_map/all_to_all | solution.py:135
  284.4 12.9 %all_gather.69 = bf16[2,32,2048]{2,1,0:T(8,128)(2,1)S(1)} all-gather(bf16[1,32,2048]{2,1,0:T(8,128)(2,1)S(1)} %fusion.85), channel_id=1, replica_groups=mesh['segment'=2,'rows'=128,'mp'=2] {'mp'}, dimensions={0}, use_global_device_ids=true | all-gather | bytes 393216 | tf_op jit(solution)/shard_map/all_gather | solution.py:143
  303.7 39.0 %all_to_all.31 = bf16[128,2,2048]{2,1,0:T(2,128)(2,1)} all-to-all(bf16[128,2,2048]{2,1,0:T(2,128)(2,1)} %reshape.295), channel_id=1, replica_groups=mesh['segment'=2,'rows'=128,'mp'=2] {'rows'}, dimensions={0} | all-to-all | bytes 2097152 | tf_op jit(solution)/shard_map/all_to_all | solution.py:120
  355.2 11.8 %all-to-all-start.5 = ((bf16[128,2,2048]{2,1,0:T(2,128)(2,1)}), bf16[128,2,2048]{2,1,0:T(2,128)(2,1)}, u32[]{:S(2)}, u32[]{:S(2)}) async-start(bf16[128,2,2048]{2,1,0:T(2,128)(2,1)} %reshape.297), calls=%async_computation.5 | async-start | bytes 2097152 | tf_op jit(solution)/shard_map/all_to_all | solution.py:135
  372.0 14.9 %collective-permute-done.4 = f32[23,512]{1,0:T(8,128)S(1)} collective-permute-done((f32[23,512]{1,0:T(8,128)S(1)}, f32[23,512]{1,0:T(8,128)S(1)}, u32[]{:S(2)}, u32[]{:S(2)}) %collective-permute-start.4) | collective-permute-done | bytes 47136 | tf_op jit(solution)/shard_map/ppermute | solution.py:11
  387.5 5.1 collective-permute-start.5
  392.7 5.0 collective-permute-done.5
  401.1 8.5 %collective-permute-done.6 = bf16[16,1024]{1,0:T(8,128)(2,1)S(1)} collective-permute-done((bf16[16,1024]{1,0:T(8,128)(2,1)S(1)}, bf16[16,1024]{1,0:T(8,128)(2,1)S(1)}, u32[]{:S(2)}, u32[]{:S(2)}) %collective-permute-start.6) | collective-permute-done | bytes 32800 | tf_op jit(solution)/shard_map/ppermute | solution.py:16
  410.1 4.9 collective-permute-start.7
  430.5 10.1 %all_gather.73 = bf16[2,32,2048]{2,1,0:T(8,128)(2,1)S(1)} all-gather(bf16[1,32,2048]{2,1,0:T(8,128)(2,1)S(1)} %fusion.81), channel_id=1, replica_groups=mesh['segment'=2,'rows'=128,'mp'=2] {'mp'}, dimensions={0}, use_global_device_ids=true | all-gather | bytes 393216 | tf_op jit(solution)/shard_map/all_gather | solution.py:143
  448.1 5.1 collective-permute-done.9
  456.2 8.9 %collective-permute-done.10 = bf16[16,1024]{1,0:T(8,128)(2,1)S(1)} collective-permute-done((bf16[16,1024]{1,0:T(8,128)(2,1)S(1)}, bf16[16,1024]{1,0:T(8,128)(2,1)S(1)}, u32[]{:S(2)}, u32[]{:S(2)}) %collective-permute-start.10) | collective-permute-done | bytes 32800 | tf_op jit(solution)/shard_map/ppermute | solution.py:16
  (223 shorter events, 202.7 us)
Async XLA Ops:
  0.6 386.3 %copy-start = (bf16[2048,512]{1,0:T(8,128)(2,1)S(1)}, bf16[2048,512]{1,0:T(8,128)(2,1)}, u32[]{:S(2)}) copy-start(bf16[2048,512]{1,0:T(8,128)(2,1)} %param.20) | copy-start | bytes 6291460
  2.1 23.8 %copy-start.25 = (f32[256]{0:T(256)}, f32[256]{0:T(256)S(1)}, u32[]{:S(2)}) copy-start(f32[256]{0:T(256)S(1)} %get-tuple-element.107) | copy-start | bytes 3076
  2.4 23.6 %copy-start.20 = (pred[64,128]{1,0:T(8,128)(4,1)}, pred[64,128]{1,0:T(8,128)(4,1)S(1)}, u32[]{:S(2)}) copy-start(pred[64,128]{1,0:T(8,128)(4,1)S(1)} %fusion.90) | copy-start | bytes 24580
  26.0 89.8 %all-to-all-start = ((bf16[128,2,2048]{2,1,0:T(2,128)(2,1)}), bf16[128,2,2048]{2,1,0:T(2,128)(2,1)S(1)}, u32[]{:S(2)}, u32[]{:S(2)}) async-start(bf16[128,2,2048]{2,1,0:T(2,128)(2,1)} %reshape.287), calls=%async_computation | async-start | bytes 2097152 | tf_op jit(solution)/shard_map/all_to_all | solution.py:120
  42.0 53.0 %collective-permute-start.3 = (bf16[96,2048]{1,0:T(8,128)(2,1)}, bf16[96,2048]{1,0:T(8,128)(2,1)}, u32[]{:S(2)}, u32[]{:S(2)}) collective-permute-start(bf16[96,2048]{1,0:T(8,128)(2,1)} %dynamic-slice_bitcast_fusion), channel_id=1, source_target_pairs={{0,1},{1,0},{2,3},{3,2},{4,5},{5,4},{6,7},{7,6},{8,9},{9,8},{10,11... | collective-permute-start | bytes 1179656 | tf_op jit(solution)/shard_map/ppermute | solution.py:11
  48.1 55.2 %collective-permute-start.2 = (bf16[1024,192]{0,1:T(8,128)(2,1)S(1)}, bf16[1024,192]{0,1:T(8,128)(2,1)S(1)}, u32[]{:S(2)}, u32[]{:S(2)}) collective-permute-start(bf16[1024,192]{0,1:T(8,128)(2,1)S(1)} %dynamic-slice_bitcast_fusion.1), channel_id=1, source_target_pairs={{0,1},{1,0},{2,3},{3,2},{4,5},{5,4},{6,7},{7,6},{8,9},{9,8},{10,11... | collective-permute-start | bytes 1179656 | tf_op jit(solution)/shard_map/ppermute | solution.py:11
  53.8 54.8 %collective-permute-start.1 = (bf16[1024,192]{0,1:T(8,128)(2,1)S(1)}, bf16[1024,192]{0,1:T(8,128)(2,1)S(1)}, u32[]{:S(2)}, u32[]{:S(2)}) collective-permute-start(bf16[1024,192]{0,1:T(8,128)(2,1)S(1)} %dynamic-slice_bitcast_fusion.2), channel_id=1, source_target_pairs={{0,1},{1,0},{2,3},{3,2},{4,5},{5,4},{6,7},{7,6},{8,9},{9,8},{10,11... | collective-permute-start | bytes 1179656 | tf_op jit(solution)/shard_map/ppermute | solution.py:11
  127.1 42.0 %all-to-all-start.1 = ((bf16[128,2,2048]{2,1,0:T(2,128)(2,1)}), bf16[128,2,2048]{2,1,0:T(2,128)(2,1)S(1)}, u32[]{:S(2)}, u32[]{:S(2)}) async-start(bf16[128,2,2048]{2,1,0:T(2,128)(2,1)} %reshape.289), calls=%async_computation.1 | async-start | bytes 2097152 | tf_op jit(solution)/shard_map/all_to_all | solution.py:135
  139.5 22.1 %collective-permute-start = (bf16[512,128]{1,0:T(8,128)(2,1)}, bf16[512,128]{1,0:T(8,128)(2,1)S(1)}, u32[]{:S(2)}, u32[]{:S(2)}) collective-permute-start(bf16[512,128]{1,0:T(8,128)(2,1)} %constant_dynamic-slice_fusion.1), channel_id=1, source_target_pairs={{0,1},{1,0},{2,3},{3,2},{4,5},{5,4},{6,7},{7,6},{8,9},{9,8},{10,11... | collective-permute-start | bytes 393224 | tf_op jit(solution)/shard_map/ppermute | solution.py:11
  174.3 14.9 %copy-start.16 = (pred[64,256]{1,0:T(32,128)(4,1)S(1)}, pred[64,256]{1,0:T(32,128)(4,1)}, u32[]{:S(2)}) copy-start(pred[64,256]{1,0:T(32,128)(4,1)} %convolution_compare_fusion.1) | copy-start | bytes 49156
  242.2 37.0 %all-to-all-start.3 = ((bf16[128,2,2048]{2,1,0:T(2,128)(2,1)}), bf16[128,2,2048]{2,1,0:T(2,128)(2,1)S(1)}, u32[]{:S(2)}, u32[]{:S(2)}) async-start(bf16[128,2,2048]{2,1,0:T(2,128)(2,1)} %reshape.293), calls=%async_computation.3 | async-start | bytes 2097152 | tf_op jit(solution)/shard_map/all_to_all | solution.py:135
  352.6 14.5 %copy-start.22 = (f32[2,512]{1,0:T(2,128)S(1)}, f32[2,512]{1,0:T(2,128)}, u32[]{:S(2)}) copy-start(f32[2,512]{1,0:T(2,128)} %param.23) | copy-start | bytes 12292
  352.6 14.5 %copy-start.23 = (f32[2,512]{1,0:T(2,128)S(1)}, f32[2,512]{1,0:T(2,128)}, u32[]{:S(2)}) copy-start(f32[2,512]{1,0:T(2,128)} %param.24) | copy-start | bytes 12292
  352.6 14.5 %copy-start.24 = (f32[512]{0:T(512)S(1)}, f32[512]{0:T(512)}, u32[]{:S(2)}) copy-start(f32[512]{0:T(512)} %param.25) | copy-start | bytes 6148
  355.2 66.9 %all-to-all-start.5 = ((bf16[128,2,2048]{2,1,0:T(2,128)(2,1)}), bf16[128,2,2048]{2,1,0:T(2,128)(2,1)}, u32[]{:S(2)}, u32[]{:S(2)}) async-start(bf16[128,2,2048]{2,1,0:T(2,128)(2,1)} %reshape.297), calls=%async_computation.5 | async-start | bytes 2097152 | tf_op jit(solution)/shard_map/all_to_all | solution.py:135
  367.2 19.7 %collective-permute-start.4 = (f32[23,512]{1,0:T(8,128)S(1)}, f32[23,512]{1,0:T(8,128)S(1)}, u32[]{:S(2)}, u32[]{:S(2)}) collective-permute-start(f32[23,512]{1,0:T(8,128)S(1)} %concatenate.87), channel_id=1, source_target_pairs={{0,1},{1,0},{2,3},{3,2},{4,5},{5,4},{6,7},{7,6},{8,9},{9,8},{10,11... | collective-permute-start | bytes 141320 | tf_op jit(solution)/shard_map/ppermute | solution.py:11
  387.4 27.6 %copy-start.13 = (bf16[1024,128]{1,0:T(8,128)(2,1)S(1)}, bf16[1024,128]{1,0:T(8,128)(2,1)}, u32[]{:S(2)}) copy-start(bf16[1024,128]{1,0:T(8,128)(2,1)} %copy-done.12) | copy-start | bytes 786436
  387.5 27.6 %copy-start.17 = (bf16[1024,128]{1,0:T(8,128)(2,1)S(1)}, bf16[1024,128]{1,0:T(8,128)(2,1)}, u32[]{:S(2)}) copy-start(bf16[1024,128]{1,0:T(8,128)(2,1)} %param.16) | copy-start | bytes 786436
  387.5 10.2 %collective-permute-start.5 = (bf16[64,512]{1,0:T(8,128)(2,1)S(1)}, bf16[64,512]{1,0:T(8,128)(2,1)S(1)}, u32[]{:S(2)}, u32[]{:S(2)}) collective-permute-start(bf16[64,512]{1,0:T(8,128)(2,1)S(1)} %convolution_convert_fusion.8), channel_id=1, source_target_pairs={{0,1},{1,0},{2,3},{3,2},{4,5},{5,4},{6,7},{7,6},{8,9},{9,8},{10,11... | collective-permute-start | bytes 196616 | tf_op jit(solution)/shard_map/ppermute | solution.py:11
  397.7 11.9 %collective-permute-start.6 = (bf16[16,1024]{1,0:T(8,128)(2,1)S(1)}, bf16[16,1024]{1,0:T(8,128)(2,1)S(1)}, u32[]{:S(2)}, u32[]{:S(2)}) collective-permute-start(bf16[16,1024]{1,0:T(8,128)(2,1)S(1)} %pad_maximum_fusion.29), channel_id=1, source_target_pairs={{0,2},{2,4},{4,6},{6,8},{8,10},{10,12},{12,14},{14,16},{16,18},{18... | collective-permute-start | bytes 98312 | tf_op jit(solution)/shard_map/ppermute | solution.py:16
  410.1 10.1 %collective-permute-start.7 = (bf16[64,512]{1,0:T(8,128)(2,1)S(1)}, bf16[64,512]{1,0:T(8,128)(2,1)S(1)}, u32[]{:S(2)}, u32[]{:S(2)}) collective-permute-start(bf16[64,512]{1,0:T(8,128)(2,1)S(1)} %convolution_convert_fusion.7), channel_id=1, source_target_pairs={{0,1},{1,0},{2,3},{3,2},{4,5},{5,4},{6,7},{7,6},{8,9},{9,8},{10,11... | collective-permute-start | bytes 196616 | tf_op jit(solution)/shard_map/ppermute | solution.py:11
  420.2 27.9 %collective-permute-start.8 = (bf16[16,1024]{1,0:T(8,128)(2,1)S(1)}, bf16[16,1024]{1,0:T(8,128)(2,1)S(1)}, u32[]{:S(2)}, u32[]{:S(2)}) collective-permute-start(bf16[16,1024]{1,0:T(8,128)(2,1)S(1)} %pad_maximum_fusion.28), channel_id=1, source_target_pairs={{0,2},{2,4},{4,6},{6,8},{8,10},{10,12},{12,14},{14,16},{16,18},{18... | collective-permute-start | bytes 98312 | tf_op jit(solution)/shard_map/ppermute | solution.py:16
  443.2 10.1 %collective-permute-start.9 = (bf16[64,512]{1,0:T(8,128)(2,1)S(1)}, bf16[64,512]{1,0:T(8,128)(2,1)S(1)}, u32[]{:S(2)}, u32[]{:S(2)}) collective-permute-start(bf16[64,512]{1,0:T(8,128)(2,1)S(1)} %convolution_convert_fusion.6), channel_id=1, source_target_pairs={{0,1},{1,0},{2,3},{3,2},{4,5},{5,4},{6,7},{7,6},{8,9},{9,8},{10,11... | collective-permute-start | bytes 196616 | tf_op jit(solution)/shard_map/ppermute | solution.py:11
  453.2 11.9 %collective-permute-start.10 = (bf16[16,1024]{1,0:T(8,128)(2,1)S(1)}, bf16[16,1024]{1,0:T(8,128)(2,1)S(1)}, u32[]{:S(2)}, u32[]{:S(2)}) collective-permute-start(bf16[16,1024]{1,0:T(8,128)(2,1)S(1)} %pad_maximum_fusion.27), channel_id=1, source_target_pairs={{0,2},{2,4},{4,6},{6,8},{8,10},{10,12},{12,14},{14,16},{16,18},{18... | collective-permute-start | bytes 98312 | tf_op jit(solution)/shard_map/ppermute | solution.py:16
  (19 other events, 96.7 us)

commit v2 on v1

v2 whole, which is shorter than its diff:
```python
import functools

import jax
import jax.numpy as jnp
from jax import lax
from jax.experimental import pallas as pl
from jax.experimental.pallas import tpu as pltpu
from jax.sharding import PartitionSpec as P

BF16 = jnp.bfloat16
F32 = jnp.float32
QUARTERS = 4
BACK = 16
LANES = 128
VMEM = pltpu.VMEM
HBM = pltpu.HBM
SMEM = pltpu.SMEM


def dot(a, b):
    return jnp.dot(a, b, preferred_element_type=F32)


def dot_t(a, b):
    return lax.dot_general(a, b, (((1,), (1,)), ((), ())), preferred_element_type=F32)


def swapped(block, axis):
    return lax.ppermute(block, axis, [(0, 1), (1, 0)])


def passed_along(block):
    count = lax.axis_size("rows")
    return lax.ppermute(block, "rows", [(i, i + 1) for i in range(count - 1)])


def call(kernel, outs, *args, scratch=(), flops=0, places=None, out_places=None, grant=40):
    single = not isinstance(outs, (list, tuple))
    listed = [outs] if single else list(outs)
    moved = sum(a.size * a.dtype.itemsize for a in args)
    moved += sum(o.size * o.dtype.itemsize for o in listed)
    places = places or [VMEM] * len(args)
    out_places = out_places or [VMEM] * len(listed)
    specs = [pl.BlockSpec(memory_space=p) for p in places]
    out_specs = [pl.BlockSpec(memory_space=p) for p in out_places]
    return pl.pallas_call(
        kernel,
        out_shape=outs,
        in_specs=specs,
        out_specs=out_specs[0] if single else out_specs,
        scratch_shapes=list(scratch),
        compiler_params=pltpu.CompilerParams(vmem_limit_bytes=grant * 1024 * 1024),
        cost_estimate=pl.CostEstimate(flops=flops, bytes_accessed=moved, transcendentals=0),
    )(*args)


def shaped(shape, dtype):
    return jax.ShapeDtypeStruct(shape, dtype)


def pack_kernel(seg_ref, state_ref, gain_ref, gate_ref, up_ref, out_ref):
    rows, half = state_ref.shape
    top = rows // 2
    share = gate_ref.shape[0] // 2
    out_ref[:top, :half] = state_ref[:top, :]
    out_ref[:top, half:] = state_ref[top:, :]
    gain = gain_ref[...]
    high = gain.astype(BF16)
    rest = gain - high.astype(F32)
    middle = rest.astype(BF16)
    low = (rest - middle.astype(F32)).astype(BF16)
    row = lax.broadcasted_iota(jnp.int32, (BACK, half), 0)
    terms = jnp.zeros((BACK, half), F32)
    for i, term in enumerate((high, middle, low)):
        terms = jnp.where(row == i, term.astype(F32), terms)
    out_ref[top : top + BACK, :half] = terms.astype(BF16)
    out_ref[top : top + BACK, half:] = terms.astype(BF16)
    place = top + BACK
    for ref in (gate_ref, up_ref):
        out_ref[place : place + share, :] = ref[pl.ds(seg_ref[0, 0] * share, share), :]
        place += share


def unpack_kernel(mp_ref, mine_ref, other_ref, x_ref, gain_ref):
    rows = x_ref.shape[0] // QUARTERS
    width = x_ref.shape[1]
    top = rows // 2
    ours = mp_ref[0, 0]
    for h in range(2):
        for q in range(2):
            for r in range(2):
                columns = slice((2 * r + q) * width, (2 * r + q + 1) * width)
                start = (2 * h + q) * rows + r * top
                mine = mine_ref[:top, columns].astype(F32)
                other = other_ref[:top, columns].astype(F32)
                x_ref[start : start + top, :] = jnp.where(ours == h, mine, other).astype(BF16)
            columns = slice(q * width, (q + 1) * width)
            mine = mine_ref[top : top + BACK, columns].astype(F32)
            other = other_ref[top : top + BACK, columns].astype(F32)
            terms = jnp.where(ours == h, mine, other)
            gain_ref[2 * h + q : 2 * h + q + 1, :] = (terms[0:1] + terms[1:2]) + terms[2:3]


def norm_kernel(depth, x_ref, gain_ref, pick_ref, out_ref, normed_ref, held_ref, sems):
    rows = x_ref.shape[0] // QUARTERS
    total = jnp.zeros((rows, 1), F32)
    for q in range(QUARTERS):
        part = x_ref[q * rows : (q + 1) * rows, :].astype(F32)
        total = total + jnp.sum(part * part, axis=1, keepdims=True)
    scale = lax.rsqrt(total / depth + 1e-06)
    for q in range(QUARTERS):
        part = x_ref[q * rows : (q + 1) * rows, :].astype(F32)
        normed_ref[q * rows : (q + 1) * rows, :] = (
            part * scale * gain_ref[q : q + 1, :]
        ).astype(BF16)
    normed = normed_ref[...]
    size = pick_ref.shape[0] // QUARTERS
    copies = []
    for i in range(QUARTERS):
        held_ref[i] = dot(pick_ref[i * size : (i + 1) * size, :], normed).astype(BF16)
        copy = pltpu.make_async_copy(
            held_ref.at[i], out_ref.at[pl.ds(i * size, size), :], sems.at[i]
        )
        copy.start()
        copies.append(copy)
    for copy in copies:
        copy.wait()


def weight_kernel(normed_ref, router_ref, hot_ref, spread_ref, mask_ref, out_ref):
    rows = normed_ref.shape[0] // QUARTERS
    width = normed_ref.shape[1]
    logits = jnp.zeros(hot_ref.shape, F32)
    for q in range(QUARTERS):
        logits = logits + dot(
            normed_ref[q * rows : (q + 1) * rows, :], router_ref[q * width : (q + 1) * width, :]
        )
    squashed = jnp.where(hot_ref[...] > 0.0, jax.nn.sigmoid(logits), 0.0)
    weights = squashed / jnp.sum(squashed, axis=1, keepdims=True)
    high = weights.astype(BF16)
    low = (weights - high.astype(F32)).astype(BF16)
    mask = mask_ref[...].astype(F32)
    out_ref[:rows, :] = (dot(high, spread_ref[...]) * mask).astype(BF16)
    out_ref[rows:, :] = (dot(low, spread_ref[...]) * mask).astype(BF16)


def expert_kernel(
    in_ref, gate, gate2, up, up2, down, down2, out_ref, wide_ref, held_ref, answer_ref, sems
):
    count, width = in_ref.shape
    slots = count // QUARTERS
    pieces = width // LANES
    loads = []
    for i, ref in enumerate((gate, gate2, up, up2, down, down2)):
        load = pltpu.make_async_copy(ref, held_ref.at[i], sems.at[i])
        load.start()
        loads.append(load)
    for c in range(pieces):
        wide_ref[c] = in_ref[:, c * LANES : (c + 1) * LANES].astype(F32)
    parts = []
    for q in range(QUARTERS):
        part = [wide_ref[c, pl.ds(q, slots, stride=QUARTERS), :] for c in range(pieces)]
        parts.append(jnp.concatenate(part, axis=1).astype(BF16))
    sums = []
    for i in range(4):
        loads[i].wait()
        sums.append(
            sum(dot_t(parts[q], held_ref[i, :, q * width : (q + 1) * width]) for q in range(QUARTERS))
        )
    first = (sums[0] / (1.0 + jnp.exp(-sums[0])) * sums[2]).astype(BF16)
    second = (sums[1] / (1.0 + jnp.exp(-sums[1])) * sums[3]).astype(BF16)
    loads[4].wait()
    loads[5].wait()
    for q in range(QUARTERS):
        columns = slice(q * width, (q + 1) * width)
        answer = dot(first, held_ref[4, :, columns]) + dot(second, held_ref[5, :, columns])
        for c in range(pieces):
            wide_ref[c, pl.ds(q, slots, stride=QUARTERS), :] = answer[:, c * LANES : (c + 1) * LANES]
    stores = []
    size = count // QUARTERS
    for i in range(QUARTERS):
        span = slice(i * size, (i + 1) * size)
        for c in range(pieces):
            answer_ref[i, :, c * LANES : (c + 1) * LANES] = wide_ref[c, span, :].astype(BF16)
        store = pltpu.make_async_copy(
            answer_ref.at[i], out_ref.at[pl.ds(i * size, size), :], sems.at[6 + i]
        )
        store.start()
        stores.append(store)
    for store in stores:
        store.wait()


def combine_kernel(weight_ref, back_ref, out_ref):
    rows = weight_ref.shape[0] // 2
    weights = weight_ref[...].astype(F32)
    lane = lax.broadcasted_iota(jnp.int32, weights.shape, 1) % QUARTERS
    chosen = jnp.concatenate(
        [jnp.where(lane == q, weights, 0.0).astype(BF16) for q in range(QUARTERS)], axis=0
    )
    mixed = dot(chosen, back_ref[...])
    for q in range(QUARTERS):
        start = 2 * q * rows
        out_ref[q * rows : (q + 1) * rows, :] = (
            mixed[start : start + rows] + mixed[start + rows : start + 2 * rows]
        ).astype(BF16)


def vocoder_kernel(layers, kernel, keep_ref, frame_ref, small_ref, out_ref, phase_ref, mixed_ref):
    count, channels = frame_ref.shape
    chunk = 256
    gains = 4 + layers * kernel
    blocks = [slice(c, c + chunk) for c in range(0, channels, chunk)]

    def back(value, frames):
        return value if frames == 0 else pltpu.roll(value, frames, 0)

    row = lax.broadcasted_iota(jnp.int32, (count, 1), 0)
    live = jnp.where(row < BACK, keep_ref[0, 0], 1.0)
    for block in blocks:
        now = frame_ref[:, block].astype(F32)
        before = back(now, 1)
        for p in range(2):
            phase_ref[p, :, block] = (
                small_ref[p : p + 1, block] * now + small_ref[p + 2 : p + 3, block] * before
            ).astype(BF16).astype(F32)
    for i in range(layers):
        dilation = 3**i
        sums = [jnp.zeros((count, 1), F32) for _ in range(2)]
        powers = [jnp.zeros((count, 1), F32) for _ in range(2)]
        for block in blocks:
            phases = [phase_ref[0, :, block], phase_ref[1, :, block]]
            for p in range(2):
                mixed = jnp.zeros((count, chunk), F32)
                for j in range(kernel):
                    at = p - j * dilation
                    tap = small_ref[4 + i * kernel + j : 5 + i * kernel + j, block]
                    mixed = mixed + tap * back(phases[at % 2], -(at // 2))
                mixed_ref[p, :, block] = mixed
                sums[p] = sums[p] + jnp.sum(mixed, axis=1, keepdims=True)
                powers[p] = powers[p] + jnp.sum(mixed * mixed, axis=1, keepdims=True)
        for p in range(2):
            center = sums[p] / channels
            scale = lax.rsqrt(powers[p] / channels - center * center + 1e-06)
            voice = jnp.zeros((count, 1), F32)
            for block in blocks:
                gain = small_ref[gains + i : gains + i + 1, block]
                bias = small_ref[gains + layers + i : gains + layers + i + 1, block]
                fresh = (
                    phase_ref[p, :, block]
                    + (mixed_ref[p, :, block] - center) * scale * gain
                    + bias
                )
                fresh = fresh.astype(BF16).astype(F32)
                if i < layers - 1:
                    phase_ref[p, :, block] = fresh * live
                else:
                    wave = small_ref[gains + 2 * layers : gains + 2 * layers + 1, block]
                    voice = voice + jnp.sum(fresh * wave, axis=1, keepdims=True)
            if i == layers - 1:
                out_ref[:, p : p + 1] = voice[BACK:, :]


def other_half(weight, axis):
    seg = lax.axis_index("segment")
    share = weight.shape[axis] // 2
    mine = lax.dynamic_slice_in_dim(weight, seg * share, share, axis)
    return swapped(mine, "mp")


def joined(share, axis):
    return lax.all_gather(share, "segment", axis=axis, tiled=True)


def route_kernel(per_device, offset_ref, ids_ref, *out_refs):
    steps, topk, wide = ids_ref.shape
    rows = wide // QUARTERS
    spread_ref = out_refs[-1]
    experts, columns = spread_ref.shape
    group = per_device * QUARTERS

    def iota(shape, axis):
        return lax.broadcasted_iota(jnp.int32, shape, axis)

    def ones(condition):
        return jnp.where(condition, 1.0, 0.0)

    name = iota((experts, wide), 0)
    ahead, behind = iota((wide, wide), 0), iota((wide, wide), 1)
    same = ahead // rows == behind // rows
    below = ones(same & (ahead % rows < behind % rows)).astype(BF16)
    unit = ones(iota((rows, wide), 0) == iota((rows, wide), 1)).astype(BF16)
    spread = ones(iota((experts, columns), 1) // group == iota((experts, columns), 0)).astype(BF16)
    tall = ones(iota((columns, experts), 0) // group == iota((columns, experts), 1)).astype(BF16)
    slot_row = iota((1, columns), 1) // QUARTERS % per_device
    column = iota((columns, wide), 0)
    slot_column = (column // QUARTERS % per_device).astype(F32)
    own = column % QUARTERS == iota((columns, wide), 1) // rows
    spread_ref[...] = spread
    for s in range(steps):
        hot_ref, mask_ref, pick_ref = out_refs[3 * s : 3 * s + 3]
        named = jnp.zeros((experts, wide), F32)
        for k in range(topk):
            named = named + ones(ids_ref[s, k : k + 1, :] == name)
        earlier = dot(named.astype(BF16), below)
        code = jnp.where(named > 0.0, earlier - offset_ref[0, 0], -64.0).astype(BF16)
        upright = dot_t(unit, code)
        hot_ref[...] = ones(upright > -32.0)
        mask_ref[...] = ones(dot(upright.astype(BF16), spread) == slot_row.astype(F32)).astype(BF16)
        pick_ref[...] = ones((dot(tall, code) == slot_column) & own).astype(BF16)


def on_device(
    start_state,
    expert_ids,
    norm_gain,
    w_router,
    w_gate,
    w_up,
    w_down,
    w_in,
    trans_taps,
    dw_kernels,
    ln_gain,
    ln_bias,
    w_out,
):
    seg = lax.axis_index("segment")
    mp = lax.axis_index("mp")
    rows, half = start_state.shape
    experts = w_router.shape[1]
    steps, _, topk = expert_ids.shape
    layers, kernel, channels = dw_kernels.shape
    channels = 2 * channels
    capacity = min(rows, max(2, 2 * rows * topk // experts))
    per_device = capacity // 4
    slots = experts * per_device
    offset = ((mp * 2 + seg) * per_device).astype(F32)
    depth = 2 * half
    width = depth // QUARTERS
    share = 2 * rows

    def ordered(mine, other, axis):
        return jnp.where(
            mp == 0,
            jnp.concatenate([mine, other], axis=axis),
            jnp.concatenate([other, mine], axis=axis),
        )

    gate, up, down = w_gate[0].T, w_up[0].T, w_down[0]
    part = gate.shape[0] // 2
    top = rows // 2
    packed = call(
        pack_kernel,
        shaped((top + BACK + 2 * part, depth), BF16),
        seg.astype(jnp.int32).reshape(1, 1),
        start_state,
        norm_gain[None],
        gate,
        up,
        places=[SMEM, VMEM, VMEM, VMEM, VMEM],
    )
    sent = swapped(packed, "mp")
    x, gain = call(
        unpack_kernel,
        (shaped((QUARTERS * rows, width), BF16), shaped((QUARTERS, width), F32)),
        mp.astype(jnp.int32).reshape(1, 1),
        packed[: top + BACK],
        sent[: top + BACK],
        places=[SMEM, VMEM, VMEM],
    )
    gate_share = sent[top + BACK : top + BACK + part]
    up_share = sent[top + BACK + part :]
    small = jnp.concatenate(
        [trans_taps, dw_kernels.reshape(layers * kernel, -1), ln_gain, ln_bias, w_out[None]], axis=0
    )
    small = jnp.concatenate([small, swapped(small, "mp")], axis=1)
    down_share = other_half(down, 0)
    router_share = other_half(w_router, 0)
    keep = jnp.where(lax.axis_index("rows") == 0, 0.0, 1.0).astype(F32).reshape(1, 1)

    turned = expert_ids.transpose(0, 2, 1)
    columns = slots * QUARTERS
    made = call(
        functools.partial(route_kernel, per_device),
        [
            shaped((rows, experts), F32),
            shaped((rows, columns), BF16),
            shaped((columns, QUARTERS * rows), BF16),
        ]
        * steps
        + [shaped((experts, columns), BF16)],
        offset.reshape(1, 1),
        jnp.concatenate([turned] * QUARTERS, axis=2),
        flops=4 * steps * columns * experts * QUARTERS * rows,
    )
    spread = made[-1]
    hots, masks, picks = made[:-1:3], made[1:-1:3], made[2:-1:3]
    gate2 = up2 = down2 = router = None
    frames = None
    voiced = []

    def voice(frames):
        return call(
            functools.partial(vocoder_kernel, layers, kernel),
            shaped((rows, 2), F32),
            keep,
            frames,
            small,
            scratch=[
                pltpu.VMEM((2, rows + BACK, channels), F32),
                pltpu.VMEM((2, rows + BACK, channels), F32),
            ],
            flops=20 * rows * channels * kernel,
        )

    for step in range(steps):
        hot, mask, pick = hots[step], masks[step], picks[step]
        outgoing, normed = call(
            functools.partial(norm_kernel, depth),
            (shaped((slots * QUARTERS, width), BF16), shaped((QUARTERS * rows, width), BF16)),
            x,
            gain,
            pick,
            scratch=[
                pltpu.VMEM((QUARTERS, slots, width), BF16),
                pltpu.SemaphoreType.DMA((QUARTERS,)),
            ],
            out_places=[HBM, VMEM],
            grant=60,
            flops=2 * slots * QUARTERS * QUARTERS * rows * width,
        )
        received = lax.all_to_all(
            outgoing.reshape(experts, per_device * QUARTERS, width),
            "rows",
            split_axis=0,
            concat_axis=0,
            tiled=True,
        )
        if step == 0:
            gate2, up2, down2 = joined(gate_share, 0), joined(up_share, 0), joined(down_share, 0)
            router = ordered(w_router, joined(router_share, 0), 0)
        weights = call(
            weight_kernel,
            shaped((2 * rows, slots * QUARTERS), BF16),
            normed,
            router,
            hot,
            spread,
            mask,
            flops=4 * rows * experts * (depth + slots * QUARTERS),
        )
        if frames is not None:
            received, frames, weights = lax.optimization_barrier((received, frames, weights))
        answer = call(
            expert_kernel,
            shaped((slots * QUARTERS, width), BF16),
            received.reshape(slots * QUARTERS, width),
            gate,
            gate2,
            up,
            up2,
            down,
            down2,
            scratch=[
                pltpu.VMEM((width // LANES, slots * QUARTERS, LANES), F32),
                pltpu.VMEM((6,) + gate.shape, BF16),
                pltpu.VMEM((QUARTERS, slots, width), BF16),
                pltpu.SemaphoreType.DMA((6 + QUARTERS,)),
            ],
            places=[VMEM] + [HBM] * 6,
            out_places=[HBM],
            grant=60,
            flops=12 * slots * depth * w_gate.shape[2],
        )
        back = lax.all_to_all(
            answer.reshape(experts, per_device * QUARTERS, width),
            "rows",
            split_axis=0,
            concat_axis=0,
            tiled=True,
        )
        if frames is not None:
            sound = voice(frames)
            back, sound = lax.optimization_barrier((back, sound))
            voiced.append(sound)
        partial = call(
            combine_kernel,
            shaped((QUARTERS * rows, width), BF16),
            weights,
            back.reshape(slots * QUARTERS, width),
            flops=4 * slots * QUARTERS * QUARTERS * rows * width,
        )
        chip = lax.all_gather(partial, "segment", axis=0)
        chip = lax.dynamic_slice_in_dim(chip, seg * share, share, 1).astype(F32)
        chip = (chip[0] + chip[1]).astype(BF16)
        total = lax.all_gather(chip, "mp", axis=0).astype(F32)
        mine = lax.dynamic_slice_in_dim(x, seg * share, share, 0).astype(F32)
        fresh = (mine + (total[0] + total[1])).astype(BF16)
        x = lax.all_gather(fresh, "segment", axis=0, tiled=True)

        own = sum(
            dot(x[q * rows : (q + 1) * rows], w_in[q * width : (q + 1) * width])
            for q in range(QUARTERS)
        ).astype(BF16)
        frames = jnp.concatenate([own, swapped(own, "mp")], axis=1)
        frames = jnp.concatenate([passed_along(frames[-BACK:]), frames], axis=0)
    voiced.append(voice(frames))
    audio = jnp.stack([v.reshape(2 * rows) for v in voiced], axis=0)
    audio = jnp.where(seg == 0, jnp.zeros_like(audio), audio)[None]
    state = lax.dynamic_slice_in_dim(x, mp * share, share, 0)
    state = jnp.concatenate([state[:rows], state[rows:]], axis=1)
    return state, audio


def solution(mesh):
    return jax.shard_map(
        on_device,
        mesh=mesh,
        in_specs=(
            P("rows", "mp"),
            P(None, "rows", None),
            P("mp"),
            P("mp", None),
            P("rows", None, "mp"),
            P("rows", None, "mp"),
            P("rows", "mp", None),
            P(None, "mp"),
            P(None, "mp"),
            P(None, None, "mp"),
            P(None, "mp"),
            P(None, "mp"),
            P("mp"),
        ),
        out_specs=(P("rows", "mp"), P("segment", None, "rows")),
        check_vma=False,
    )
```

time: 537 us -> 443 us (0.82)
  the two profiles are of different devices: /device:TPU:256 before, /device:TPU:65 now
where the time goes in v2:
time: 443 us; the launch traced here: 440 us
  waiting for transfers between devices  198 us (45%)
  starting transfers between devices  113 us (26%)
  blocking collectives  71.8 us (16%)
  Pallas kernels  41.1 us (9%)
  local copies, waits for them, and re-layouts  11.1 us (3%)
    ppermute x7, waiting for transfers between devices, swapped(): return lax.ppermute(block, axis, [(0, 1), (1, 0)])  131 us
    all_to_all x3, waiting for transfers between devices, on_device(): lax.all_to_all(answer.reshape(experts, per_device * QUARTERS, width), 'ro...  45 us
    pallas_call x18, Pallas kernels, call(): pl.pallas_call(kernel, out_shape=outs, in_specs=specs, out_specs=out_spec...  41.1 us
    all_to_all x3, starting transfers between devices, on_device(): lax.all_to_all(outgoing.reshape(experts, per_device * QUARTERS, width), '...  40.3 us
    all_gather x3, blocking collectives, on_device(): total = lax.all_gather(chip, 'mp', axis=0).astype(F32)  38.1 us
    ppermute x7, starting transfers between devices, swapped(): return lax.ppermute(block, axis, [(0, 1), (1, 0)])  35 us
    all_to_all x3, starting transfers between devices, on_device(): lax.all_to_all(answer.reshape(experts, per_device * QUARTERS, width), 'ro...  29 us
    ppermute x3, waiting for transfers between devices, passed_along(): return lax.ppermute(block, 'rows', [(i, i + 1) for i in range(count - 1)])  18.3 us
  transfers between devices with their start and end apart: 16, of which 16 were waited for; matrix products, arithmetic and copies ran while one was open for 1% of the time, Pallas kernels for 1%

profile of v2, /device:TPU:65, one launch (start us, length us, event | category | flops | bytes accessed | tf_op | source)
XLA Modules:
  0.0 440.0 jit_solution(15489522534001713869)
XLA Ops:
  4.6 7.5 %collective-permute-start = (bf16[240,2048]{1,0:T(8,128)(2,1)S(1)}, bf16[240,2048]{1,0:T(8,128)(2,1)}, u32[]{:S(2)}, u32[]{:S(2)}) collective-permute-start(bf16[240,2048]{1,0:T(8,128)(2,1)S(1)} %shard_map.140), channel_id=1, source_target_pairs={{0,1},{1,0},{2,3},{3,2},{4,5},{5,4},{6,7},{7,6},{8,9},{9,8},{10,11... | collective-permute-start | bytes 2949128 | tf_op jit(solution)/shard_map/ppermute | solution.py:29
  15.4 29.8 %collective-permute-done = bf16[240,2048]{1,0:T(8,128)(2,1)} collective-permute-done((bf16[240,2048]{1,0:T(8,128)(2,1)S(1)}, bf16[240,2048]{1,0:T(8,128)(2,1)}, u32[]{:S(2)}, u32[]{:S(2)}) %collective-permute-start) | collective-permute-done | bytes 983072 | tf_op jit(solution)/shard_map/ppermute | solution.py:29
  50.8 25.3 %all-to-all-start = ((bf16[128,8,512]{2,1,0:T(8,128)(2,1)}), bf16[128,8,512]{2,1,0:T(8,128)(2,1)S(1)}, u32[]{:S(2)}, u32[]{:S(2)}) async-start(bf16[128,8,512]{2,1,0:T(8,128)(2,1)} %bitcast.72), calls=%async_computation | async-start | bytes 2097152 | tf_op jit(solution)/shard_map/all_to_all | solution.py:433
  80.7 29.8 %collective-permute-done.2 = bf16[96,2048]{1,0:T(8,128)(2,1)S(1)} collective-permute-done((bf16[96,2048]{1,0:T(8,128)(2,1)S(1)}, bf16[96,2048]{1,0:T(8,128)(2,1)S(1)}, u32[]{:S(2)}, u32[]{:S(2)}) %collective-permute-start.2) | collective-permute-done | bytes 393248 | tf_op jit(solution)/shard_map/ppermute | solution.py:29
  123.7 7.0 %shard_map.145 = bf16[1024,512]{1,0:T(8,128)(2,1)} custom-call(bf16[1024,512]{1,0:T(8,128)(2,1)} %bitcast.65, bf16[192,2048]{1,0:T(8,128)(2,1)} %bitcast.49, bf16[192,2048]{1,0:T(8,128)(2,1)} %all_gather.52.gate2, bf16[192,2048]{1,0:T(8,128)(2,1)} %bitcast.53, bf16[192,2048]{1,0:T(8,128)(2,1)} %all_gather.53.up2, bf16[192,2048]{1,0:T(8,128)(2,1)} %bitcast.61, ...), custom_call_target="tpu_custom_call" | custom-call | flops 1207959552 | bytes 6815744 | tf_op jit(solution)/shard_map/pallas_call | solution.py:46
  130.8 12.6 %all-to-all-start.1 = ((bf16[128,8,512]{2,1,0:T(8,128)(2,1)}), bf16[128,8,512]{2,1,0:T(8,128)(2,1)S(1)}, u32[]{:S(2)}, u32[]{:S(2)}) async-start(bf16[128,8,512]{2,1,0:T(8,128)(2,1)} %bitcast.64), calls=%async_computation.1 | async-start | bytes 2097152 | tf_op jit(solution)/shard_map/all_to_all | solution.py:476
  148.1 20.0 %collective-permute-done.1 = bf16[512,128]{1,0:T(8,128)(2,1)S(1)} collective-permute-done((bf16[512,128]{1,0:T(8,128)(2,1)S(1)}, bf16[512,128]{1,0:T(8,128)(2,1)S(1)}, u32[]{:S(2)}, u32[]{:S(2)}) %collective-permute-start.1) | collective-permute-done | bytes 131104 | tf_op jit(solution)/shard_map/ppermute | solution.py:29
  171.8 7.0 %all-to-all-done.1 = bf16[128,8,512]{2,1,0:T(8,128)(2,1)S(1)} async-done(((bf16[128,8,512]{2,1,0:T(8,128)(2,1)}), bf16[128,8,512]{2,1,0:T(8,128)(2,1)S(1)}, u32[]{:S(2)}, u32[]{:S(2)}) %all-to-all-start.1) | async-done | bytes 1048608 | tf_op jit(solution)/shard_map/all_to_all | solution.py:476
  183.8 12.7 %all_gather.57 = bf16[2,128,512]{2,1,0:T(8,128)(2,1)S(1)} all-gather(bf16[1,128,512]{2,1,0:T(8,128)(2,1)S(1)} %fusion.29), channel_id=1, replica_groups=mesh['segment'=2,'rows'=128,'mp'=2] {'mp'}, dimensions={0}, use_global_device_ids=true | all-gather | bytes 393216 | tf_op jit(solution)/shard_map/all_gather | solution.py:497
  202.3 7.6 %all-to-all-start.2 = ((bf16[128,8,512]{2,1,0:T(8,128)(2,1)}), bf16[128,8,512]{2,1,0:T(8,128)(2,1)}, u32[]{:S(2)}, u32[]{:S(2)}) async-start(bf16[128,8,512]{2,1,0:T(8,128)(2,1)} %bitcast.73), calls=%async_computation.2 | async-start | bytes 2097152 | tf_op jit(solution)/shard_map/all_to_all | solution.py:433
  215.4 16.3 %collective-permute-done.3 = bf16[64,512]{1,0:T(8,128)(2,1)S(1)} collective-permute-done((bf16[64,512]{1,0:T(8,128)(2,1)S(1)}, bf16[64,512]{1,0:T(8,128)(2,1)S(1)}, u32[]{:S(2)}, u32[]{:S(2)}) %collective-permute-start.3) | collective-permute-done | bytes 65568 | tf_op jit(solution)/shard_map/ppermute | solution.py:29
  235.3 6.0 %collective-permute-done.4 = bf16[16,1024]{1,0:T(8,128)(2,1)S(1)} collective-permute-done((bf16[16,1024]{1,0:T(8,128)(2,1)S(1)}, bf16[16,1024]{1,0:T(8,128)(2,1)S(1)}, u32[]{:S(2)}, u32[]{:S(2)}) %collective-permute-start.4) | collective-permute-done | bytes 32800 | tf_op jit(solution)/shard_map/ppermute | solution.py:34
  242.6 7.0 %shard_map.149 = bf16[1024,512]{1,0:T(8,128)(2,1)} custom-call(bf16[1024,512]{1,0:T(8,128)(2,1)} %bitcast.20.in_ref, bf16[192,2048]{1,0:T(8,128)(2,1)} %bitcast.50, bf16[192,2048]{1,0:T(8,128)(2,1)} %all_gather.52.gate2, bf16[192,2048]{1,0:T(8,128)(2,1)} %bitcast.54, bf16[192,2048]{1,0:T(8,128)(2,1)} %all_gather.53.up2, bf16[192,2048]{1,0:T(8,128)(2,1)} %bitcast.62, ...), custom_call_target="tpu_custom_call" | custom-call | flops 1207959552 | bytes 6815744 | tf_op jit(solution)/shard_map/pallas_call | solution.py:46
  249.7 8.2 %all-to-all-start.3 = ((bf16[128,8,512]{2,1,0:T(8,128)(2,1)}), bf16[128,8,512]{2,1,0:T(8,128)(2,1)S(1)}, u32[]{:S(2)}, u32[]{:S(2)}) async-start(bf16[128,8,512]{2,1,0:T(8,128)(2,1)} %bitcast.66), calls=%async_computation.3 | async-start | bytes 2097152 | tf_op jit(solution)/shard_map/all_to_all | solution.py:476
  262.8 14.3 %collective-permute-done.5 = f32[23,512]{1,0:T(8,128)S(1)} collective-permute-done((f32[23,512]{1,0:T(8,128)S(1)}, f32[23,512]{1,0:T(8,128)S(1)}, u32[]{:S(2)}, u32[]{:S(2)}) %collective-permute-start.5) | collective-permute-done | bytes 47136 | tf_op jit(solution)/shard_map/ppermute | solution.py:29
  278.8 10.5 %all-to-all-done.3 = bf16[128,8,512]{2,1,0:T(8,128)(2,1)S(1)} async-done(((bf16[128,8,512]{2,1,0:T(8,128)(2,1)}), bf16[128,8,512]{2,1,0:T(8,128)(2,1)S(1)}, u32[]{:S(2)}, u32[]{:S(2)}) %all-to-all-start.3) | async-done | bytes 1048608 | tf_op jit(solution)/shard_map/all_to_all | solution.py:476
  294.7 12.6 %all_gather.61 = bf16[2,128,512]{2,1,0:T(8,128)(2,1)S(1)} all-gather(bf16[1,128,512]{2,1,0:T(8,128)(2,1)S(1)} %fusion.25), channel_id=1, replica_groups=mesh['segment'=2,'rows'=128,'mp'=2] {'mp'}, dimensions={0}, use_global_device_ids=true | all-gather | bytes 393216 | tf_op jit(solution)/shard_map/all_gather | solution.py:497
  313.3 7.4 %all-to-all-start.4 = ((bf16[128,8,512]{2,1,0:T(8,128)(2,1)}), bf16[128,8,512]{2,1,0:T(8,128)(2,1)}, u32[]{:S(2)}, u32[]{:S(2)}) async-start(bf16[128,8,512]{2,1,0:T(8,128)(2,1)} %bitcast.71), calls=%async_computation.4 | async-start | bytes 2097152 | tf_op jit(solution)/shard_map/all_to_all | solution.py:433
  326.2 16.3 %collective-permute-done.6 = bf16[64,512]{1,0:T(8,128)(2,1)S(1)} collective-permute-done((bf16[64,512]{1,0:T(8,128)(2,1)S(1)}, bf16[64,512]{1,0:T(8,128)(2,1)S(1)}, u32[]{:S(2)}, u32[]{:S(2)}) %collective-permute-start.6) | collective-permute-done | bytes 65568 | tf_op jit(solution)/shard_map/ppermute | solution.py:29
  353.4 7.0 %shard_map.154 = bf16[1024,512]{1,0:T(8,128)(2,1)} custom-call(bf16[1024,512]{1,0:T(8,128)(2,1)} %bitcast.28.in_ref, bf16[192,2048]{1,0:T(8,128)(2,1)} %bitcast.51, bf16[192,2048]{1,0:T(8,128)(2,1)} %all_gather.52.gate2, bf16[192,2048]{1,0:T(8,128)(2,1)} %bitcast.55, bf16[192,2048]{1,0:T(8,128)(2,1)} %all_gather.53.up2, bf16[192,2048]{1,0:T(8,128)(2,1)} %bitcast.63, ...), custom_call_target="tpu_custom_call" | custom-call | flops 1207959552 | bytes 6815744 | tf_op jit(solution)/shard_map/pallas_call | solution.py:46
  360.4 8.2 %all-to-all-start.5 = ((bf16[128,8,512]{2,1,0:T(8,128)(2,1)}), bf16[128,8,512]{2,1,0:T(8,128)(2,1)S(1)}, u32[]{:S(2)}, u32[]{:S(2)}) async-start(bf16[128,8,512]{2,1,0:T(8,128)(2,1)} %bitcast.67), calls=%async_computation.5 | async-start | bytes 2097152 | tf_op jit(solution)/shard_map/all_to_all | solution.py:476
  370.3 27.5 %all-to-all-done.5 = bf16[128,8,512]{2,1,0:T(8,128)(2,1)S(1)} async-done(((bf16[128,8,512]{2,1,0:T(8,128)(2,1)}), bf16[128,8,512]{2,1,0:T(8,128)(2,1)S(1)}, u32[]{:S(2)}, u32[]{:S(2)}) %all-to-all-start.5) | async-done | bytes 1048608 | tf_op jit(solution)/shard_map/all_to_all | solution.py:476
  403.2 12.8 %all_gather.65 = bf16[2,128,512]{2,1,0:T(8,128)(2,1)S(1)} all-gather(bf16[1,128,512]{2,1,0:T(8,128)(2,1)S(1)} %fusion.21), channel_id=1, replica_groups=mesh['segment'=2,'rows'=128,'mp'=2] {'mp'}, dimensions={0}, use_global_device_ids=true | all-gather | bytes 393216 | tf_op jit(solution)/shard_map/all_gather | solution.py:497
  431.2 6.4 %collective-permute-done.9 = bf16[16,1024]{1,0:T(8,128)(2,1)S(1)} collective-permute-done((bf16[16,1024]{1,0:T(8,128)(2,1)S(1)}, bf16[16,1024]{1,0:T(8,128)(2,1)S(1)}, u32[]{:S(2)}, u32[]{:S(2)}) %collective-permute-start.9) | collective-permute-done | bytes 32800 | tf_op jit(solution)/shard_map/ppermute | solution.py:34
  (141 shorter events, 118.7 us)
Async XLA Ops:
  4.6 40.6 %collective-permute-start = (bf16[240,2048]{1,0:T(8,128)(2,1)S(1)}, bf16[240,2048]{1,0:T(8,128)(2,1)}, u32[]{:S(2)}, u32[]{:S(2)}) collective-permute-start(bf16[240,2048]{1,0:T(8,128)(2,1)S(1)} %shard_map.140), channel_id=1, source_target_pairs={{0,1},{1,0},{2,3},{3,2},{4,5},{5,4},{6,7},{7,6},{8,9},{9,8},{10,11... | collective-permute-start | bytes 2949128 | tf_op jit(solution)/shard_map/ppermute | solution.py:29
  15.4 60.8 %copy-start.10 = (bf16[1024,256]{1,0:T(8,128)(2,1)}, bf16[1024,256]{1,0:T(8,128)(2,1)S(1)}, u32[]{:S(2)}) copy-start(bf16[1024,256]{1,0:T(8,128)(2,1)S(1)} %get-tuple-element.47.pick_ref) | copy-start | bytes 1572868
  15.4 60.7 %copy-start.16 = (bf16[1,192,2048]{2,1,0:T(8,128)(2,1)S(1)}, bf16[1,192,2048]{2,1,0:T(8,128)(2,1)}, u32[]{:S(2)}) copy-start(bf16[1,192,2048]{2,1,0:T(8,128)(2,1)} %param.19) | copy-start | bytes 2359300
  50.8 71.9 %all-to-all-start = ((bf16[128,8,512]{2,1,0:T(8,128)(2,1)}), bf16[128,8,512]{2,1,0:T(8,128)(2,1)S(1)}, u32[]{:S(2)}, u32[]{:S(2)}) async-start(bf16[128,8,512]{2,1,0:T(8,128)(2,1)} %bitcast.72), calls=%async_computation | async-start | bytes 2097152 | tf_op jit(solution)/shard_map/all_to_all | solution.py:433
  76.2 34.4 %collective-permute-start.2 = (bf16[96,2048]{1,0:T(8,128)(2,1)S(1)}, bf16[96,2048]{1,0:T(8,128)(2,1)S(1)}, u32[]{:S(2)}, u32[]{:S(2)}) collective-permute-start(bf16[96,2048]{1,0:T(8,128)(2,1)S(1)} %dynamic-slice_bitcast_fusion), channel_id=1, source_target_pairs={{0,1},{1,0},{2,3},{3,2},{4,5},{5,4},{6,7},{7,6},{8,9},{9,8},{10,11... | collective-permute-start | bytes 1179656 | tf_op jit(solution)/shard_map/ppermute | solution.py:29
  130.8 40.6 %copy-start.2 = (bf16[256,512]{1,0:T(8,128)(2,1)S(1)}, bf16[256,512]{1,0:T(8,128)(2,1)}, u32[]{:S(2)}) copy-start(bf16[256,512]{1,0:T(8,128)(2,1)} %get-tuple-element.33.normed_ref) | copy-start | bytes 786436
  130.8 48.0 %all-to-all-start.1 = ((bf16[128,8,512]{2,1,0:T(8,128)(2,1)}), bf16[128,8,512]{2,1,0:T(8,128)(2,1)S(1)}, u32[]{:S(2)}, u32[]{:S(2)}) async-start(bf16[128,8,512]{2,1,0:T(8,128)(2,1)} %bitcast.64), calls=%async_computation.1 | async-start | bytes 2097152 | tf_op jit(solution)/shard_map/all_to_all | solution.py:476
  143.4 24.6 %collective-permute-start.1 = (bf16[512,128]{1,0:T(8,128)(2,1)S(1)}, bf16[512,128]{1,0:T(8,128)(2,1)S(1)}, u32[]{:S(2)}, u32[]{:S(2)}) collective-permute-start(bf16[512,128]{1,0:T(8,128)(2,1)S(1)} %constant_dynamic-slice_fusion.2), channel_id=1, source_target_pairs={{0,1},{1,0},{2,3},{3,2},{4,5},{5,4},{6,7},{7,6},{8,9},{9,8},{10,11... | collective-permute-start | bytes 393224 | tf_op jit(solution)/shard_map/ppermute | solution.py:29
  179.5 17.1 %copy-start.7 = (bf16[256,512]{1,0:T(8,128)(2,1)S(1)}, bf16[256,512]{1,0:T(8,128)(2,1)}, u32[]{:S(2)}) copy-start(bf16[256,512]{1,0:T(8,128)(2,1)} %copy-done.6) | copy-start | bytes 786436
  202.3 40.3 %all-to-all-start.2 = ((bf16[128,8,512]{2,1,0:T(8,128)(2,1)}), bf16[128,8,512]{2,1,0:T(8,128)(2,1)}, u32[]{:S(2)}, u32[]{:S(2)}) async-start(bf16[128,8,512]{2,1,0:T(8,128)(2,1)} %bitcast.73), calls=%async_computation.2 | async-start | bytes 2097152 | tf_op jit(solution)/shard_map/all_to_all | solution.py:433
  210.0 24.8 %copy-start.4 = (bf16[256,512]{1,0:T(8,128)(2,1)S(1)}, bf16[256,512]{1,0:T(8,128)(2,1)}, u32[]{:S(2)}) copy-start(bf16[256,512]{1,0:T(8,128)(2,1)} %get-tuple-element.40.normed_ref) | copy-start | bytes 786436
  210.8 20.9 %collective-permute-start.3 = (bf16[64,512]{1,0:T(8,128)(2,1)S(1)}, bf16[64,512]{1,0:T(8,128)(2,1)S(1)}, u32[]{:S(2)}, u32[]{:S(2)}) collective-permute-start(bf16[64,512]{1,0:T(8,128)(2,1)S(1)} %fusion), channel_id=1, source_target_pairs={{0,1},{1,0},{2,3},{3,2},{4,5},{5,4},{6,7},{7,6},{8,9},{9,8},{10,11... | collective-permute-start | bytes 196616 | tf_op jit(solution)/shard_map/ppermute | solution.py:29
  231.7 9.6 %collective-permute-start.4 = (bf16[16,1024]{1,0:T(8,128)(2,1)S(1)}, bf16[16,1024]{1,0:T(8,128)(2,1)S(1)}, u32[]{:S(2)}, u32[]{:S(2)}) collective-permute-start(bf16[16,1024]{1,0:T(8,128)(2,1)S(1)} %pad_maximum_fusion.4), channel_id=1, source_target_pairs={{0,2},{2,4},{4,6},{6,8},{8,10},{10,12},{12,14},{14,16},{16,18},{18... | collective-permute-start | bytes 98312 | tf_op jit(solution)/shard_map/ppermute | solution.py:34
  249.7 39.6 %all-to-all-start.3 = ((bf16[128,8,512]{2,1,0:T(8,128)(2,1)}), bf16[128,8,512]{2,1,0:T(8,128)(2,1)S(1)}, u32[]{:S(2)}, u32[]{:S(2)}) async-start(bf16[128,8,512]{2,1,0:T(8,128)(2,1)} %bitcast.66), calls=%async_computation.3 | async-start | bytes 2097152 | tf_op jit(solution)/shard_map/all_to_all | solution.py:476
  258.2 19.0 %collective-permute-start.5 = (f32[23,512]{1,0:T(8,128)S(1)}, f32[23,512]{1,0:T(8,128)S(1)}, u32[]{:S(2)}, u32[]{:S(2)}) collective-permute-start(f32[23,512]{1,0:T(8,128)S(1)} %concatenate.48), channel_id=1, source_target_pairs={{0,1},{1,0},{2,3},{3,2},{4,5},{5,4},{6,7},{7,6},{8,9},{9,8},{10,11... | collective-permute-start | bytes 141320 | tf_op jit(solution)/shard_map/ppermute | solution.py:29
  307.3 13.4 %copy-start.14 = (bf16[2048,512]{1,0:T(8,128)(2,1)S(1)}, bf16[2048,512]{1,0:T(8,128)(2,1)}, u32[]{:S(2)}) copy-start(bf16[2048,512]{1,0:T(8,128)(2,1)} %param.20) | copy-start | bytes 6291460
  313.3 40.1 %all-to-all-start.4 = ((bf16[128,8,512]{2,1,0:T(8,128)(2,1)}), bf16[128,8,512]{2,1,0:T(8,128)(2,1)}, u32[]{:S(2)}, u32[]{:S(2)}) async-start(bf16[128,8,512]{2,1,0:T(8,128)(2,1)} %bitcast.71), calls=%async_computation.4 | async-start | bytes 2097152 | tf_op jit(solution)/shard_map/all_to_all | solution.py:433
  320.7 25.1 %copy-start.3 = (bf16[256,512]{1,0:T(8,128)(2,1)S(1)}, bf16[256,512]{1,0:T(8,128)(2,1)}, u32[]{:S(2)}) copy-start(bf16[256,512]{1,0:T(8,128)(2,1)} %get-tuple-element.49.normed_ref) | copy-start | bytes 786436
  321.6 21.0 %collective-permute-start.6 = (bf16[64,512]{1,0:T(8,128)(2,1)S(1)}, bf16[64,512]{1,0:T(8,128)(2,1)S(1)}, u32[]{:S(2)}, u32[]{:S(2)}) collective-permute-start(bf16[64,512]{1,0:T(8,128)(2,1)S(1)} %fusion.1), channel_id=1, source_target_pairs={{0,1},{1,0},{2,3},{3,2},{4,5},{5,4},{6,7},{7,6},{8,9},{9,8},{10,11... | collective-permute-start | bytes 196616 | tf_op jit(solution)/shard_map/ppermute | solution.py:29
  342.5 9.6 %collective-permute-start.7 = (bf16[16,1024]{1,0:T(8,128)(2,1)S(1)}, bf16[16,1024]{1,0:T(8,128)(2,1)S(1)}, u32[]{:S(2)}, u32[]{:S(2)}) collective-permute-start(bf16[16,1024]{1,0:T(8,128)(2,1)S(1)} %pad_maximum_fusion.3), channel_id=1, source_target_pairs={{0,2},{2,4},{4,6},{6,8},{8,10},{10,12},{12,14},{14,16},{16,18},{18... | collective-permute-start | bytes 98312 | tf_op jit(solution)/shard_map/ppermute | solution.py:34
  360.4 37.5 %all-to-all-start.5 = ((bf16[128,8,512]{2,1,0:T(8,128)(2,1)}), bf16[128,8,512]{2,1,0:T(8,128)(2,1)S(1)}, u32[]{:S(2)}, u32[]{:S(2)}) async-start(bf16[128,8,512]{2,1,0:T(8,128)(2,1)} %bitcast.67), calls=%async_computation.5 | async-start | bytes 2097152 | tf_op jit(solution)/shard_map/all_to_all | solution.py:476
  403.1 15.3 %copy-start.15 = (bf16[2048,512]{1,0:T(8,128)(2,1)S(1)}, bf16[2048,512]{1,0:T(8,128)(2,1)}, u32[]{:S(2)}) copy-start(bf16[2048,512]{1,0:T(8,128)(2,1)} %param.20) | copy-start | bytes 6291460
  419.3 8.9 %collective-permute-start.8 = (bf16[64,512]{1,0:T(8,128)(2,1)S(1)}, bf16[64,512]{1,0:T(8,128)(2,1)S(1)}, u32[]{:S(2)}, u32[]{:S(2)}) collective-permute-start(bf16[64,512]{1,0:T(8,128)(2,1)S(1)} %fusion.2), channel_id=1, source_target_pairs={{0,1},{1,0},{2,3},{3,2},{4,5},{5,4},{6,7},{7,6},{8,9},{9,8},{10,11... | collective-permute-start | bytes 196616 | tf_op jit(solution)/shard_map/ppermute | solution.py:29
  428.2 9.5 %collective-permute-start.9 = (bf16[16,1024]{1,0:T(8,128)(2,1)S(1)}, bf16[16,1024]{1,0:T(8,128)(2,1)S(1)}, u32[]{:S(2)}, u32[]{:S(2)}) collective-permute-start(bf16[16,1024]{1,0:T(8,128)(2,1)S(1)} %pad_maximum_fusion.2), channel_id=1, source_target_pairs={{0,2},{2,4},{4,6},{6,8},{8,10},{10,12},{12,14},{14,16},{16,18},{18... | collective-permute-start | bytes 98312 | tf_op jit(solution)/shard_map/ppermute | solution.py:34
  (19 other events, 108.1 us)

commit v3 on v2

--- a/solution.py
+++ b/solution.py
@@ -13,7 +13,6 @@
 BACK = 16
 LANES = 128
 VMEM = pltpu.VMEM
-HBM = pltpu.HBM
 SMEM = pltpu.SMEM
 
 
@@ -29,20 +28,24 @@
     return lax.ppermute(block, axis, [(0, 1), (1, 0)])
 
 
-def passed_along(block):
+def voiced_swap(block):
+    return lax.ppermute(block, ("segment", "mp"), [(2, 3), (3, 2)])
+
+
+def voiced_pass(block):
     count = lax.axis_size("rows")
-    return lax.ppermute(block, "rows", [(i, i + 1) for i in range(count - 1)])
-
-
-def call(kernel, outs, *args, scratch=(), flops=0, places=None, out_places=None, grant=40):
+    route = [(count + i, count + i + 1) for i in range(count - 1)]
+    return lax.ppermute(block, ("segment", "rows"), route)
+
+
+def call(kernel, outs, *args, scratch=(), flops=0, places=None, grant=10):
     single = not isinstance(outs, (list, tuple))
     listed = [outs] if single else list(outs)
     moved = sum(a.size * a.dtype.itemsize for a in args)
     moved += sum(o.size * o.dtype.itemsize for o in listed)
     places = places or [VMEM] * len(args)
-    out_places = out_places or [VMEM] * len(listed)
     specs = [pl.BlockSpec(memory_space=p) for p in places]
-    out_specs = [pl.BlockSpec(memory_space=p) for p in out_places]
+    out_specs = [pl.BlockSpec(memory_space=VMEM)] * len(listed)
     return pl.pallas_call(
         kernel,
         out_shape=outs,
@@ -58,7 +61,7 @@
     return jax.ShapeDtypeStruct(shape, dtype)
 
 
-def pack_kernel(seg_ref, state_ref, gain_ref, gate_ref, up_ref, out_ref):
+def pack_kernel(seg_ref, state_ref, gain_ref, gate_ref, up_ref, down_ref, out_ref):
     rows, half = state_ref.shape
     top = rows // 2
     share = gate_ref.shape[0] // 2
@@ -76,7 +79,7 @@
     out_ref[top : top + BACK, :half] = terms.astype(BF16)
     out_ref[top : top + BACK, half:] = terms.astype(BF16)
     place = top + BACK
-    for ref in (gate_ref, up_ref):
+    for ref in (gate_ref, up_ref, down_ref):
         out_ref[place : place + share, :] = ref[pl.ds(seg_ref[0, 0] * share, share), :]
         place += share
 
@@ -101,7 +104,7 @@
             gain_ref[2 * h + q : 2 * h + q + 1, :] = (terms[0:1] + terms[1:2]) + terms[2:3]
 
 
-def norm_kernel(depth, x_ref, gain_ref, pick_ref, out_ref, normed_ref, held_ref, sems):
+def norm_kernel(depth, x_ref, gain_ref, pick_ref, out_ref, normed_ref):
     rows = x_ref.shape[0] // QUARTERS
     total = jnp.zeros((rows, 1), F32)
     for q in range(QUARTERS):
@@ -113,18 +116,7 @@
         normed_ref[q * rows : (q + 1) * rows, :] = (
             part * scale * gain_ref[q : q + 1, :]
         ).astype(BF16)
-    normed = normed_ref[...]
-    size = pick_ref.shape[0] // QUARTERS
-    copies = []
-    for i in range(QUARTERS):
-        held_ref[i] = dot(pick_ref[i * size : (i + 1) * size, :], normed).astype(BF16)
-        copy = pltpu.make_async_copy(
-            held_ref.at[i], out_ref.at[pl.ds(i * size, size), :], sems.at[i]
-        )
-        copy.start()
-        copies.append(copy)
-    for copy in copies:
-        copy.wait()
+    out_ref[...] = dot(pick_ref[...], normed_ref[...]).astype(BF16)
 
 
 def weight_kernel(normed_ref, router_ref, hot_ref, spread_ref, mask_ref, out_ref):
@@ -145,50 +137,31 @@
 
 
 def expert_kernel(
-    in_ref, gate, gate2, up, up2, down, down2, out_ref, wide_ref, held_ref, answer_ref, sems
+    in_ref, gate_ref, gate2_ref, up_ref, up2_ref, down_ref, down2_ref, out_ref, wide_ref
 ):
     count, width = in_ref.shape
     slots = count // QUARTERS
+    lanes = gate_ref.shape[0]
     pieces = width // LANES
-    loads = []
-    for i, ref in enumerate((gate, gate2, up, up2, down, down2)):
-        load = pltpu.make_async_copy(ref, held_ref.at[i], sems.at[i])
-        load.start()
-        loads.append(load)
     for c in range(pieces):
         wide_ref[c] = in_ref[:, c * LANES : (c + 1) * LANES].astype(F32)
-    parts = []
+    sums = [jnp.zeros((slots, lanes), F32) for _ in range(4)]
     for q in range(QUARTERS):
-        part = [wide_ref[c, pl.ds(q, slots, stride=QUARTERS), :] for c in range(pieces)]
-        parts.append(jnp.concatenate(part, axis=1).astype(BF16))
-    sums = []
-    for i in range(4):
-        loads[i].wait()
-        sums.append(
-            sum(dot_t(parts[q], held_ref[i, :, q * width : (q + 1) * width]) for q in range(QUARTERS))
-        )
+        part = jnp.concatenate(
+            [wide_ref[c, pl.ds(q, slots, stride=QUARTERS), :] for c in range(pieces)], axis=1
+        ).astype(BF16)
+        columns = slice(q * width, (q + 1) * width)
+        for i, ref in enumerate((gate_ref, gate2_ref, up_ref, up2_ref)):
+            sums[i] = sums[i] + dot_t(part, ref[:, columns])
     first = (sums[0] / (1.0 + jnp.exp(-sums[0])) * sums[2]).astype(BF16)
     second = (sums[1] / (1.0 + jnp.exp(-sums[1])) * sums[3]).astype(BF16)
-    loads[4].wait()
-    loads[5].wait()
     for q in range(QUARTERS):
         columns = slice(q * width, (q + 1) * width)
-        answer = dot(first, held_ref[4, :, columns]) + dot(second, held_ref[5, :, columns])
+        answer = dot(first, down_ref[:, columns]) + dot(second, down2_ref[:, columns])
         for c in range(pieces):
             wide_ref[c, pl.ds(q, slots, stride=QUARTERS), :] = answer[:, c * LANES : (c + 1) * LANES]
-    stores = []
-    size = count // QUARTERS
-    for i in range(QUARTERS):
-        span = slice(i * size, (i + 1) * size)
-        for c in range(pieces):
-            answer_ref[i, :, c * LANES : (c + 1) * LANES] = wide_ref[c, span, :].astype(BF16)
-        store = pltpu.make_async_copy(
-            answer_ref.at[i], out_ref.at[pl.ds(i * size, size), :], sems.at[6 + i]
-        )
-        store.start()
-        stores.append(store)
-    for store in stores:
-        store.wait()
+    for c in range(pieces):
+        out_ref[:, c * LANES : (c + 1) * LANES] = wide_ref[c].astype(BF16)
 
 
 def combine_kernel(weight_ref, back_ref, out_ref):
@@ -352,13 +325,15 @@
     top = rows // 2
     packed = call(
         pack_kernel,
-        shaped((top + BACK + 2 * part, depth), BF16),
+        shaped((top + BACK + 3 * part, depth), BF16),
         seg.astype(jnp.int32).reshape(1, 1),
         start_state,
         norm_gain[None],
         gate,
         up,
-        places=[SMEM, VMEM, VMEM, VMEM, VMEM],
+        down,
+        places=[SMEM] + [VMEM] * 5,
+        grant=14,
     )
     sent = swapped(packed, "mp")
     x, gain = call(
@@ -369,13 +344,13 @@
         sent[: top + BACK],
         places=[SMEM, VMEM, VMEM],
     )
-    gate_share = sent[top + BACK : top + BACK + part]
-    up_share = sent[top + BACK + part :]
+    gate_share, up_share, down_share = (
+        sent[top + BACK + i * part : top + BACK + (i + 1) * part] for i in range(3)
+    )
     small = jnp.concatenate(
         [trans_taps, dw_kernels.reshape(layers * kernel, -1), ln_gain, ln_bias, w_out[None]], axis=0
     )
-    small = jnp.concatenate([small, swapped(small, "mp")], axis=1)
-    down_share = other_half(down, 0)
+    small = jnp.concatenate([small, voiced_swap(small)], axis=1)
     router_share = other_half(w_router, 0)
     keep = jnp.where(lax.axis_index("rows") == 0, 0.0, 1.0).astype(F32).reshape(1, 1)
 
@@ -392,6 +367,7 @@
         + [shaped((experts, columns), BF16)],
         offset.reshape(1, 1),
         jnp.concatenate([turned] * QUARTERS, axis=2),
+        grant=16,
         flops=4 * steps * columns * experts * QUARTERS * rows,
     )
     spread = made[-1]
@@ -422,12 +398,6 @@
             x,
             gain,
             pick,
-            scratch=[
-                pltpu.VMEM((QUARTERS, slots, width), BF16),
-                pltpu.SemaphoreType.DMA((QUARTERS,)),
-            ],
-            out_places=[HBM, VMEM],
-            grant=60,
             flops=2 * slots * QUARTERS * QUARTERS * rows * width,
         )
         received = lax.all_to_all(
@@ -462,15 +432,8 @@
             up2,
             down,
             down2,
-            scratch=[
-                pltpu.VMEM((width // LANES, slots * QUARTERS, LANES), F32),
-                pltpu.VMEM((6,) + gate.shape, BF16),
-                pltpu.VMEM((QUARTERS, slots, width), BF16),
-                pltpu.SemaphoreType.DMA((6 + QUARTERS,)),
-            ],
-            places=[VMEM] + [HBM] * 6,
-            out_places=[HBM],
-            grant=60,
+            scratch=[pltpu.VMEM((width // LANES, slots * QUARTERS, LANES), F32)],
+            grant=16,
             flops=12 * slots * depth * w_gate.shape[2],
         )
         back = lax.all_to_all(
@@ -503,8 +466,8 @@
             dot(x[q * rows : (q + 1) * rows], w_in[q * width : (q + 1) * width])
             for q in range(QUARTERS)
         ).astype(BF16)
-        frames = jnp.concatenate([own, swapped(own, "mp")], axis=1)
-        frames = jnp.concatenate([passed_along(frames[-BACK:]), frames], axis=0)
+        frames = jnp.concatenate([own, voiced_swap(own)], axis=1)
+        frames = jnp.concatenate([voiced_pass(frames[-BACK:]), frames], axis=0)
     voiced.append(voice(frames))
     audio = jnp.stack([v.reshape(2 * rows) for v in voiced], axis=0)
     audio = jnp.where(seg == 0, jnp.zeros_like(audio), audio)[None]

time: 443 us -> 435 us (0.982)
  local copies, waits for them, and re-layouts: 11.1 us -> 35.5 us
  waiting for transfers between devices: 198 us -> 176 us
  Pallas kernels: 41.1 us -> 26.5 us
  matrix products: 2.45 us -> 11.2 us
  blocking collectives: 71.8 us -> 67.3 us
    ppermute x7 -> x2, waiting for transfers between devices: 131 us -> 58.6 us  [swapped(): return lax.ppermute(block, axis, [(0, 1), (1, 0)])]
    ppermute x3 -> x7, waiting for transfers between devices: 18.3 us -> 59.4 us  [the longest x4 42.4 us: voiced_swap(): return lax.ppermute(block, ('segment', 'mp'), [(2, 3), (3, 2)])]
    ppermute x7 -> x2, starting transfers between devices: 35 us -> 12.1 us  [swapped(): return lax.ppermute(block, axis, [(0, 1), (1, 0)])]
    unnamed x56 -> x124, local copies, waits for them, and re-layouts: 8.34 us -> 30.1 us
    ppermute x3 -> x7, starting transfers between devices: 8.6 us -> 27.1 us  [the longest x4 18.4 us: voiced_swap(): return lax.ppermute(block, ('segment', 'mp'), [(2, 3), (3, 2)])]
    all_to_all x3, waiting for transfers between devices: 3.55 us -> 20.3 us  [on_device(): lax.all_to_all(outgoing.reshape(experts, per_device * QUARTERS, width), '...]
    pallas_call x18, Pallas kernels: 41.1 us -> 26.5 us  [call(): pl.pallas_call(kernel, out_shape=outs, in_specs=specs, out_specs=out_spec...]
    dot_general x12, matrix products: 2.45 us -> 11.2 us  [dot(): return jnp.dot(a, b, preferred_element_type=F32)]
  transfers between devices with their start and end apart: 16 -> 15, of which waited for: 16 -> 14; matrix products, arithmetic and copies ran while one was open for 1% -> 4% of each run, Pallas kernels for 1% -> 1%
where the time goes in v3:
time: 435 us; the launch traced here: 433 us
  waiting for transfers between devices  176 us (40%)
  starting transfers between devices  110 us (25%)
  blocking collectives  67.3 us (15%)
  local copies, waits for them, and re-layouts  35.5 us (8%)
  Pallas kernels  26.5 us (6%)
  matrix products  11.2 us (3%)
    ppermute x2, waiting for transfers between devices, swapped(): return lax.ppermute(block, axis, [(0, 1), (1, 0)])  58.6 us
    all_to_all x3, starting transfers between devices, on_device(): lax.all_to_all(outgoing.reshape(experts, per_device * QUARTERS, width), '...  44.8 us
    ppermute x4, waiting for transfers between devices, voiced_swap(): return lax.ppermute(block, ('segment', 'mp'), [(2, 3), (3, 2)])  42.4 us
    all_to_all x3, waiting for transfers between devices, on_device(): lax.all_to_all(answer.reshape(experts, per_device * QUARTERS, width), 'ro...  38.1 us
    all_gather x3, blocking collectives, on_device(): total = lax.all_gather(chip, 'mp', axis=0).astype(F32)  37.7 us
    unnamed x124, local copies, waits for them, and re-layouts  30.1 us
    pallas_call x18, Pallas kernels, call(): pl.pallas_call(kernel, out_shape=outs, in_specs=specs, out_specs=out_spec...  26.5 us
    all_to_all x3, starting transfers between devices, on_device(): lax.all_to_all(answer.reshape(experts, per_device * QUARTERS, width), 'ro...  26.2 us
  transfers between devices with their start and end apart: 15, of which 14 were waited for; matrix products, arithmetic and copies ran while one was open for 4% of the time, Pallas kernels for 1%

profile of v3, /device:TPU:65, one launch (start us, length us, event | category | flops | bytes accessed | tf_op | source)
XLA Modules:
  0.0 432.9 jit_solution(8297055661037410659)
XLA Ops:
  6.8 7.4 %collective-permute-start = (bf16[336,2048]{1,0:T(8,128)(2,1)}, bf16[336,2048]{1,0:T(8,128)(2,1)}, u32[]{:S(2)}, u32[]{:S(2)}) collective-permute-start(bf16[336,2048]{1,0:T(8,128)(2,1)} %shard_map.140), channel_id=1, source_target_pairs={{0,1},{1,0},{2,3},{3,2},{4,5},{5,4},{6,7},{7,6},{8,9},{9,8},{10,11... | collective-permute-start | bytes 4128776 | tf_op jit(solution)/shard_map/ppermute | solution.py:28
  18.6 42.2 %collective-permute-done = bf16[336,2048]{1,0:T(8,128)(2,1)} collective-permute-done((bf16[336,2048]{1,0:T(8,128)(2,1)}, bf16[336,2048]{1,0:T(8,128)(2,1)}, u32[]{:S(2)}, u32[]{:S(2)}) %collective-permute-start) | collective-permute-done | bytes 1376288 | tf_op jit(solution)/shard_map/ppermute | solution.py:28
  63.4 29.5 %all-to-all-start = ((bf16[128,8,512]{2,1,0:T(8,128)(2,1)}), bf16[128,8,512]{2,1,0:T(8,128)(2,1)}, u32[]{:S(2)}, u32[]{:S(2)}) async-start(bf16[128,8,512]{2,1,0:T(8,128)(2,1)} %bitcast.10), calls=%async_computation | async-start | bytes 2097152 | tf_op jit(solution)/shard_map/all_to_all | solution.py:403
  102.3 20.1 %all-to-all-done = bf16[128,8,512]{2,1,0:T(8,128)(2,1)} async-done(((bf16[128,8,512]{2,1,0:T(8,128)(2,1)}), bf16[128,8,512]{2,1,0:T(8,128)(2,1)}, u32[]{:S(2)}, u32[]{:S(2)}) %all-to-all-start) | async-done | bytes 1048608 | tf_op jit(solution)/shard_map/all_to_all | solution.py:403
  129.0 7.5 %all-to-all-start.1 = ((bf16[128,8,512]{2,1,0:T(8,128)(2,1)}), bf16[128,8,512]{2,1,0:T(8,128)(2,1)}, u32[]{:S(2)}, u32[]{:S(2)}) async-start(bf16[128,8,512]{2,1,0:T(8,128)(2,1)} %bitcast.59), calls=%async_computation.1 | async-start | bytes 2097152 | tf_op jit(solution)/shard_map/all_to_all | solution.py:439
  138.0 4.7 %collective-permute-start.1 = (bf16[512,128]{1,0:T(8,128)(2,1)}, bf16[512,128]{1,0:T(8,128)(2,1)}, u32[]{:S(2)}, u32[]{:S(2)}) collective-permute-start(bf16[512,128]{1,0:T(8,128)(2,1)} %constant_dynamic-slice_fusion.2), channel_id=1, source_target_pairs={{0,1},{1,0},{2,3},{3,2},{4,5},{5,4},{6,7},{7,6},{8,9},{9,8},{10,11... | collective-permute-start | bytes 393224 | tf_op jit(solution)/shard_map/ppermute | solution.py:28
  142.7 16.4 %collective-permute-done.1 = bf16[512,128]{1,0:T(8,128)(2,1)} collective-permute-done((bf16[512,128]{1,0:T(8,128)(2,1)}, bf16[512,128]{1,0:T(8,128)(2,1)}, u32[]{:S(2)}, u32[]{:S(2)}) %collective-permute-start.1) | collective-permute-done | bytes 131104 | tf_op jit(solution)/shard_map/ppermute | solution.py:28
  159.2 5.0 %all_gather.51 = bf16[1024,128]{1,0:T(8,128)(2,1)S(1)} all-gather(bf16[512,128]{1,0:T(8,128)(2,1)} %collective-permute-done.1), channel_id=1, replica_groups=mesh['segment'=2,'rows'=128,'mp'=2] {'segment'}, dimensions={0}, use_global_device_ids=true | all-gather | bytes 393216 | tf_op jit(solution)/shard_map/all_gather | solution.py:245
  178.7 12.6 %all_gather.57 = bf16[2,128,512]{2,1,0:T(8,128)(2,1)S(1)} all-gather(bf16[1,128,512]{2,1,0:T(8,128)(2,1)S(1)} %fusion.29), channel_id=1, replica_groups=mesh['segment'=2,'rows'=128,'mp'=2] {'mp'}, dimensions={0}, use_global_device_ids=true | all-gather | bytes 393216 | tf_op jit(solution)/shard_map/all_gather | solution.py:460
  196.8 7.7 %all-to-all-start.2 = ((bf16[128,8,512]{2,1,0:T(8,128)(2,1)}), bf16[128,8,512]{2,1,0:T(8,128)(2,1)}, u32[]{:S(2)}, u32[]{:S(2)}) async-start(bf16[128,8,512]{2,1,0:T(8,128)(2,1)} %bitcast.63), calls=%async_computation.2 | async-start | bytes 2097152 | tf_op jit(solution)/shard_map/all_to_all | solution.py:403
  214.4 11.0 %collective-permute-done.2 = bf16[64,512]{1,0:T(8,128)(2,1)S(1)} collective-permute-done((bf16[64,512]{1,0:T(8,128)(2,1)S(1)}, bf16[64,512]{1,0:T(8,128)(2,1)S(1)}, u32[]{:S(2)}, u32[]{:S(2)}) %collective-permute-start.2) | collective-permute-done | bytes 65568 | tf_op jit(solution)/shard_map/ppermute | solution.py:32
  229.7 5.5 %collective-permute-done.3 = bf16[16,1024]{1,0:T(8,128)(2,1)S(1)} collective-permute-done((bf16[16,1024]{1,0:T(8,128)(2,1)S(1)}, bf16[16,1024]{1,0:T(8,128)(2,1)S(1)}, u32[]{:S(2)}, u32[]{:S(2)}) %collective-permute-start.3) | collective-permute-done | bytes 32800 | tf_op jit(solution)/shard_map/ppermute | solution.py:38
  242.6 9.7 %all-to-all-start.3 = ((bf16[128,8,512]{2,1,0:T(8,128)(2,1)}), bf16[128,8,512]{2,1,0:T(8,128)(2,1)}, u32[]{:S(2)}, u32[]{:S(2)}) async-start(bf16[128,8,512]{2,1,0:T(8,128)(2,1)} %bitcast.60), calls=%async_computation.3 | async-start | bytes 2097152 | tf_op jit(solution)/shard_map/all_to_all | solution.py:439
  257.1 15.9 %collective-permute-done.4 = f32[23,512]{1,0:T(8,128)} collective-permute-done((f32[23,512]{1,0:T(8,128)S(1)}, f32[23,512]{1,0:T(8,128)}, u32[]{:S(2)}, u32[]{:S(2)}) %collective-permute-start.4) | collective-permute-done | bytes 47136 | tf_op jit(solution)/shard_map/ppermute | solution.py:32
  276.5 7.8 %all-to-all-done.3 = bf16[128,8,512]{2,1,0:T(8,128)(2,1)} async-done(((bf16[128,8,512]{2,1,0:T(8,128)(2,1)}), bf16[128,8,512]{2,1,0:T(8,128)(2,1)}, u32[]{:S(2)}, u32[]{:S(2)}) %all-to-all-start.3) | async-done | bytes 1048608 | tf_op jit(solution)/shard_map/all_to_all | solution.py:439
  289.7 12.7 %all_gather.61 = bf16[2,128,512]{2,1,0:T(8,128)(2,1)S(1)} all-gather(bf16[1,128,512]{2,1,0:T(8,128)(2,1)S(1)} %fusion.25), channel_id=1, replica_groups=mesh['segment'=2,'rows'=128,'mp'=2] {'mp'}, dimensions={0}, use_global_device_ids=true | all-gather | bytes 393216 | tf_op jit(solution)/shard_map/all_gather | solution.py:460
  307.6 7.6 %all-to-all-start.4 = ((bf16[128,8,512]{2,1,0:T(8,128)(2,1)}), bf16[128,8,512]{2,1,0:T(8,128)(2,1)}, u32[]{:S(2)}, u32[]{:S(2)}) async-start(bf16[128,8,512]{2,1,0:T(8,128)(2,1)} %bitcast.62), calls=%async_computation.4 | async-start | bytes 2097152 | tf_op jit(solution)/shard_map/all_to_all | solution.py:403
  320.5 4.7 %collective-permute-start.5 = (bf16[64,512]{1,0:T(8,128)(2,1)S(1)}, bf16[64,512]{1,0:T(8,128)(2,1)S(1)}, u32[]{:S(2)}, u32[]{:S(2)}) collective-permute-start(bf16[64,512]{1,0:T(8,128)(2,1)S(1)} %fusion.1), channel_id=1, source_target_pairs={{256,257},{257,256},{258,259},{259,258},{260,261},{261,260},{262,2... | collective-permute-start | bytes 196616 | tf_op jit(solution)/shard_map/ppermute | solution.py:32
  325.1 11.2 %collective-permute-done.5 = bf16[64,512]{1,0:T(8,128)(2,1)S(1)} collective-permute-done((bf16[64,512]{1,0:T(8,128)(2,1)S(1)}, bf16[64,512]{1,0:T(8,128)(2,1)S(1)}, u32[]{:S(2)}, u32[]{:S(2)}) %collective-permute-start.5) | collective-permute-done | bytes 65568 | tf_op jit(solution)/shard_map/ppermute | solution.py:32
  340.9 5.3 %collective-permute-done.6 = bf16[16,1024]{1,0:T(8,128)(2,1)S(1)} collective-permute-done((bf16[16,1024]{1,0:T(8,128)(2,1)S(1)}, bf16[16,1024]{1,0:T(8,128)(2,1)S(1)}, u32[]{:S(2)}, u32[]{:S(2)}) %collective-permute-start.6) | collective-permute-done | bytes 32800 | tf_op jit(solution)/shard_map/ppermute | solution.py:38
  353.0 9.0 %all-to-all-start.5 = ((bf16[128,8,512]{2,1,0:T(8,128)(2,1)}), bf16[128,8,512]{2,1,0:T(8,128)(2,1)S(1)}, u32[]{:S(2)}, u32[]{:S(2)}) async-start(bf16[128,8,512]{2,1,0:T(8,128)(2,1)} %bitcast.61), calls=%async_computation.5 | async-start | bytes 2097152 | tf_op jit(solution)/shard_map/all_to_all | solution.py:439
  363.8 29.1 %all-to-all-done.5 = bf16[128,8,512]{2,1,0:T(8,128)(2,1)S(1)} async-done(((bf16[128,8,512]{2,1,0:T(8,128)(2,1)}), bf16[128,8,512]{2,1,0:T(8,128)(2,1)S(1)}, u32[]{:S(2)}, u32[]{:S(2)}) %all-to-all-start.5) | async-done | bytes 1048608 | tf_op jit(solution)/shard_map/all_to_all | solution.py:439
  396.1 12.4 %all_gather.65 = bf16[2,128,512]{2,1,0:T(8,128)(2,1)S(1)} all-gather(bf16[1,128,512]{2,1,0:T(8,128)(2,1)S(1)} %fusion.21), channel_id=1, replica_groups=mesh['segment'=2,'rows'=128,'mp'=2] {'mp'}, dimensions={0}, use_global_device_ids=true | all-gather | bytes 393216 | tf_op jit(solution)/shard_map/all_gather | solution.py:460
  424.3 6.3 %collective-permute-done.8 = bf16[16,1024]{1,0:T(8,128)(2,1)S(1)} collective-permute-done((bf16[16,1024]{1,0:T(8,128)(2,1)S(1)}, bf16[16,1024]{1,0:T(8,128)(2,1)S(1)}, u32[]{:S(2)}, u32[]{:S(2)}) %collective-permute-start.8) | collective-permute-done | bytes 32800 | tf_op jit(solution)/shard_map/ppermute | solution.py:38
  (206 shorter events, 130.0 us)
Async XLA Ops:
  6.8 54.0 %collective-permute-start = (bf16[336,2048]{1,0:T(8,128)(2,1)}, bf16[336,2048]{1,0:T(8,128)(2,1)}, u32[]{:S(2)}, u32[]{:S(2)}) collective-permute-start(bf16[336,2048]{1,0:T(8,128)(2,1)} %shard_map.140), channel_id=1, source_target_pairs={{0,1},{1,0},{2,3},{3,2},{4,5},{5,4},{6,7},{7,6},{8,9},{9,8},{10,11... | collective-permute-start | bytes 4128776 | tf_op jit(solution)/shard_map/ppermute | solution.py:28
  18.6 43.2 %copy-start.36 = (bf16[64,1024]{1,0:T(8,128)(2,1)}, bf16[64,1024]{1,0:T(8,128)(2,1)S(1)}, u32[]{:S(2)}) copy-start(bf16[64,1024]{1,0:T(8,128)(2,1)S(1)} %get-tuple-element.51.mask_ref) | copy-start | bytes 393220
  18.6 43.2 %copy-start.38 = (bf16[64,1024]{1,0:T(8,128)(2,1)}, bf16[64,1024]{1,0:T(8,128)(2,1)S(1)}, u32[]{:S(2)}) copy-start(bf16[64,1024]{1,0:T(8,128)(2,1)S(1)} %get-tuple-element.36.mask_ref) | copy-start | bytes 393220
  18.6 43.3 %copy-start.42 = (f32[64,128]{1,0:T(8,128)}, f32[64,128]{1,0:T(8,128)S(1)}, u32[]{:S(2)}) copy-start(f32[64,128]{1,0:T(8,128)S(1)} %get-tuple-element.50.hot_ref) | copy-start | bytes 98308
  18.6 43.3 %copy-start.44 = (f32[64,128]{1,0:T(8,128)}, f32[64,128]{1,0:T(8,128)S(1)}, u32[]{:S(2)}) copy-start(f32[64,128]{1,0:T(8,128)S(1)} %get-tuple-element.41.hot_ref) | copy-start | bytes 98308
  18.6 43.3 %copy-start.46 = (f32[64,128]{1,0:T(8,128)}, f32[64,128]{1,0:T(8,128)S(1)}, u32[]{:S(2)}) copy-start(f32[64,128]{1,0:T(8,128)S(1)} %get-tuple-element.34.hot_ref) | copy-start | bytes 98308
  61.8 32.4 %copy-start.40 = (bf16[256,512]{1,0:T(8,128)(2,1)}, bf16[256,512]{1,0:T(8,128)(2,1)S(1)}, u32[]{:S(2)}) copy-start(bf16[256,512]{1,0:T(8,128)(2,1)S(1)} %get-tuple-element.30.x_ref) | copy-start | bytes 786436
  63.4 30.8 %copy-start.23 = (bf16[256,512]{1,0:T(8,128)(2,1)}, bf16[256,512]{1,0:T(8,128)(2,1)S(1)}, u32[]{:S(2)}) copy-start(bf16[256,512]{1,0:T(8,128)(2,1)S(1)} %get-tuple-element.33.normed_ref) | copy-start | bytes 786436
  63.4 58.9 %all-to-all-start = ((bf16[128,8,512]{2,1,0:T(8,128)(2,1)}), bf16[128,8,512]{2,1,0:T(8,128)(2,1)}, u32[]{:S(2)}, u32[]{:S(2)}) async-start(bf16[128,8,512]{2,1,0:T(8,128)(2,1)} %bitcast.10), calls=%async_computation | async-start | bytes 2097152 | tf_op jit(solution)/shard_map/all_to_all | solution.py:403
  94.3 28.1 %copy-start.1 = (bf16[1,2048,192]{1,2,0:T(8,128)(2,1)S(1)}, bf16[1,2048,192]{1,2,0:T(8,128)(2,1)}, u32[]{:S(2)}) copy-start(bf16[1,2048,192]{1,2,0:T(8,128)(2,1)} %param.17) | copy-start | bytes 2359300
  129.0 42.2 %all-to-all-start.1 = ((bf16[128,8,512]{2,1,0:T(8,128)(2,1)}), bf16[128,8,512]{2,1,0:T(8,128)(2,1)}, u32[]{:S(2)}, u32[]{:S(2)}) async-start(bf16[128,8,512]{2,1,0:T(8,128)(2,1)} %bitcast.59), calls=%async_computation.1 | async-start | bytes 2097152 | tf_op jit(solution)/shard_map/all_to_all | solution.py:439
  138.0 21.2 %collective-permute-start.1 = (bf16[512,128]{1,0:T(8,128)(2,1)}, bf16[512,128]{1,0:T(8,128)(2,1)}, u32[]{:S(2)}, u32[]{:S(2)}) collective-permute-start(bf16[512,128]{1,0:T(8,128)(2,1)} %constant_dynamic-slice_fusion.2), channel_id=1, source_target_pairs={{0,1},{1,0},{2,3},{3,2},{4,5},{5,4},{6,7},{7,6},{8,9},{9,8},{10,11... | collective-permute-start | bytes 393224 | tf_op jit(solution)/shard_map/ppermute | solution.py:28
  196.8 39.1 %all-to-all-start.2 = ((bf16[128,8,512]{2,1,0:T(8,128)(2,1)}), bf16[128,8,512]{2,1,0:T(8,128)(2,1)}, u32[]{:S(2)}, u32[]{:S(2)}) async-start(bf16[128,8,512]{2,1,0:T(8,128)(2,1)} %bitcast.63), calls=%async_computation.2 | async-start | bytes 2097152 | tf_op jit(solution)/shard_map/all_to_all | solution.py:403
  209.9 15.5 %collective-permute-start.2 = (bf16[64,512]{1,0:T(8,128)(2,1)S(1)}, bf16[64,512]{1,0:T(8,128)(2,1)S(1)}, u32[]{:S(2)}, u32[]{:S(2)}) collective-permute-start(bf16[64,512]{1,0:T(8,128)(2,1)S(1)} %fusion), channel_id=1, source_target_pairs={{256,257},{257,256},{258,259},{259,258},{260,261},{261,260},{262,2... | collective-permute-start | bytes 196616 | tf_op jit(solution)/shard_map/ppermute | solution.py:32
  225.4 9.9 %collective-permute-start.3 = (bf16[16,1024]{1,0:T(8,128)(2,1)S(1)}, bf16[16,1024]{1,0:T(8,128)(2,1)S(1)}, u32[]{:S(2)}, u32[]{:S(2)}) collective-permute-start(bf16[16,1024]{1,0:T(8,128)(2,1)S(1)} %pad_maximum_fusion.4), channel_id=1, source_target_pairs={{256,258},{258,260},{260,262},{262,264},{264,266},{266,268},{268,2... | collective-permute-start | bytes 98312 | tf_op jit(solution)/shard_map/ppermute | solution.py:38
  242.6 41.7 %all-to-all-start.3 = ((bf16[128,8,512]{2,1,0:T(8,128)(2,1)}), bf16[128,8,512]{2,1,0:T(8,128)(2,1)}, u32[]{:S(2)}, u32[]{:S(2)}) async-start(bf16[128,8,512]{2,1,0:T(8,128)(2,1)} %bitcast.60), calls=%async_computation.3 | async-start | bytes 2097152 | tf_op jit(solution)/shard_map/all_to_all | solution.py:439
  252.6 20.5 %collective-permute-start.4 = (f32[23,512]{1,0:T(8,128)S(1)}, f32[23,512]{1,0:T(8,128)}, u32[]{:S(2)}, u32[]{:S(2)}) collective-permute-start(f32[23,512]{1,0:T(8,128)S(1)} %concatenate.48), channel_id=1, source_target_pairs={{256,257},{257,256},{258,259},{259,258},{260,261},{261,260},{262,2... | collective-permute-start | bytes 141320 | tf_op jit(solution)/shard_map/ppermute | solution.py:32
  307.6 38.8 %all-to-all-start.4 = ((bf16[128,8,512]{2,1,0:T(8,128)(2,1)}), bf16[128,8,512]{2,1,0:T(8,128)(2,1)}, u32[]{:S(2)}, u32[]{:S(2)}) async-start(bf16[128,8,512]{2,1,0:T(8,128)(2,1)} %bitcast.62), calls=%async_computation.4 | async-start | bytes 2097152 | tf_op jit(solution)/shard_map/all_to_all | solution.py:403
  320.5 15.9 %collective-permute-start.5 = (bf16[64,512]{1,0:T(8,128)(2,1)S(1)}, bf16[64,512]{1,0:T(8,128)(2,1)S(1)}, u32[]{:S(2)}, u32[]{:S(2)}) collective-permute-start(bf16[64,512]{1,0:T(8,128)(2,1)S(1)} %fusion.1), channel_id=1, source_target_pairs={{256,257},{257,256},{258,259},{259,258},{260,261},{261,260},{262,2... | collective-permute-start | bytes 196616 | tf_op jit(solution)/shard_map/ppermute | solution.py:32
  336.3 9.9 %collective-permute-start.6 = (bf16[16,1024]{1,0:T(8,128)(2,1)S(1)}, bf16[16,1024]{1,0:T(8,128)(2,1)S(1)}, u32[]{:S(2)}, u32[]{:S(2)}) collective-permute-start(bf16[16,1024]{1,0:T(8,128)(2,1)S(1)} %pad_maximum_fusion.3), channel_id=1, source_target_pairs={{256,258},{258,260},{260,262},{262,264},{264,266},{266,268},{268,2... | collective-permute-start | bytes 98312 | tf_op jit(solution)/shard_map/ppermute | solution.py:38
  353.0 40.0 %copy-start.28 = (bf16[128,1024]{1,0:T(8,128)(2,1)S(1)}, bf16[128,1024]{1,0:T(8,128)(2,1)}, u32[]{:S(2)}) copy-start(bf16[128,1024]{1,0:T(8,128)(2,1)} %copy-done.27) | copy-start | bytes 786436
  353.0 40.0 %all-to-all-start.5 = ((bf16[128,8,512]{2,1,0:T(8,128)(2,1)}), bf16[128,8,512]{2,1,0:T(8,128)(2,1)S(1)}, u32[]{:S(2)}, u32[]{:S(2)}) async-start(bf16[128,8,512]{2,1,0:T(8,128)(2,1)} %bitcast.61), calls=%async_computation.5 | async-start | bytes 2097152 | tf_op jit(solution)/shard_map/all_to_all | solution.py:439
  412.2 8.9 %collective-permute-start.7 = (bf16[64,512]{1,0:T(8,128)(2,1)S(1)}, bf16[64,512]{1,0:T(8,128)(2,1)S(1)}, u32[]{:S(2)}, u32[]{:S(2)}) collective-permute-start(bf16[64,512]{1,0:T(8,128)(2,1)S(1)} %fusion.2), channel_id=1, source_target_pairs={{256,257},{257,256},{258,259},{259,258},{260,261},{261,260},{262,2... | collective-permute-start | bytes 196616 | tf_op jit(solution)/shard_map/ppermute | solution.py:32
  421.1 9.5 %collective-permute-start.8 = (bf16[16,1024]{1,0:T(8,128)(2,1)S(1)}, bf16[16,1024]{1,0:T(8,128)(2,1)S(1)}, u32[]{:S(2)}, u32[]{:S(2)}) collective-permute-start(bf16[16,1024]{1,0:T(8,128)(2,1)S(1)} %pad_maximum_fusion.2), channel_id=1, source_target_pairs={{256,258},{258,260},{260,262},{262,264},{264,266},{266,268},{268,2... | collective-permute-start | bytes 98312 | tf_op jit(solution)/shard_map/ppermute | solution.py:38
  (52 other events, 355.5 us)

commit v4 on v3

--- a/solution.py
+++ b/solution.py
@@ -1,4 +1,5 @@
 import functools
+import math
 
 import jax
 import jax.numpy as jnp
@@ -14,6 +15,7 @@
 LANES = 128
 VMEM = pltpu.VMEM
 SMEM = pltpu.SMEM
+HBM = pltpu.HBM
 
 
 def dot(a, b):
@@ -41,11 +43,13 @@
 def call(kernel, outs, *args, scratch=(), flops=0, places=None, grant=10):
     single = not isinstance(outs, (list, tuple))
     listed = [outs] if single else list(outs)
-    moved = sum(a.size * a.dtype.itemsize for a in args)
-    moved += sum(o.size * o.dtype.itemsize for o in listed)
+    moved = sum(math.prod(a.shape) * a.dtype.itemsize for a in list(args) + listed)
     places = places or [VMEM] * len(args)
-    specs = [pl.BlockSpec(memory_space=p) for p in places]
-    out_specs = [pl.BlockSpec(memory_space=VMEM)] * len(listed)
+    specs = [p if isinstance(p, pl.BlockSpec) else pl.BlockSpec(memory_space=p) for p in places]
+    out_specs = [pl.BlockSpec(memory_space=getattr(o, "memory_space", VMEM)) for o in listed]
+    out_specs = [
+        s if s.memory_space in (VMEM, HBM) else pl.BlockSpec(memory_space=VMEM) for s in out_specs
+    ]
     return pl.pallas_call(
         kernel,
         out_shape=outs,
@@ -61,12 +65,23 @@
     return jax.ShapeDtypeStruct(shape, dtype)
 
 
-def pack_kernel(seg_ref, state_ref, gain_ref, gate_ref, up_ref, down_ref, out_ref):
+def pack_kernel(
+    seg_ref, state_ref, gain_ref, gate_ref, up_ref, down_ref, out_ref, head_out, head_ref, sems
+):
     rows, half = state_ref.shape
     top = rows // 2
     share = gate_ref.shape[0] // 2
-    out_ref[:top, :half] = state_ref[:top, :]
-    out_ref[:top, half:] = state_ref[top:, :]
+    copies = []
+    from_row = pl.multiple_of(seg_ref[0, 0] * share, share)
+    for i, ref in enumerate((gate_ref, up_ref, down_ref)):
+        place = top + BACK + i * share
+        copy = pltpu.make_async_copy(
+            ref.at[pl.ds(from_row, share), :], out_ref.at[pl.ds(place, share), :], sems.at[i]
+        )
+        copy.start()
+        copies.append(copy)
+    head_ref[:top, :half] = state_ref[:top, :]
+    head_ref[:top, half:] = state_ref[top:, :]
     gain = gain_ref[...]
     high = gain.astype(BF16)
     rest = gain - high.astype(F32)
@@ -76,12 +91,16 @@
     terms = jnp.zeros((BACK, half), F32)
     for i, term in enumerate((high, middle, low)):
         terms = jnp.where(row == i, term.astype(F32), terms)
-    out_ref[top : top + BACK, :half] = terms.astype(BF16)
-    out_ref[top : top + BACK, half:] = terms.astype(BF16)
-    place = top + BACK
-    for ref in (gate_ref, up_ref, down_ref):
-        out_ref[place : place + share, :] = ref[pl.ds(seg_ref[0, 0] * share, share), :]
-        place += share
+    head_ref[top:, :half] = terms.astype(BF16)
+    head_ref[top:, half:] = terms.astype(BF16)
+    copies.append(
+        pltpu.make_async_copy(head_ref, out_ref.at[pl.ds(0, top + BACK), :], sems.at[3])
+    )
+    copies.append(pltpu.make_async_copy(head_ref, head_out, sems.at[4]))
+    for copy in copies[3:]:
+        copy.start()
+    for copy in copies:
+        copy.wait()
 
 
 def unpack_kernel(mp_ref, mine_ref, other_ref, x_ref, gain_ref):
@@ -104,7 +123,7 @@
             gain_ref[2 * h + q : 2 * h + q + 1, :] = (terms[0:1] + terms[1:2]) + terms[2:3]
 
 
-def norm_kernel(depth, x_ref, gain_ref, pick_ref, out_ref, normed_ref):
+def norm_kernel(depth, x_ref, gain_ref, pick_ref, out_ref, normed_out, normed_ref, held_ref, sems):
     rows = x_ref.shape[0] // QUARTERS
     total = jnp.zeros((rows, 1), F32)
     for q in range(QUARTERS):
@@ -116,7 +135,19 @@
         normed_ref[q * rows : (q + 1) * rows, :] = (
             part * scale * gain_ref[q : q + 1, :]
         ).astype(BF16)
-    out_ref[...] = dot(pick_ref[...], normed_ref[...]).astype(BF16)
+    copies = [pltpu.make_async_copy(normed_ref, normed_out, sems.at[QUARTERS])]
+    copies[0].start()
+    normed = normed_ref[...]
+    size = pick_ref.shape[0] // QUARTERS
+    for i in range(QUARTERS):
+        held_ref[i] = dot(pick_ref[i * size : (i + 1) * size, :], normed).astype(BF16)
+        copy = pltpu.make_async_copy(
+            held_ref.at[i], out_ref.at[pl.ds(i * size, size), :], sems.at[i]
+        )
+        copy.start()
+        copies.append(copy)
+    for copy in copies:
+        copy.wait()
 
 
 def weight_kernel(normed_ref, router_ref, hot_ref, spread_ref, mask_ref, out_ref):
@@ -137,7 +168,17 @@
 
 
 def expert_kernel(
-    in_ref, gate_ref, gate2_ref, up_ref, up2_ref, down_ref, down2_ref, out_ref, wide_ref
+    in_ref,
+    gate_ref,
+    gate2_ref,
+    up_ref,
+    up2_ref,
+    down_ref,
+    down2_ref,
+    out_ref,
+    wide_ref,
+    answer_ref,
+    sems,
 ):
     count, width = in_ref.shape
     slots = count // QUARTERS
@@ -160,8 +201,19 @@
         answer = dot(first, down_ref[:, columns]) + dot(second, down2_ref[:, columns])
         for c in range(pieces):
             wide_ref[c, pl.ds(q, slots, stride=QUARTERS), :] = answer[:, c * LANES : (c + 1) * LANES]
-    for c in range(pieces):
-        out_ref[:, c * LANES : (c + 1) * LANES] = wide_ref[c].astype(BF16)
+    stores = []
+    size = count // QUARTERS
+    for i in range(QUARTERS):
+        span = slice(i * size, (i + 1) * size)
+        for c in range(pieces):
+            answer_ref[i, :, c * LANES : (c + 1) * LANES] = wide_ref[c, span, :].astype(BF16)
+        store = pltpu.make_async_copy(
+            answer_ref.at[i], out_ref.at[pl.ds(i * size, size), :], sems.at[i]
+        )
+        store.start()
+        stores.append(store)
+    for store in stores:
+        store.wait()
 
 
 def combine_kernel(weight_ref, back_ref, out_ref):
@@ -323,24 +375,28 @@
     gate, up, down = w_gate[0].T, w_up[0].T, w_down[0]
     part = gate.shape[0] // 2
     top = rows // 2
-    packed = call(
+    packed, head = call(
         pack_kernel,
-        shaped((top + BACK + 3 * part, depth), BF16),
+        (HBM((top + BACK + 3 * part, depth), BF16), HBM((top + BACK, depth), BF16)),
         seg.astype(jnp.int32).reshape(1, 1),
         start_state,
         norm_gain[None],
         gate,
         up,
         down,
-        places=[SMEM] + [VMEM] * 5,
-        grant=14,
+        scratch=[
+            pltpu.VMEM((top + BACK, depth), BF16),
+            pltpu.SemaphoreType.DMA((5,)),
+        ],
+        places=[SMEM, VMEM, VMEM, HBM, HBM, HBM],
+        grant=60,
     )
     sent = swapped(packed, "mp")
     x, gain = call(
         unpack_kernel,
         (shaped((QUARTERS * rows, width), BF16), shaped((QUARTERS, width), F32)),
         mp.astype(jnp.int32).reshape(1, 1),
-        packed[: top + BACK],
+        head,
         sent[: top + BACK],
         places=[SMEM, VMEM, VMEM],
     )
@@ -394,10 +450,15 @@
         hot, mask, pick = hots[step], masks[step], picks[step]
         outgoing, normed = call(
             functools.partial(norm_kernel, depth),
-            (shaped((slots * QUARTERS, width), BF16), shaped((QUARTERS * rows, width), BF16)),
+            (HBM((slots * QUARTERS, width), BF16), HBM((QUARTERS * rows, width), BF16)),
             x,
             gain,
             pick,
+            scratch=[
+                pltpu.VMEM((QUARTERS * rows, width), BF16),
+                pltpu.VMEM((QUARTERS, slots, width), BF16),
+                pltpu.SemaphoreType.DMA((QUARTERS + 1,)),
+            ],
             flops=2 * slots * QUARTERS * QUARTERS * rows * width,
         )
         received = lax.all_to_all(
@@ -424,7 +485,7 @@
             received, frames, weights = lax.optimization_barrier((received, frames, weights))
         answer = call(
             expert_kernel,
-            shaped((slots * QUARTERS, width), BF16),
+            HBM((slots * QUARTERS, width), BF16),
             received.reshape(slots * QUARTERS, width),
             gate,
             gate2,
@@ -432,8 +493,12 @@
             up2,
             down,
             down2,
-            scratch=[pltpu.VMEM((width // LANES, slots * QUARTERS, LANES), F32)],
-            grant=16,
+            scratch=[
+                pltpu.VMEM((width // LANES, slots * QUARTERS, LANES), F32),
+                pltpu.VMEM((QUARTERS, slots, width), BF16),
+                pltpu.SemaphoreType.DMA((QUARTERS,)),
+            ],
+            grant=12,
             flops=12 * slots * depth * w_gate.shape[2],
         )
         back = lax.all_to_all(

time: 435 us -> 465 us (1.069)
  Pallas kernels: 26.5 us -> 67.3 us
  local copies, waits for them, and re-layouts: 35.5 us -> 24.2 us
    pallas_call x18, Pallas kernels: 26.5 us -> 67.3 us  [call(): pl.pallas_call(kernel, out_shape=outs, in_specs=specs, out_specs=out_spec...]
    unnamed x124 -> x100, local copies, waits for them, and re-layouts: 30.1 us -> 19.8 us
where the time goes in v4:
time: 465 us; the launch traced here: 463 us
  waiting for transfers between devices  177 us (38%)
  starting transfers between devices  110 us (24%)
  blocking collectives  67.4 us (14%)
  Pallas kernels  67.3 us (14%)
  local copies, waits for them, and re-layouts  24.2 us (5%)
  matrix products  11.2 us (2%)
    pallas_call x18, Pallas kernels, call(): pl.pallas_call(kernel, out_shape=outs, in_specs=specs, out_specs=out_spec...  67.3 us
    ppermute x2, waiting for transfers between devices, swapped(): return lax.ppermute(block, axis, [(0, 1), (1, 0)])  59.6 us
    all_to_all x3, starting transfers between devices, on_device(): lax.all_to_all(outgoing.reshape(experts, per_device * QUARTERS, width), '...  44.9 us
    ppermute x4, waiting for transfers between devices, voiced_swap(): return lax.ppermute(block, ('segment', 'mp'), [(2, 3), (3, 2)])  42.4 us
    all_to_all x3, waiting for transfers between devices, on_device(): lax.all_to_all(answer.reshape(experts, per_device * QUARTERS, width), 'ro...  37.9 us
    all_gather x3, blocking collectives, on_device(): total = lax.all_gather(chip, 'mp', axis=0).astype(F32)  37.8 us
    all_to_all x3, starting transfers between devices, on_device(): lax.all_to_all(answer.reshape(experts, per_device * QUARTERS, width), 'ro...  26.2 us
    all_to_all x3, waiting for transfers between devices, on_device(): lax.all_to_all(outgoing.reshape(experts, per_device * QUARTERS, width), '...  20.3 us
  transfers between devices with their start and end apart: 15, of which 14 were waited for; matrix products, arithmetic and copies ran while one was open for 4% of the time, Pallas kernels for 1%

profile of v4, /device:TPU:65, one launch (start us, length us, event | category | flops | bytes accessed | tf_op | source)
XLA Modules:
  0.0 463.4 jit_solution(16755137309621382917)
XLA Ops:
  0.6 37.8 %shard_map.140 = (bf16[336,2048]{1,0:T(8,128)(2,1)}, bf16[48,2048]{1,0:T(8,128)(2,1)}) custom-call(s32[1,1]{1,0:T(1,128)} %bitcast.1.seg_ref, bf16[64,1024]{1,0:T(8,128)(2,1)} %state_ref.1, f32[1,1024]{1,0:T(1,128)} %bitcast.70, bf16[192,2048]{1,0:T(8,128)(2,1)} %bitcast.47, bf16[192,2048]{1,0:T(8,128)(2,1)} %bitcast.51, bf16[192,2048]{1,0:T(8,128)(2,1)} %bitcast.55), custom_call_target="tpu_custom_call" | custom-call | bytes 4067332 | tf_op jit(solution)/shard_map/pallas_call | solution.py:53
  38.4 7.5 %collective-permute-start = (bf16[336,2048]{1,0:T(8,128)(2,1)}, bf16[336,2048]{1,0:T(8,128)(2,1)}, u32[]{:S(2)}, u32[]{:S(2)}) collective-permute-start(bf16[336,2048]{1,0:T(8,128)(2,1)} %get-tuple-element.33), channel_id=1, source_target_pairs={{0,1},{1,0},{2,3},{3,2},{4,5},{5,4},{6,7},{7,6},{8,9},{9,8},{10,11... | collective-permute-start | bytes 4128776 | tf_op jit(solution)/shard_map/ppermute | solution.py:30
  49.3 43.1 %collective-permute-done = bf16[336,2048]{1,0:T(8,128)(2,1)} collective-permute-done((bf16[336,2048]{1,0:T(8,128)(2,1)}, bf16[336,2048]{1,0:T(8,128)(2,1)}, u32[]{:S(2)}, u32[]{:S(2)}) %collective-permute-start) | collective-permute-done | bytes 1376288 | tf_op jit(solution)/shard_map/ppermute | solution.py:30
  95.8 29.5 %all-to-all-start = ((bf16[128,8,512]{2,1,0:T(8,128)(2,1)}), bf16[128,8,512]{2,1,0:T(8,128)(2,1)}, u32[]{:S(2)}, u32[]{:S(2)}) async-start(bf16[128,8,512]{2,1,0:T(8,128)(2,1)} %bitcast.68), calls=%async_computation | async-start | bytes 2097152 | tf_op jit(solution)/shard_map/all_to_all | solution.py:464
  134.7 20.0 %all-to-all-done = bf16[128,8,512]{2,1,0:T(8,128)(2,1)} async-done(((bf16[128,8,512]{2,1,0:T(8,128)(2,1)}), bf16[128,8,512]{2,1,0:T(8,128)(2,1)}, u32[]{:S(2)}, u32[]{:S(2)}) %all-to-all-start) | async-done | bytes 1048608 | tf_op jit(solution)/shard_map/all_to_all | solution.py:464
  161.2 7.5 %all-to-all-start.1 = ((bf16[128,8,512]{2,1,0:T(8,128)(2,1)}), bf16[128,8,512]{2,1,0:T(8,128)(2,1)}, u32[]{:S(2)}, u32[]{:S(2)}) async-start(bf16[128,8,512]{2,1,0:T(8,128)(2,1)} %bitcast.60), calls=%async_computation.1 | async-start | bytes 2097152 | tf_op jit(solution)/shard_map/all_to_all | solution.py:504
  170.3 4.7 %collective-permute-start.1 = (bf16[512,128]{1,0:T(8,128)(2,1)}, bf16[512,128]{1,0:T(8,128)(2,1)}, u32[]{:S(2)}, u32[]{:S(2)}) collective-permute-start(bf16[512,128]{1,0:T(8,128)(2,1)} %constant_dynamic-slice_fusion.2), channel_id=1, source_target_pairs={{0,1},{1,0},{2,3},{3,2},{4,5},{5,4},{6,7},{7,6},{8,9},{9,8},{10,11... | collective-permute-start | bytes 393224 | tf_op jit(solution)/shard_map/ppermute | solution.py:30
  175.0 16.4 %collective-permute-done.1 = bf16[512,128]{1,0:T(8,128)(2,1)} collective-permute-done((bf16[512,128]{1,0:T(8,128)(2,1)}, bf16[512,128]{1,0:T(8,128)(2,1)}, u32[]{:S(2)}, u32[]{:S(2)}) %collective-permute-start.1) | collective-permute-done | bytes 131104 | tf_op jit(solution)/shard_map/ppermute | solution.py:30
  191.5 5.0 %all_gather.51 = bf16[1024,128]{1,0:T(8,128)(2,1)S(1)} all-gather(bf16[512,128]{1,0:T(8,128)(2,1)} %collective-permute-done.1), channel_id=1, replica_groups=mesh['segment'=2,'rows'=128,'mp'=2] {'segment'}, dimensions={0}, use_global_device_ids=true | all-gather | bytes 393216 | tf_op jit(solution)/shard_map/all_gather | solution.py:297
  211.0 12.6 %all_gather.57 = bf16[2,128,512]{2,1,0:T(8,128)(2,1)S(1)} all-gather(bf16[1,128,512]{2,1,0:T(8,128)(2,1)S(1)} %fusion.29), channel_id=1, replica_groups=mesh['segment'=2,'rows'=128,'mp'=2] {'mp'}, dimensions={0}, use_global_device_ids=true | all-gather | bytes 393216 | tf_op jit(solution)/shard_map/all_gather | solution.py:525
  228.3 7.8 %all-to-all-start.2 = ((bf16[128,8,512]{2,1,0:T(8,128)(2,1)}), bf16[128,8,512]{2,1,0:T(8,128)(2,1)}, u32[]{:S(2)}, u32[]{:S(2)}) async-start(bf16[128,8,512]{2,1,0:T(8,128)(2,1)} %bitcast.67), calls=%async_computation.2 | async-start | bytes 2097152 | tf_op jit(solution)/shard_map/all_to_all | solution.py:464
  245.9 11.0 %collective-permute-done.2 = bf16[64,512]{1,0:T(8,128)(2,1)S(1)} collective-permute-done((bf16[64,512]{1,0:T(8,128)(2,1)S(1)}, bf16[64,512]{1,0:T(8,128)(2,1)S(1)}, u32[]{:S(2)}, u32[]{:S(2)}) %collective-permute-start.2) | collective-permute-done | bytes 65568 | tf_op jit(solution)/shard_map/ppermute | solution.py:34
  261.1 5.5 %collective-permute-done.3 = bf16[16,1024]{1,0:T(8,128)(2,1)S(1)} collective-permute-done((bf16[16,1024]{1,0:T(8,128)(2,1)S(1)}, bf16[16,1024]{1,0:T(8,128)(2,1)S(1)}, u32[]{:S(2)}, u32[]{:S(2)}) %collective-permute-start.3) | collective-permute-done | bytes 32800 | tf_op jit(solution)/shard_map/ppermute | solution.py:40
  273.9 9.8 %all-to-all-start.3 = ((bf16[128,8,512]{2,1,0:T(8,128)(2,1)}), bf16[128,8,512]{2,1,0:T(8,128)(2,1)}, u32[]{:S(2)}, u32[]{:S(2)}) async-start(bf16[128,8,512]{2,1,0:T(8,128)(2,1)} %bitcast.61), calls=%async_computation.3 | async-start | bytes 2097152 | tf_op jit(solution)/shard_map/all_to_all | solution.py:504
  288.5 15.9 %collective-permute-done.4 = f32[23,512]{1,0:T(8,128)} collective-permute-done((f32[23,512]{1,0:T(8,128)S(1)}, f32[23,512]{1,0:T(8,128)}, u32[]{:S(2)}, u32[]{:S(2)}) %collective-permute-start.4) | collective-permute-done | bytes 47136 | tf_op jit(solution)/shard_map/ppermute | solution.py:34
  307.9 7.7 %all-to-all-done.3 = bf16[128,8,512]{2,1,0:T(8,128)(2,1)} async-done(((bf16[128,8,512]{2,1,0:T(8,128)(2,1)}), bf16[128,8,512]{2,1,0:T(8,128)(2,1)}, u32[]{:S(2)}, u32[]{:S(2)}) %all-to-all-start.3) | async-done | bytes 1048608 | tf_op jit(solution)/shard_map/all_to_all | solution.py:504
  321.1 12.7 %all_gather.61 = bf16[2,128,512]{2,1,0:T(8,128)(2,1)S(1)} all-gather(bf16[1,128,512]{2,1,0:T(8,128)(2,1)S(1)} %fusion.25), channel_id=1, replica_groups=mesh['segment'=2,'rows'=128,'mp'=2] {'mp'}, dimensions={0}, use_global_device_ids=true | all-gather | bytes 393216 | tf_op jit(solution)/shard_map/all_gather | solution.py:525
  338.2 7.6 %all-to-all-start.4 = ((bf16[128,8,512]{2,1,0:T(8,128)(2,1)}), bf16[128,8,512]{2,1,0:T(8,128)(2,1)}, u32[]{:S(2)}, u32[]{:S(2)}) async-start(bf16[128,8,512]{2,1,0:T(8,128)(2,1)} %bitcast.66), calls=%async_computation.4 | async-start | bytes 2097152 | tf_op jit(solution)/shard_map/all_to_all | solution.py:464
  355.6 11.2 %collective-permute-done.5 = bf16[64,512]{1,0:T(8,128)(2,1)S(1)} collective-permute-done((bf16[64,512]{1,0:T(8,128)(2,1)S(1)}, bf16[64,512]{1,0:T(8,128)(2,1)S(1)}, u32[]{:S(2)}, u32[]{:S(2)}) %collective-permute-start.5) | collective-permute-done | bytes 65568 | tf_op jit(solution)/shard_map/ppermute | solution.py:34
  371.4 5.3 %collective-permute-done.6 = bf16[16,1024]{1,0:T(8,128)(2,1)S(1)} collective-permute-done((bf16[16,1024]{1,0:T(8,128)(2,1)S(1)}, bf16[16,1024]{1,0:T(8,128)(2,1)S(1)}, u32[]{:S(2)}, u32[]{:S(2)}) %collective-permute-start.6) | collective-permute-done | bytes 32800 | tf_op jit(solution)/shard_map/ppermute | solution.py:40
  383.5 9.0 %all-to-all-start.5 = ((bf16[128,8,512]{2,1,0:T(8,128)(2,1)}), bf16[128,8,512]{2,1,0:T(8,128)(2,1)S(1)}, u32[]{:S(2)}, u32[]{:S(2)}) async-start(bf16[128,8,512]{2,1,0:T(8,128)(2,1)} %bitcast.62), calls=%async_computation.5 | async-start | bytes 2097152 | tf_op jit(solution)/shard_map/all_to_all | solution.py:504
  394.3 29.1 %all-to-all-done.5 = bf16[128,8,512]{2,1,0:T(8,128)(2,1)S(1)} async-done(((bf16[128,8,512]{2,1,0:T(8,128)(2,1)}), bf16[128,8,512]{2,1,0:T(8,128)(2,1)S(1)}, u32[]{:S(2)}, u32[]{:S(2)}) %all-to-all-start.5) | async-done | bytes 1048608 | tf_op jit(solution)/shard_map/all_to_all | solution.py:504
  426.6 12.4 %all_gather.65 = bf16[2,128,512]{2,1,0:T(8,128)(2,1)S(1)} all-gather(bf16[1,128,512]{2,1,0:T(8,128)(2,1)S(1)} %fusion.21), channel_id=1, replica_groups=mesh['segment'=2,'rows'=128,'mp'=2] {'mp'}, dimensions={0}, use_global_device_ids=true | all-gather | bytes 393216 | tf_op jit(solution)/shard_map/all_gather | solution.py:525
  454.7 6.3 %collective-permute-done.8 = bf16[16,1024]{1,0:T(8,128)(2,1)S(1)} collective-permute-done((bf16[16,1024]{1,0:T(8,128)(2,1)S(1)}, bf16[16,1024]{1,0:T(8,128)(2,1)S(1)}, u32[]{:S(2)}, u32[]{:S(2)}) %collective-permute-start.8) | collective-permute-done | bytes 32800 | tf_op jit(solution)/shard_map/ppermute | solution.py:40
  (181 shorter events, 126.5 us)
Async XLA Ops:
  0.6 45.3 %copy-start.44 = (s32[3,64,8]{1,2,0:T(8,128)S(1)}, s32[3,64,8]{1,2,0:T(8,128)}, u32[]{:S(2)}) copy-start(s32[3,64,8]{1,2,0:T(8,128)} %param.14) | copy-start | bytes 18436
  38.4 54.0 %collective-permute-start = (bf16[336,2048]{1,0:T(8,128)(2,1)}, bf16[336,2048]{1,0:T(8,128)(2,1)}, u32[]{:S(2)}, u32[]{:S(2)}) collective-permute-start(bf16[336,2048]{1,0:T(8,128)(2,1)} %get-tuple-element.33), channel_id=1, source_target_pairs={{0,1},{1,0},{2,3},{3,2},{4,5},{5,4},{6,7},{7,6},{8,9},{9,8},{10,11... | collective-permute-start | bytes 4128776 | tf_op jit(solution)/shard_map/ppermute | solution.py:30
  49.3 77.4 %copy-start.25 = (bf16[64,1024]{1,0:T(8,128)(2,1)}, bf16[64,1024]{1,0:T(8,128)(2,1)S(1)}, u32[]{:S(2)}) copy-start(bf16[64,1024]{1,0:T(8,128)(2,1)S(1)} %get-tuple-element.55.mask_ref) | copy-start | bytes 393220
  49.3 77.4 %copy-start.27 = (bf16[64,1024]{1,0:T(8,128)(2,1)}, bf16[64,1024]{1,0:T(8,128)(2,1)S(1)}, u32[]{:S(2)}) copy-start(bf16[64,1024]{1,0:T(8,128)(2,1)S(1)} %get-tuple-element.40.mask_ref) | copy-start | bytes 393220
  49.3 77.4 %copy-start.31 = (f32[64,128]{1,0:T(8,128)}, f32[64,128]{1,0:T(8,128)S(1)}, u32[]{:S(2)}) copy-start(f32[64,128]{1,0:T(8,128)S(1)} %get-tuple-element.54.hot_ref) | copy-start | bytes 98308
  49.3 77.4 %copy-start.33 = (f32[64,128]{1,0:T(8,128)}, f32[64,128]{1,0:T(8,128)S(1)}, u32[]{:S(2)}) copy-start(f32[64,128]{1,0:T(8,128)S(1)} %get-tuple-element.45.hot_ref) | copy-start | bytes 98308
  49.3 77.4 %copy-start.35 = (f32[64,128]{1,0:T(8,128)}, f32[64,128]{1,0:T(8,128)S(1)}, u32[]{:S(2)}) copy-start(f32[64,128]{1,0:T(8,128)S(1)} %get-tuple-element.38.hot_ref) | copy-start | bytes 98308
  94.4 32.3 %copy-start.29 = (bf16[256,512]{1,0:T(8,128)(2,1)}, bf16[256,512]{1,0:T(8,128)(2,1)S(1)}, u32[]{:S(2)}) copy-start(bf16[256,512]{1,0:T(8,128)(2,1)S(1)} %get-tuple-element.34.x_ref) | copy-start | bytes 786436
  95.8 58.9 %all-to-all-start = ((bf16[128,8,512]{2,1,0:T(8,128)(2,1)}), bf16[128,8,512]{2,1,0:T(8,128)(2,1)}, u32[]{:S(2)}, u32[]{:S(2)}) async-start(bf16[128,8,512]{2,1,0:T(8,128)(2,1)} %bitcast.68), calls=%async_computation | async-start | bytes 2097152 | tf_op jit(solution)/shard_map/all_to_all | solution.py:464
  126.7 28.0 %copy-start = (bf16[1,2048,192]{1,2,0:T(8,128)(2,1)S(1)}, bf16[1,2048,192]{1,2,0:T(8,128)(2,1)}, u32[]{:S(2)}) copy-start(bf16[1,2048,192]{1,2,0:T(8,128)(2,1)} %param.17) | copy-start | bytes 2359300
  161.2 42.2 %all-to-all-start.1 = ((bf16[128,8,512]{2,1,0:T(8,128)(2,1)}), bf16[128,8,512]{2,1,0:T(8,128)(2,1)}, u32[]{:S(2)}, u32[]{:S(2)}) async-start(bf16[128,8,512]{2,1,0:T(8,128)(2,1)} %bitcast.60), calls=%async_computation.1 | async-start | bytes 2097152 | tf_op jit(solution)/shard_map/all_to_all | solution.py:504
  170.3 21.2 %collective-permute-start.1 = (bf16[512,128]{1,0:T(8,128)(2,1)}, bf16[512,128]{1,0:T(8,128)(2,1)}, u32[]{:S(2)}, u32[]{:S(2)}) collective-permute-start(bf16[512,128]{1,0:T(8,128)(2,1)} %constant_dynamic-slice_fusion.2), channel_id=1, source_target_pairs={{0,1},{1,0},{2,3},{3,2},{4,5},{5,4},{6,7},{7,6},{8,9},{9,8},{10,11... | collective-permute-start | bytes 393224 | tf_op jit(solution)/shard_map/ppermute | solution.py:30
  228.3 39.1 %all-to-all-start.2 = ((bf16[128,8,512]{2,1,0:T(8,128)(2,1)}), bf16[128,8,512]{2,1,0:T(8,128)(2,1)}, u32[]{:S(2)}, u32[]{:S(2)}) async-start(bf16[128,8,512]{2,1,0:T(8,128)(2,1)} %bitcast.67), calls=%async_computation.2 | async-start | bytes 2097152 | tf_op jit(solution)/shard_map/all_to_all | solution.py:464
  241.3 15.5 %collective-permute-start.2 = (bf16[64,512]{1,0:T(8,128)(2,1)S(1)}, bf16[64,512]{1,0:T(8,128)(2,1)S(1)}, u32[]{:S(2)}, u32[]{:S(2)}) collective-permute-start(bf16[64,512]{1,0:T(8,128)(2,1)S(1)} %fusion), channel_id=1, source_target_pairs={{256,257},{257,256},{258,259},{259,258},{260,261},{261,260},{262,2... | collective-permute-start | bytes 196616 | tf_op jit(solution)/shard_map/ppermute | solution.py:34
  256.8 9.9 %collective-permute-start.3 = (bf16[16,1024]{1,0:T(8,128)(2,1)S(1)}, bf16[16,1024]{1,0:T(8,128)(2,1)S(1)}, u32[]{:S(2)}, u32[]{:S(2)}) collective-permute-start(bf16[16,1024]{1,0:T(8,128)(2,1)S(1)} %pad_maximum_fusion.4), channel_id=1, source_target_pairs={{256,258},{258,260},{260,262},{262,264},{264,266},{266,268},{268,2... | collective-permute-start | bytes 98312 | tf_op jit(solution)/shard_map/ppermute | solution.py:40
  273.9 41.6 %all-to-all-start.3 = ((bf16[128,8,512]{2,1,0:T(8,128)(2,1)}), bf16[128,8,512]{2,1,0:T(8,128)(2,1)}, u32[]{:S(2)}, u32[]{:S(2)}) async-start(bf16[128,8,512]{2,1,0:T(8,128)(2,1)} %bitcast.61), calls=%async_computation.3 | async-start | bytes 2097152 | tf_op jit(solution)/shard_map/all_to_all | solution.py:504
  283.9 20.5 %collective-permute-start.4 = (f32[23,512]{1,0:T(8,128)S(1)}, f32[23,512]{1,0:T(8,128)}, u32[]{:S(2)}, u32[]{:S(2)}) collective-permute-start(f32[23,512]{1,0:T(8,128)S(1)} %concatenate.48), channel_id=1, source_target_pairs={{256,257},{257,256},{258,259},{259,258},{260,261},{261,260},{262,2... | collective-permute-start | bytes 141320 | tf_op jit(solution)/shard_map/ppermute | solution.py:34
  338.2 38.8 %all-to-all-start.4 = ((bf16[128,8,512]{2,1,0:T(8,128)(2,1)}), bf16[128,8,512]{2,1,0:T(8,128)(2,1)}, u32[]{:S(2)}, u32[]{:S(2)}) async-start(bf16[128,8,512]{2,1,0:T(8,128)(2,1)} %bitcast.66), calls=%async_computation.4 | async-start | bytes 2097152 | tf_op jit(solution)/shard_map/all_to_all | solution.py:464
  351.0 15.8 %collective-permute-start.5 = (bf16[64,512]{1,0:T(8,128)(2,1)S(1)}, bf16[64,512]{1,0:T(8,128)(2,1)S(1)}, u32[]{:S(2)}, u32[]{:S(2)}) collective-permute-start(bf16[64,512]{1,0:T(8,128)(2,1)S(1)} %fusion.1), channel_id=1, source_target_pairs={{256,257},{257,256},{258,259},{259,258},{260,261},{261,260},{262,2... | collective-permute-start | bytes 196616 | tf_op jit(solution)/shard_map/ppermute | solution.py:34
  366.8 9.9 %collective-permute-start.6 = (bf16[16,1024]{1,0:T(8,128)(2,1)S(1)}, bf16[16,1024]{1,0:T(8,128)(2,1)S(1)}, u32[]{:S(2)}, u32[]{:S(2)}) collective-permute-start(bf16[16,1024]{1,0:T(8,128)(2,1)S(1)} %pad_maximum_fusion.3), channel_id=1, source_target_pairs={{256,258},{258,260},{260,262},{262,264},{264,266},{266,268},{268,2... | collective-permute-start | bytes 98312 | tf_op jit(solution)/shard_map/ppermute | solution.py:40
  383.5 39.9 %copy-start.19 = (bf16[128,1024]{1,0:T(8,128)(2,1)S(1)}, bf16[128,1024]{1,0:T(8,128)(2,1)}, u32[]{:S(2)}) copy-start(bf16[128,1024]{1,0:T(8,128)(2,1)} %copy-done.18) | copy-start | bytes 786436
  383.5 39.9 %all-to-all-start.5 = ((bf16[128,8,512]{2,1,0:T(8,128)(2,1)}), bf16[128,8,512]{2,1,0:T(8,128)(2,1)S(1)}, u32[]{:S(2)}, u32[]{:S(2)}) async-start(bf16[128,8,512]{2,1,0:T(8,128)(2,1)} %bitcast.62), calls=%async_computation.5 | async-start | bytes 2097152 | tf_op jit(solution)/shard_map/all_to_all | solution.py:504
  442.6 8.9 %collective-permute-start.7 = (bf16[64,512]{1,0:T(8,128)(2,1)S(1)}, bf16[64,512]{1,0:T(8,128)(2,1)S(1)}, u32[]{:S(2)}, u32[]{:S(2)}) collective-permute-start(bf16[64,512]{1,0:T(8,128)(2,1)S(1)} %fusion.2), channel_id=1, source_target_pairs={{256,257},{257,256},{258,259},{259,258},{260,261},{261,260},{262,2... | collective-permute-start | bytes 196616 | tf_op jit(solution)/shard_map/ppermute | solution.py:34
  451.5 9.5 %collective-permute-start.8 = (bf16[16,1024]{1,0:T(8,128)(2,1)S(1)}, bf16[16,1024]{1,0:T(8,128)(2,1)S(1)}, u32[]{:S(2)}, u32[]{:S(2)}) collective-permute-start(bf16[16,1024]{1,0:T(8,128)(2,1)S(1)} %pad_maximum_fusion.2), channel_id=1, source_target_pairs={{256,258},{258,260},{260,262},{262,264},{264,266},{266,268},{268,2... | collective-permute-start | bytes 98312 | tf_op jit(solution)/shard_map/ppermute | solution.py:40
  (40 other events, 335.6 us)

commit v5 on v4

--- a/solution.py
+++ b/solution.py
@@ -34,10 +34,14 @@
     return lax.ppermute(block, ("segment", "mp"), [(2, 3), (3, 2)])
 
 
-def voiced_pass(block):
+def voiced_pass(block, across):
     count = lax.axis_size("rows")
-    route = [(count + i, count + i + 1) for i in range(count - 1)]
-    return lax.ppermute(block, ("segment", "rows"), route)
+    route = [
+        (2 * (count + i) + m, 2 * (count + i + 1) + (m ^ across))
+        for i in range(count - 1)
+        for m in range(2)
+    ]
+    return lax.ppermute(block, ("segment", "rows", "mp"), route)
 
 
 def call(kernel, outs, *args, scratch=(), flops=0, places=None, grant=10):
@@ -66,20 +70,29 @@
 
 
 def pack_kernel(
-    seg_ref, state_ref, gain_ref, gate_ref, up_ref, down_ref, out_ref, head_out, head_ref, sems
+    seg_ref,
+    state_ref,
+    gain_ref,
+    gate_ref,
+    up_ref,
+    down_ref,
+    out_ref,
+    head_out,
+    head_ref,
+    part_ref,
+    sems,
 ):
     rows, half = state_ref.shape
     top = rows // 2
     share = gate_ref.shape[0] // 2
-    copies = []
     from_row = pl.multiple_of(seg_ref[0, 0] * share, share)
+    loads = []
     for i, ref in enumerate((gate_ref, up_ref, down_ref)):
-        place = top + BACK + i * share
-        copy = pltpu.make_async_copy(
-            ref.at[pl.ds(from_row, share), :], out_ref.at[pl.ds(place, share), :], sems.at[i]
-        )
-        copy.start()
-        copies.append(copy)
+        load = pltpu.make_async_copy(
+            ref.at[pl.ds(from_row, share), :], part_ref.at[i], sems.at[i]
+        )
+        load.start()
+        loads.append(load)
     head_ref[:top, :half] = state_ref[:top, :]
     head_ref[:top, half:] = state_ref[top:, :]
     gain = gain_ref[...]
@@ -93,12 +106,20 @@
         terms = jnp.where(row == i, term.astype(F32), terms)
     head_ref[top:, :half] = terms.astype(BF16)
     head_ref[top:, half:] = terms.astype(BF16)
-    copies.append(
-        pltpu.make_async_copy(head_ref, out_ref.at[pl.ds(0, top + BACK), :], sems.at[3])
-    )
-    copies.append(pltpu.make_async_copy(head_ref, head_out, sems.at[4]))
-    for copy in copies[3:]:
+    copies = [
+        pltpu.make_async_copy(head_ref, out_ref.at[pl.ds(0, top + BACK), :], sems.at[3]),
+        pltpu.make_async_copy(head_ref, head_out, sems.at[4]),
+    ]
+    for copy in copies:
         copy.start()
+    for i, load in enumerate(loads):
+        load.wait()
+        place = top + BACK + i * share
+        copy = pltpu.make_async_copy(
+            part_ref.at[i], out_ref.at[pl.ds(place, share), :], sems.at[5 + i]
+        )
+        copy.start()
+        copies.append(copy)
     for copy in copies:
         copy.wait()
 
@@ -386,7 +407,8 @@
         down,
         scratch=[
             pltpu.VMEM((top + BACK, depth), BF16),
-            pltpu.SemaphoreType.DMA((5,)),
+            pltpu.VMEM((3, part, depth), BF16),
+            pltpu.SemaphoreType.DMA((8,)),
         ],
         places=[SMEM, VMEM, VMEM, HBM, HBM, HBM],
         grant=60,
@@ -531,8 +553,10 @@
             dot(x[q * rows : (q + 1) * rows], w_in[q * width : (q + 1) * width])
             for q in range(QUARTERS)
         ).astype(BF16)
-        frames = jnp.concatenate([own, voiced_swap(own)], axis=1)
-        frames = jnp.concatenate([voiced_pass(frames[-BACK:]), frames], axis=0)
+        last = own[-BACK:]
+        near = jnp.concatenate([voiced_pass(last, 0), own], axis=0)
+        far = jnp.concatenate([voiced_pass(last, 1), voiced_swap(own)], axis=0)
+        frames = jnp.concatenate([near, far], axis=1)
     voiced.append(voice(frames))
     audio = jnp.stack([v.reshape(2 * rows) for v in voiced], axis=0)
     audio = jnp.where(seg == 0, jnp.zeros_like(audio), audio)[None]

time: 465 us -> 429 us (0.923)
  Pallas kernels: 67.3 us -> 32.7 us
  waiting for transfers between devices: 177 us -> 160 us
  starting transfers between devices: 110 us -> 122 us
    pallas_call x18, Pallas kernels: 67.3 us -> 32.7 us  [call(): pl.pallas_call(kernel, out_shape=outs, in_specs=specs, out_specs=out_spec...]
    ppermute x4, waiting for transfers between devices: 42.4 us -> 14.6 us  [voiced_swap(): return lax.ppermute(block, ('segment', 'mp'), [(2, 3), (3, 2)])]
    ppermute x3 -> x6, starting transfers between devices: 8.75 us -> 24 us  [voiced_pass(): return lax.ppermute(block, ('segment', 'rows', 'mp'), route)]
    all_to_all x3, waiting for transfers between devices: 20.3 us -> 34.9 us  [on_device(): lax.all_to_all(outgoing.reshape(experts, per_device * QUARTERS, width), '...]
    ppermute x3 -> x6, waiting for transfers between devices: 17.1 us -> 14.1 us  [voiced_pass(): return lax.ppermute(block, ('segment', 'rows', 'mp'), route)]
  transfers between devices with their start and end apart: 15 -> 18, of which waited for: 14 -> 13; matrix products, arithmetic and copies ran while one was open for 4% -> 4% of each run, Pallas kernels for 1% -> 2%
where the time goes in v5:
time: 429 us; the launch traced here: 427 us
  waiting for transfers between devices  160 us (37%)
  starting transfers between devices  122 us (28%)
  blocking collectives  71.3 us (17%)
  Pallas kernels  32.7 us (8%)
  local copies, waits for them, and re-layouts  24.2 us (6%)
  matrix products  11.2 us (3%)
    ppermute x2, waiting for transfers between devices, swapped(): return lax.ppermute(block, axis, [(0, 1), (1, 0)])  59.6 us
    all_to_all x3, starting transfers between devices, on_device(): lax.all_to_all(outgoing.reshape(experts, per_device * QUARTERS, width), '...  44.6 us
    all_gather x3, blocking collectives, on_device(): total = lax.all_gather(chip, 'mp', axis=0).astype(F32)  38.2 us
    all_to_all x3, waiting for transfers between devices, on_device(): lax.all_to_all(answer.reshape(experts, per_device * QUARTERS, width), 'ro...  36.6 us
    all_to_all x3, waiting for transfers between devices, on_device(): lax.all_to_all(outgoing.reshape(experts, per_device * QUARTERS, width), '...  34.9 us
    pallas_call x18, Pallas kernels, call(): pl.pallas_call(kernel, out_shape=outs, in_specs=specs, out_specs=out_spec...  32.7 us
    ppermute x6, starting transfers between devices, voiced_pass(): return lax.ppermute(block, ('segment', 'rows', 'mp'), route)  24 us
    all_to_all x3, starting transfers between devices, on_device(): lax.all_to_all(answer.reshape(experts, per_device * QUARTERS, width), 'ro...  23 us
  transfers between devices with their start and end apart: 18, of which 13 were waited for; matrix products, arithmetic and copies ran while one was open for 4% of the time, Pallas kernels for 2%

profile of v5, /device:TPU:65, one launch (start us, length us, event | category | flops | bytes accessed | tf_op | source)
XLA Modules:
  0.0 427.0 jit_solution(18171032847335862901)
XLA Ops:
  3.8 7.5 %collective-permute-start = (bf16[336,2048]{1,0:T(8,128)(2,1)}, bf16[336,2048]{1,0:T(8,128)(2,1)}, u32[]{:S(2)}, u32[]{:S(2)}) collective-permute-start(bf16[336,2048]{1,0:T(8,128)(2,1)} %get-tuple-element.33), channel_id=1, source_target_pairs={{0,1},{1,0},{2,3},{3,2},{4,5},{5,4},{6,7},{7,6},{8,9},{9,8},{10,11... | collective-permute-start | bytes 4128776 | tf_op jit(solution)/shard_map/ppermute | solution.py:30
  14.7 43.1 %collective-permute-done = bf16[336,2048]{1,0:T(8,128)(2,1)} collective-permute-done((bf16[336,2048]{1,0:T(8,128)(2,1)}, bf16[336,2048]{1,0:T(8,128)(2,1)}, u32[]{:S(2)}, u32[]{:S(2)}) %collective-permute-start) | collective-permute-done | bytes 1376288 | tf_op jit(solution)/shard_map/ppermute | solution.py:30
  61.2 29.5 %all-to-all-start = ((bf16[128,8,512]{2,1,0:T(8,128)(2,1)}), bf16[128,8,512]{2,1,0:T(8,128)(2,1)}, u32[]{:S(2)}, u32[]{:S(2)}) async-start(bf16[128,8,512]{2,1,0:T(8,128)(2,1)} %bitcast.68), calls=%async_computation | async-start | bytes 2097152 | tf_op jit(solution)/shard_map/all_to_all | solution.py:486
  100.1 20.0 %all-to-all-done = bf16[128,8,512]{2,1,0:T(8,128)(2,1)} async-done(((bf16[128,8,512]{2,1,0:T(8,128)(2,1)}), bf16[128,8,512]{2,1,0:T(8,128)(2,1)}, u32[]{:S(2)}, u32[]{:S(2)}) %all-to-all-start) | async-done | bytes 1048608 | tf_op jit(solution)/shard_map/all_to_all | solution.py:486
  126.6 7.5 %all-to-all-start.1 = ((bf16[128,8,512]{2,1,0:T(8,128)(2,1)}), bf16[128,8,512]{2,1,0:T(8,128)(2,1)}, u32[]{:S(2)}, u32[]{:S(2)}) async-start(bf16[128,8,512]{2,1,0:T(8,128)(2,1)} %bitcast.60), calls=%async_computation.1 | async-start | bytes 2097152 | tf_op jit(solution)/shard_map/all_to_all | solution.py:526
  135.7 4.7 %collective-permute-start.1 = (bf16[512,128]{1,0:T(8,128)(2,1)}, bf16[512,128]{1,0:T(8,128)(2,1)}, u32[]{:S(2)}, u32[]{:S(2)}) collective-permute-start(bf16[512,128]{1,0:T(8,128)(2,1)} %constant_dynamic-slice_fusion.2), channel_id=1, source_target_pairs={{0,1},{1,0},{2,3},{3,2},{4,5},{5,4},{6,7},{7,6},{8,9},{9,8},{10,11... | collective-permute-start | bytes 393224 | tf_op jit(solution)/shard_map/ppermute | solution.py:30
  140.4 16.4 %collective-permute-done.1 = bf16[512,128]{1,0:T(8,128)(2,1)} collective-permute-done((bf16[512,128]{1,0:T(8,128)(2,1)}, bf16[512,128]{1,0:T(8,128)(2,1)}, u32[]{:S(2)}, u32[]{:S(2)}) %collective-permute-start.1) | collective-permute-done | bytes 131104 | tf_op jit(solution)/shard_map/ppermute | solution.py:30
  156.8 5.0 %all_gather.51 = bf16[1024,128]{1,0:T(8,128)(2,1)S(1)} all-gather(bf16[512,128]{1,0:T(8,128)(2,1)} %collective-permute-done.1), channel_id=1, replica_groups=mesh['segment'=2,'rows'=128,'mp'=2] {'segment'}, dimensions={0}, use_global_device_ids=true | all-gather | bytes 393216 | tf_op jit(solution)/shard_map/all_gather | solution.py:318
  176.3 12.7 %all_gather.57 = bf16[2,128,512]{2,1,0:T(8,128)(2,1)S(1)} all-gather(bf16[1,128,512]{2,1,0:T(8,128)(2,1)S(1)} %fusion.29), channel_id=1, replica_groups=mesh['segment'=2,'rows'=128,'mp'=2] {'mp'}, dimensions={0}, use_global_device_ids=true | all-gather | bytes 393216 | tf_op jit(solution)/shard_map/all_gather | solution.py:547
  193.6 7.7 %all-to-all-start.2 = ((bf16[128,8,512]{2,1,0:T(8,128)(2,1)}), bf16[128,8,512]{2,1,0:T(8,128)(2,1)}, u32[]{:S(2)}, u32[]{:S(2)}) async-start(bf16[128,8,512]{2,1,0:T(8,128)(2,1)} %bitcast.67), calls=%async_computation.2 | async-start | bytes 2097152 | tf_op jit(solution)/shard_map/all_to_all | solution.py:486
  214.3 5.5 %collective-permute-start.3 = (bf16[16,512]{1,0:T(8,128)(2,1)S(1)}, bf16[16,512]{1,0:T(8,128)(2,1)S(1)}, u32[]{:S(2)}, u32[]{:S(2)}) collective-permute-start(bf16[16,512]{1,0:T(8,128)(2,1)S(1)} %slice.168), channel_id=1, source_target_pairs={{256,259},{257,258},{258,261},{259,260},{260,263},{261,262},{262,2... | collective-permute-start | bytes 49160 | tf_op jit(solution)/shard_map/ppermute | solution.py:44
  225.6 7.0 %all-to-all-done.2 = bf16[128,8,512]{2,1,0:T(8,128)(2,1)} async-done(((bf16[128,8,512]{2,1,0:T(8,128)(2,1)}), bf16[128,8,512]{2,1,0:T(8,128)(2,1)}, u32[]{:S(2)}, u32[]{:S(2)}) %all-to-all-start.2) | async-done | bytes 1048608 | tf_op jit(solution)/shard_map/all_to_all | solution.py:486
  239.2 8.4 %all-to-all-start.3 = ((bf16[128,8,512]{2,1,0:T(8,128)(2,1)}), bf16[128,8,512]{2,1,0:T(8,128)(2,1)}, u32[]{:S(2)}, u32[]{:S(2)}) async-start(bf16[128,8,512]{2,1,0:T(8,128)(2,1)} %bitcast.61), calls=%async_computation.3 | async-start | bytes 2097152 | tf_op jit(solution)/shard_map/all_to_all | solution.py:526
  252.5 14.6 %collective-permute-done.5 = f32[23,512]{1,0:T(8,128)} collective-permute-done((f32[23,512]{1,0:T(8,128)S(1)}, f32[23,512]{1,0:T(8,128)}, u32[]{:S(2)}, u32[]{:S(2)}) %collective-permute-start.5) | collective-permute-done | bytes 47136 | tf_op jit(solution)/shard_map/ppermute | solution.py:34
  270.5 7.5 %all-to-all-done.3 = bf16[128,8,512]{2,1,0:T(8,128)(2,1)} async-done(((bf16[128,8,512]{2,1,0:T(8,128)(2,1)}), bf16[128,8,512]{2,1,0:T(8,128)(2,1)}, u32[]{:S(2)}, u32[]{:S(2)}) %all-to-all-start.3) | async-done | bytes 1048608 | tf_op jit(solution)/shard_map/all_to_all | solution.py:526
  285.3 12.8 %all_gather.61 = bf16[2,128,512]{2,1,0:T(8,128)(2,1)S(1)} all-gather(bf16[1,128,512]{2,1,0:T(8,128)(2,1)S(1)} %fusion.25), channel_id=1, replica_groups=mesh['segment'=2,'rows'=128,'mp'=2] {'mp'}, dimensions={0}, use_global_device_ids=true | all-gather | bytes 393216 | tf_op jit(solution)/shard_map/all_gather | solution.py:547
  302.6 7.4 %all-to-all-start.4 = ((bf16[128,8,512]{2,1,0:T(8,128)(2,1)}), bf16[128,8,512]{2,1,0:T(8,128)(2,1)}, u32[]{:S(2)}, u32[]{:S(2)}) async-start(bf16[128,8,512]{2,1,0:T(8,128)(2,1)} %bitcast.66), calls=%async_computation.4 | async-start | bytes 2097152 | tf_op jit(solution)/shard_map/all_to_all | solution.py:486
  323.0 5.7 %collective-permute-start.7 = (bf16[16,512]{1,0:T(8,128)(2,1)S(1)}, bf16[16,512]{1,0:T(8,128)(2,1)S(1)}, u32[]{:S(2)}, u32[]{:S(2)}) collective-permute-start(bf16[16,512]{1,0:T(8,128)(2,1)S(1)} %slice.177), channel_id=1, source_target_pairs={{256,259},{257,258},{258,261},{259,260},{260,263},{261,262},{262,2... | collective-permute-start | bytes 49160 | tf_op jit(solution)/shard_map/ppermute | solution.py:44
  333.8 7.8 %all-to-all-done.4 = bf16[128,8,512]{2,1,0:T(8,128)(2,1)} async-done(((bf16[128,8,512]{2,1,0:T(8,128)(2,1)}), bf16[128,8,512]{2,1,0:T(8,128)(2,1)}, u32[]{:S(2)}, u32[]{:S(2)}) %all-to-all-start.4) | async-done | bytes 1048608 | tf_op jit(solution)/shard_map/all_to_all | solution.py:486
  348.1 7.2 %all-to-all-start.5 = ((bf16[128,8,512]{2,1,0:T(8,128)(2,1)}), bf16[128,8,512]{2,1,0:T(8,128)(2,1)S(1)}, u32[]{:S(2)}, u32[]{:S(2)}) async-start(bf16[128,8,512]{2,1,0:T(8,128)(2,1)} %bitcast.62), calls=%async_computation.5 | async-start | bytes 2097152 | tf_op jit(solution)/shard_map/all_to_all | solution.py:526
  357.1 27.9 %all-to-all-done.5 = bf16[128,8,512]{2,1,0:T(8,128)(2,1)S(1)} async-done(((bf16[128,8,512]{2,1,0:T(8,128)(2,1)}), bf16[128,8,512]{2,1,0:T(8,128)(2,1)S(1)}, u32[]{:S(2)}, u32[]{:S(2)}) %all-to-all-start.5) | async-done | bytes 1048608 | tf_op jit(solution)/shard_map/all_to_all | solution.py:526
  390.1 12.7 %all_gather.65 = bf16[2,128,512]{2,1,0:T(8,128)(2,1)S(1)} all-gather(bf16[1,128,512]{2,1,0:T(8,128)(2,1)S(1)} %fusion.21), channel_id=1, replica_groups=mesh['segment'=2,'rows'=128,'mp'=2] {'mp'}, dimensions={0}, use_global_device_ids=true | all-gather | bytes 393216 | tf_op jit(solution)/shard_map/all_gather | solution.py:547
  410.7 4.6 %collective-permute-start.10 = (bf16[16,512]{1,0:T(8,128)(2,1)S(1)}, bf16[16,512]{1,0:T(8,128)(2,1)S(1)}, u32[]{:S(2)}, u32[]{:S(2)}) collective-permute-start(bf16[16,512]{1,0:T(8,128)(2,1)S(1)} %slice.186), channel_id=1, source_target_pairs={{256,259},{257,258},{258,261},{259,260},{260,263},{261,262},{262,2... | collective-permute-start | bytes 49160 | tf_op jit(solution)/shard_map/ppermute | solution.py:44
  419.4 5.2 %collective-permute-done.9 = bf16[16,512]{1,0:T(8,128)(2,1)S(1)} collective-permute-done((bf16[16,512]{1,0:T(8,128)(2,1)S(1)}, bf16[16,512]{1,0:T(8,128)(2,1)S(1)}, u32[]{:S(2)}, u32[]{:S(2)}) %collective-permute-start.9) | collective-permute-done | bytes 16416 | tf_op jit(solution)/shard_map/ppermute | solution.py:44
  (187 shorter events, 136.9 us)
Async XLA Ops:
  3.8 54.0 %collective-permute-start = (bf16[336,2048]{1,0:T(8,128)(2,1)}, bf16[336,2048]{1,0:T(8,128)(2,1)}, u32[]{:S(2)}, u32[]{:S(2)}) collective-permute-start(bf16[336,2048]{1,0:T(8,128)(2,1)} %get-tuple-element.33), channel_id=1, source_target_pairs={{0,1},{1,0},{2,3},{3,2},{4,5},{5,4},{6,7},{7,6},{8,9},{9,8},{10,11... | collective-permute-start | bytes 4128776 | tf_op jit(solution)/shard_map/ppermute | solution.py:30
  14.7 77.4 %copy-start.25 = (bf16[64,1024]{1,0:T(8,128)(2,1)}, bf16[64,1024]{1,0:T(8,128)(2,1)S(1)}, u32[]{:S(2)}) copy-start(bf16[64,1024]{1,0:T(8,128)(2,1)S(1)} %get-tuple-element.55.mask_ref) | copy-start | bytes 393220
  14.7 77.4 %copy-start.27 = (bf16[64,1024]{1,0:T(8,128)(2,1)}, bf16[64,1024]{1,0:T(8,128)(2,1)S(1)}, u32[]{:S(2)}) copy-start(bf16[64,1024]{1,0:T(8,128)(2,1)S(1)} %get-tuple-element.40.mask_ref) | copy-start | bytes 393220
  14.7 77.4 %copy-start.31 = (f32[64,128]{1,0:T(8,128)}, f32[64,128]{1,0:T(8,128)S(1)}, u32[]{:S(2)}) copy-start(f32[64,128]{1,0:T(8,128)S(1)} %get-tuple-element.54.hot_ref) | copy-start | bytes 98308
  14.7 77.4 %copy-start.33 = (f32[64,128]{1,0:T(8,128)}, f32[64,128]{1,0:T(8,128)S(1)}, u32[]{:S(2)}) copy-start(f32[64,128]{1,0:T(8,128)S(1)} %get-tuple-element.45.hot_ref) | copy-start | bytes 98308
  14.7 77.4 %copy-start.35 = (f32[64,128]{1,0:T(8,128)}, f32[64,128]{1,0:T(8,128)S(1)}, u32[]{:S(2)}) copy-start(f32[64,128]{1,0:T(8,128)S(1)} %get-tuple-element.38.hot_ref) | copy-start | bytes 98308
  61.2 58.9 %all-to-all-start = ((bf16[128,8,512]{2,1,0:T(8,128)(2,1)}), bf16[128,8,512]{2,1,0:T(8,128)(2,1)}, u32[]{:S(2)}, u32[]{:S(2)}) async-start(bf16[128,8,512]{2,1,0:T(8,128)(2,1)} %bitcast.68), calls=%async_computation | async-start | bytes 2097152 | tf_op jit(solution)/shard_map/all_to_all | solution.py:486
  126.6 42.2 %all-to-all-start.1 = ((bf16[128,8,512]{2,1,0:T(8,128)(2,1)}), bf16[128,8,512]{2,1,0:T(8,128)(2,1)}, u32[]{:S(2)}, u32[]{:S(2)}) async-start(bf16[128,8,512]{2,1,0:T(8,128)(2,1)} %bitcast.60), calls=%async_computation.1 | async-start | bytes 2097152 | tf_op jit(solution)/shard_map/all_to_all | solution.py:526
  135.7 21.2 %collective-permute-start.1 = (bf16[512,128]{1,0:T(8,128)(2,1)}, bf16[512,128]{1,0:T(8,128)(2,1)}, u32[]{:S(2)}, u32[]{:S(2)}) collective-permute-start(bf16[512,128]{1,0:T(8,128)(2,1)} %constant_dynamic-slice_fusion.2), channel_id=1, source_target_pairs={{0,1},{1,0},{2,3},{3,2},{4,5},{5,4},{6,7},{7,6},{8,9},{9,8},{10,11... | collective-permute-start | bytes 393224 | tf_op jit(solution)/shard_map/ppermute | solution.py:30
  193.6 39.0 %all-to-all-start.2 = ((bf16[128,8,512]{2,1,0:T(8,128)(2,1)}), bf16[128,8,512]{2,1,0:T(8,128)(2,1)}, u32[]{:S(2)}, u32[]{:S(2)}) async-start(bf16[128,8,512]{2,1,0:T(8,128)(2,1)} %bitcast.67), calls=%async_computation.2 | async-start | bytes 2097152 | tf_op jit(solution)/shard_map/all_to_all | solution.py:486
  206.7 18.3 %collective-permute-start.4 = (bf16[64,512]{1,0:T(8,128)(2,1)S(1)}, bf16[64,512]{1,0:T(8,128)(2,1)S(1)}, u32[]{:S(2)}, u32[]{:S(2)}) collective-permute-start(bf16[64,512]{1,0:T(8,128)(2,1)S(1)} %fusion), channel_id=1, source_target_pairs={{256,257},{257,256},{258,259},{259,258},{260,261},{261,260},{262,2... | collective-permute-start | bytes 196616 | tf_op jit(solution)/shard_map/ppermute | solution.py:34
  211.2 13.7 %collective-permute-start.2 = (bf16[16,512]{1,0:T(8,128)(2,1)S(1)}, bf16[16,512]{1,0:T(8,128)(2,1)S(1)}, u32[]{:S(2)}, u32[]{:S(2)}) collective-permute-start(bf16[16,512]{1,0:T(8,128)(2,1)S(1)} %slice.168), channel_id=1, source_target_pairs={{256,258},{257,259},{258,260},{259,261},{260,262},{261,263},{262,2... | collective-permute-start | bytes 49160 | tf_op jit(solution)/shard_map/ppermute | solution.py:44
  214.3 10.6 %collective-permute-start.3 = (bf16[16,512]{1,0:T(8,128)(2,1)S(1)}, bf16[16,512]{1,0:T(8,128)(2,1)S(1)}, u32[]{:S(2)}, u32[]{:S(2)}) collective-permute-start(bf16[16,512]{1,0:T(8,128)(2,1)S(1)} %slice.168), channel_id=1, source_target_pairs={{256,259},{257,258},{258,261},{259,260},{260,263},{261,262},{262,2... | collective-permute-start | bytes 49160 | tf_op jit(solution)/shard_map/ppermute | solution.py:44
  239.2 38.8 %all-to-all-start.3 = ((bf16[128,8,512]{2,1,0:T(8,128)(2,1)}), bf16[128,8,512]{2,1,0:T(8,128)(2,1)}, u32[]{:S(2)}, u32[]{:S(2)}) async-start(bf16[128,8,512]{2,1,0:T(8,128)(2,1)} %bitcast.61), calls=%async_computation.3 | async-start | bytes 2097152 | tf_op jit(solution)/shard_map/all_to_all | solution.py:526
  247.8 19.3 %collective-permute-start.5 = (f32[23,512]{1,0:T(8,128)S(1)}, f32[23,512]{1,0:T(8,128)}, u32[]{:S(2)}, u32[]{:S(2)}) collective-permute-start(f32[23,512]{1,0:T(8,128)S(1)} %concatenate.58), channel_id=1, source_target_pairs={{256,257},{257,256},{258,259},{259,258},{260,261},{261,260},{262,2... | collective-permute-start | bytes 141320 | tf_op jit(solution)/shard_map/ppermute | solution.py:34
  302.6 39.0 %all-to-all-start.4 = ((bf16[128,8,512]{2,1,0:T(8,128)(2,1)}), bf16[128,8,512]{2,1,0:T(8,128)(2,1)}, u32[]{:S(2)}, u32[]{:S(2)}) async-start(bf16[128,8,512]{2,1,0:T(8,128)(2,1)} %bitcast.66), calls=%async_computation.4 | async-start | bytes 2097152 | tf_op jit(solution)/shard_map/all_to_all | solution.py:486
  315.2 18.5 %collective-permute-start.8 = (bf16[64,512]{1,0:T(8,128)(2,1)S(1)}, bf16[64,512]{1,0:T(8,128)(2,1)S(1)}, u32[]{:S(2)}, u32[]{:S(2)}) collective-permute-start(bf16[64,512]{1,0:T(8,128)(2,1)S(1)} %fusion.1), channel_id=1, source_target_pairs={{256,257},{257,256},{258,259},{259,258},{260,261},{261,260},{262,2... | collective-permute-start | bytes 196616 | tf_op jit(solution)/shard_map/ppermute | solution.py:34
  319.9 13.9 %collective-permute-start.6 = (bf16[16,512]{1,0:T(8,128)(2,1)S(1)}, bf16[16,512]{1,0:T(8,128)(2,1)S(1)}, u32[]{:S(2)}, u32[]{:S(2)}) collective-permute-start(bf16[16,512]{1,0:T(8,128)(2,1)S(1)} %slice.177), channel_id=1, source_target_pairs={{256,258},{257,259},{258,260},{259,261},{260,262},{261,263},{262,2... | collective-permute-start | bytes 49160 | tf_op jit(solution)/shard_map/ppermute | solution.py:44
  323.0 10.8 %collective-permute-start.7 = (bf16[16,512]{1,0:T(8,128)(2,1)S(1)}, bf16[16,512]{1,0:T(8,128)(2,1)S(1)}, u32[]{:S(2)}, u32[]{:S(2)}) collective-permute-start(bf16[16,512]{1,0:T(8,128)(2,1)S(1)} %slice.177), channel_id=1, source_target_pairs={{256,259},{257,258},{258,261},{259,260},{260,263},{261,262},{262,2... | collective-permute-start | bytes 49160 | tf_op jit(solution)/shard_map/ppermute | solution.py:44
  348.1 36.9 %copy-start.19 = (bf16[128,1024]{1,0:T(8,128)(2,1)S(1)}, bf16[128,1024]{1,0:T(8,128)(2,1)}, u32[]{:S(2)}) copy-start(bf16[128,1024]{1,0:T(8,128)(2,1)} %copy-done.18) | copy-start | bytes 786436
  348.1 36.9 %all-to-all-start.5 = ((bf16[128,8,512]{2,1,0:T(8,128)(2,1)}), bf16[128,8,512]{2,1,0:T(8,128)(2,1)S(1)}, u32[]{:S(2)}, u32[]{:S(2)}) async-start(bf16[128,8,512]{2,1,0:T(8,128)(2,1)} %bitcast.62), calls=%async_computation.5 | async-start | bytes 2097152 | tf_op jit(solution)/shard_map/all_to_all | solution.py:526
  406.1 18.5 %collective-permute-start.11 = (bf16[64,512]{1,0:T(8,128)(2,1)S(1)}, bf16[64,512]{1,0:T(8,128)(2,1)S(1)}, u32[]{:S(2)}, u32[]{:S(2)}) collective-permute-start(bf16[64,512]{1,0:T(8,128)(2,1)S(1)} %fusion.2), channel_id=1, source_target_pairs={{256,257},{257,256},{258,259},{259,258},{260,261},{261,260},{262,2... | collective-permute-start | bytes 196616 | tf_op jit(solution)/shard_map/ppermute | solution.py:34
  410.7 8.7 %collective-permute-start.10 = (bf16[16,512]{1,0:T(8,128)(2,1)S(1)}, bf16[16,512]{1,0:T(8,128)(2,1)S(1)}, u32[]{:S(2)}, u32[]{:S(2)}) collective-permute-start(bf16[16,512]{1,0:T(8,128)(2,1)S(1)} %slice.186), channel_id=1, source_target_pairs={{256,259},{257,258},{258,261},{259,260},{260,263},{261,262},{262,2... | collective-permute-start | bytes 49160 | tf_op jit(solution)/shard_map/ppermute | solution.py:44
  415.3 9.3 %collective-permute-start.9 = (bf16[16,512]{1,0:T(8,128)(2,1)S(1)}, bf16[16,512]{1,0:T(8,128)(2,1)S(1)}, u32[]{:S(2)}, u32[]{:S(2)}) collective-permute-start(bf16[16,512]{1,0:T(8,128)(2,1)S(1)} %slice.186), channel_id=1, source_target_pairs={{256,258},{257,259},{258,260},{259,261},{260,262},{261,263},{262,2... | collective-permute-start | bytes 49160 | tf_op jit(solution)/shard_map/ppermute | solution.py:44
  (43 other events, 365.2 us)

commit v6 on v5

--- a/solution.py
+++ b/solution.py
@@ -107,16 +107,14 @@
     head_ref[top:, :half] = terms.astype(BF16)
     head_ref[top:, half:] = terms.astype(BF16)
     copies = [
-        pltpu.make_async_copy(head_ref, out_ref.at[pl.ds(0, top + BACK), :], sems.at[3]),
-        pltpu.make_async_copy(head_ref, head_out, sems.at[4]),
+        pltpu.make_async_copy(head_ref, head_out, sems.at[3]),
     ]
     for copy in copies:
         copy.start()
     for i, load in enumerate(loads):
         load.wait()
-        place = top + BACK + i * share
         copy = pltpu.make_async_copy(
-            part_ref.at[i], out_ref.at[pl.ds(place, share), :], sems.at[5 + i]
+            part_ref.at[i], out_ref.at[pl.ds(i * share, share), :], sems.at[4 + i]
         )
         copy.start()
         copies.append(copy)
@@ -398,7 +396,7 @@
     top = rows // 2
     packed, head = call(
         pack_kernel,
-        (HBM((top + BACK + 3 * part, depth), BF16), HBM((top + BACK, depth), BF16)),
+        (HBM((3 * part, depth), BF16), HBM((top + BACK, depth), BF16)),
         seg.astype(jnp.int32).reshape(1, 1),
         start_state,
         norm_gain[None],
@@ -408,22 +406,23 @@
         scratch=[
             pltpu.VMEM((top + BACK, depth), BF16),
             pltpu.VMEM((3, part, depth), BF16),
-            pltpu.SemaphoreType.DMA((8,)),
+            pltpu.SemaphoreType.DMA((7,)),
         ],
         places=[SMEM, VMEM, VMEM, HBM, HBM, HBM],
         grant=60,
     )
+    head_sent = swapped(head, "mp")
     sent = swapped(packed, "mp")
     x, gain = call(
         unpack_kernel,
         (shaped((QUARTERS * rows, width), BF16), shaped((QUARTERS, width), F32)),
         mp.astype(jnp.int32).reshape(1, 1),
         head,
-        sent[: top + BACK],
+        head_sent,
         places=[SMEM, VMEM, VMEM],
     )
     gate_share, up_share, down_share = (
-        sent[top + BACK + i * part : top + BACK + (i + 1) * part] for i in range(3)
+        sent[i * part : (i + 1) * part] for i in range(3)
     )
     small = jnp.concatenate(
         [trans_taps, dw_kernels.reshape(layers * kernel, -1), ln_gain, ln_bias, w_out[None]], axis=0

time: 429 us -> 412 us (0.960)
  the two profiles are of different devices: /device:TPU:65 before, /device:TPU:31 now
where the time goes in v6:
time: 412 us; the launch traced here: 410 us
  waiting for transfers between devices  146 us (35%)
  starting transfers between devices  124 us (30%)
  blocking collectives  67.5 us (16%)
  Pallas kernels  32.6 us (8%)
  local copies, waits for them, and re-layouts  23.2 us (6%)
  matrix products  11.2 us (3%)
    ppermute x3, waiting for transfers between devices, swapped(): return lax.ppermute(block, axis, [(0, 1), (1, 0)])  45.3 us
    all_to_all x3, starting transfers between devices, on_device(): lax.all_to_all(outgoing.reshape(experts, per_device * QUARTERS, width), '...  41.7 us
    all_gather x3, blocking collectives, on_device(): total = lax.all_gather(chip, 'mp', axis=0).astype(F32)  38.3 us
    all_to_all x3, waiting for transfers between devices, on_device(): lax.all_to_all(outgoing.reshape(experts, per_device * QUARTERS, width), '...  34.8 us
    all_to_all x3, waiting for transfers between devices, on_device(): lax.all_to_all(answer.reshape(experts, per_device * QUARTERS, width), 'ro...  33.4 us
    all_to_all x3, starting transfers between devices, on_device(): lax.all_to_all(answer.reshape(experts, per_device * QUARTERS, width), 'ro...  32.7 us
    pallas_call x18, Pallas kernels, call(): pl.pallas_call(kernel, out_shape=outs, in_specs=specs, out_specs=out_spec...  32.6 us
    unnamed x100, local copies, waits for them, and re-layouts  19.7 us
  transfers between devices with their start and end apart: 19, of which 14 were waited for; matrix products, arithmetic and copies ran while one was open for 4% of the time, Pallas kernels for 2%

profile of v6, /device:TPU:31, one launch (start us, length us, event | category | flops | bytes accessed | tf_op | source)
XLA Modules:
  0.0 410.2 jit_solution(5212490402893402092)
XLA Ops:
  3.7 4.8 %collective-permute-start = (bf16[48,2048]{1,0:T(8,128)(2,1)}, bf16[48,2048]{1,0:T(8,128)(2,1)S(1)}, u32[]{:S(2)}, u32[]{:S(2)}) collective-permute-start(bf16[48,2048]{1,0:T(8,128)(2,1)} %get-tuple-element.32.mine_ref), channel_id=1, source_target_pairs={{0,1},{1,0},{2,3},{3,2},{4,5},{5,4},{6,7},{7,6},{8,9},{9,8},{10,11... | collective-permute-start | bytes 589832 | tf_op jit(solution)/shard_map/ppermute | solution.py:30
  20.5 20.4 %all-to-all-start = ((bf16[128,8,512]{2,1,0:T(8,128)(2,1)}), bf16[128,8,512]{2,1,0:T(8,128)(2,1)}, u32[]{:S(2)}, u32[]{:S(2)}) async-start(bf16[128,8,512]{2,1,0:T(8,128)(2,1)} %bitcast.68), calls=%async_computation | async-start | bytes 2097152 | tf_op jit(solution)/shard_map/all_to_all | solution.py:485
  40.9 26.1 %collective-permute-done.2 = bf16[288,2048]{1,0:T(8,128)(2,1)} collective-permute-done((bf16[288,2048]{1,0:T(8,128)(2,1)}, bf16[288,2048]{1,0:T(8,128)(2,1)}, u32[]{:S(2)}, u32[]{:S(2)}) %collective-permute-start.2) | collective-permute-done | bytes 1179680 | tf_op jit(solution)/shard_map/ppermute | solution.py:30
  68.4 4.8 %all_gather.52.gate2_ref = bf16[192,2048]{1,0:T(8,128)(2,1)S(1)} all-gather(bf16[96,2048]{1,0:T(8,128)(2,1)S(1)} %get-tuple-element.70), channel_id=1, replica_groups=mesh['segment'=2,'rows'=128,'mp'=2] {'segment'}, dimensions={0}, use_global_device_ids=true | all-gather | bytes 1179648 | tf_op jit(solution)/shard_map/all_gather | solution.py:316
  78.0 25.0 %all-to-all-done = bf16[128,8,512]{2,1,0:T(8,128)(2,1)} async-done(((bf16[128,8,512]{2,1,0:T(8,128)(2,1)}), bf16[128,8,512]{2,1,0:T(8,128)(2,1)}, u32[]{:S(2)}, u32[]{:S(2)}) %all-to-all-start) | async-done | bytes 1048608 | tf_op jit(solution)/shard_map/all_to_all | solution.py:485
  109.5 10.1 %all-to-all-start.1 = ((bf16[128,8,512]{2,1,0:T(8,128)(2,1)}), bf16[128,8,512]{2,1,0:T(8,128)(2,1)}, u32[]{:S(2)}, u32[]{:S(2)}) async-start(bf16[128,8,512]{2,1,0:T(8,128)(2,1)} %bitcast.60), calls=%async_computation.1 | async-start | bytes 2097152 | tf_op jit(solution)/shard_map/all_to_all | solution.py:525
  124.5 17.5 %collective-permute-done.1 = bf16[512,128]{1,0:T(8,128)(2,1)} collective-permute-done((bf16[512,128]{1,0:T(8,128)(2,1)}, bf16[512,128]{1,0:T(8,128)(2,1)}, u32[]{:S(2)}, u32[]{:S(2)}) %collective-permute-start.1) | collective-permute-done | bytes 131104 | tf_op jit(solution)/shard_map/ppermute | solution.py:30
  157.9 12.6 %all_gather.57 = bf16[2,128,512]{2,1,0:T(8,128)(2,1)S(1)} all-gather(bf16[1,128,512]{2,1,0:T(8,128)(2,1)S(1)} %fusion.29), channel_id=1, replica_groups=mesh['segment'=2,'rows'=128,'mp'=2] {'mp'}, dimensions={0}, use_global_device_ids=true | all-gather | bytes 393216 | tf_op jit(solution)/shard_map/all_gather | solution.py:546
  174.9 10.6 %all-to-all-start.2 = ((bf16[128,8,512]{2,1,0:T(8,128)(2,1)}), bf16[128,8,512]{2,1,0:T(8,128)(2,1)}, u32[]{:S(2)}, u32[]{:S(2)}) async-start(bf16[128,8,512]{2,1,0:T(8,128)(2,1)} %bitcast.67), calls=%async_computation.2 | async-start | bytes 2097152 | tf_op jit(solution)/shard_map/all_to_all | solution.py:485
  190.8 5.9 %collective-permute-start.5 = (bf16[64,512]{1,0:T(8,128)(2,1)S(1)}, bf16[64,512]{1,0:T(8,128)(2,1)S(1)}, u32[]{:S(2)}, u32[]{:S(2)}) collective-permute-start(bf16[64,512]{1,0:T(8,128)(2,1)S(1)} %fusion), channel_id=1, source_target_pairs={{256,257},{257,256},{258,259},{259,258},{260,261},{261,260},{262,2... | collective-permute-start | bytes 196616 | tf_op jit(solution)/shard_map/ppermute | solution.py:34
  203.1 6.3 %collective-permute-done.4 = bf16[16,512]{1,0:T(8,128)(2,1)S(1)} collective-permute-done((bf16[16,512]{1,0:T(8,128)(2,1)S(1)}, bf16[16,512]{1,0:T(8,128)(2,1)S(1)}, u32[]{:S(2)}, u32[]{:S(2)}) %collective-permute-start.4) | collective-permute-done | bytes 16416 | tf_op jit(solution)/shard_map/ppermute | solution.py:44
  220.5 12.5 %all-to-all-start.3 = ((bf16[128,8,512]{2,1,0:T(8,128)(2,1)}), bf16[128,8,512]{2,1,0:T(8,128)(2,1)}, u32[]{:S(2)}, u32[]{:S(2)}) async-start(bf16[128,8,512]{2,1,0:T(8,128)(2,1)} %bitcast.61), calls=%async_computation.3 | async-start | bytes 2097152 | tf_op jit(solution)/shard_map/all_to_all | solution.py:525
  237.0 13.7 %collective-permute-done.6 = f32[23,512]{1,0:T(8,128)} collective-permute-done((f32[23,512]{1,0:T(8,128)S(1)}, f32[23,512]{1,0:T(8,128)}, u32[]{:S(2)}, u32[]{:S(2)}) %collective-permute-start.6) | collective-permute-done | bytes 47136 | tf_op jit(solution)/shard_map/ppermute | solution.py:34
  254.1 7.1 %all-to-all-done.3 = bf16[128,8,512]{2,1,0:T(8,128)(2,1)} async-done(((bf16[128,8,512]{2,1,0:T(8,128)(2,1)}), bf16[128,8,512]{2,1,0:T(8,128)(2,1)}, u32[]{:S(2)}, u32[]{:S(2)}) %all-to-all-start.3) | async-done | bytes 1048608 | tf_op jit(solution)/shard_map/all_to_all | solution.py:525
  266.7 12.8 %all_gather.61 = bf16[2,128,512]{2,1,0:T(8,128)(2,1)S(1)} all-gather(bf16[1,128,512]{2,1,0:T(8,128)(2,1)S(1)} %fusion.25), channel_id=1, replica_groups=mesh['segment'=2,'rows'=128,'mp'=2] {'mp'}, dimensions={0}, use_global_device_ids=true | all-gather | bytes 393216 | tf_op jit(solution)/shard_map/all_gather | solution.py:546
  284.0 10.6 %all-to-all-start.4 = ((bf16[128,8,512]{2,1,0:T(8,128)(2,1)}), bf16[128,8,512]{2,1,0:T(8,128)(2,1)}, u32[]{:S(2)}, u32[]{:S(2)}) async-start(bf16[128,8,512]{2,1,0:T(8,128)(2,1)} %bitcast.66), calls=%async_computation.4 | async-start | bytes 2097152 | tf_op jit(solution)/shard_map/all_to_all | solution.py:485
  299.9 4.5 %collective-permute-start.9 = (bf16[64,512]{1,0:T(8,128)(2,1)S(1)}, bf16[64,512]{1,0:T(8,128)(2,1)S(1)}, u32[]{:S(2)}, u32[]{:S(2)}) collective-permute-start(bf16[64,512]{1,0:T(8,128)(2,1)S(1)} %fusion.1), channel_id=1, source_target_pairs={{256,257},{257,256},{258,259},{259,258},{260,261},{261,260},{262,2... | collective-permute-start | bytes 196616 | tf_op jit(solution)/shard_map/ppermute | solution.py:34
  312.5 4.7 %collective-permute-done.8 = bf16[16,512]{1,0:T(8,128)(2,1)S(1)} collective-permute-done((bf16[16,512]{1,0:T(8,128)(2,1)S(1)}, bf16[16,512]{1,0:T(8,128)(2,1)S(1)}, u32[]{:S(2)}, u32[]{:S(2)}) %collective-permute-start.8) | collective-permute-done | bytes 16416 | tf_op jit(solution)/shard_map/ppermute | solution.py:44
  317.2 6.0 %all-to-all-done.4 = bf16[128,8,512]{2,1,0:T(8,128)(2,1)} async-done(((bf16[128,8,512]{2,1,0:T(8,128)(2,1)}), bf16[128,8,512]{2,1,0:T(8,128)(2,1)}, u32[]{:S(2)}, u32[]{:S(2)}) %all-to-all-start.4) | async-done | bytes 1048608 | tf_op jit(solution)/shard_map/all_to_all | solution.py:485
  329.7 10.1 %all-to-all-start.5 = ((bf16[128,8,512]{2,1,0:T(8,128)(2,1)}), bf16[128,8,512]{2,1,0:T(8,128)(2,1)S(1)}, u32[]{:S(2)}, u32[]{:S(2)}) async-start(bf16[128,8,512]{2,1,0:T(8,128)(2,1)} %bitcast.62), calls=%async_computation.5 | async-start | bytes 2097152 | tf_op jit(solution)/shard_map/all_to_all | solution.py:525
  341.6 26.3 %all-to-all-done.5 = bf16[128,8,512]{2,1,0:T(8,128)(2,1)S(1)} async-done(((bf16[128,8,512]{2,1,0:T(8,128)(2,1)}), bf16[128,8,512]{2,1,0:T(8,128)(2,1)S(1)}, u32[]{:S(2)}, u32[]{:S(2)}) %all-to-all-start.5) | async-done | bytes 1048608 | tf_op jit(solution)/shard_map/all_to_all | solution.py:525
  372.3 12.9 %all_gather.65 = bf16[2,128,512]{2,1,0:T(8,128)(2,1)S(1)} all-gather(bf16[1,128,512]{2,1,0:T(8,128)(2,1)S(1)} %fusion.21), channel_id=1, replica_groups=mesh['segment'=2,'rows'=128,'mp'=2] {'mp'}, dimensions={0}, use_global_device_ids=true | all-gather | bytes 393216 | tf_op jit(solution)/shard_map/all_gather | solution.py:546
  392.7 5.8 %collective-permute-start.10 = (bf16[16,512]{1,0:T(8,128)(2,1)S(1)}, bf16[16,512]{1,0:T(8,128)(2,1)S(1)}, u32[]{:S(2)}, u32[]{:S(2)}) collective-permute-start(bf16[16,512]{1,0:T(8,128)(2,1)S(1)} %slice.181), channel_id=1, source_target_pairs={{256,258},{257,259},{258,260},{259,261},{260,262},{261,263},{262,2... | collective-permute-start | bytes 49160 | tf_op jit(solution)/shard_map/ppermute | solution.py:44
  401.2 6.5 %collective-permute-done.11 = bf16[16,512]{1,0:T(8,128)(2,1)S(1)} collective-permute-done((bf16[16,512]{1,0:T(8,128)(2,1)S(1)}, bf16[16,512]{1,0:T(8,128)(2,1)S(1)}, u32[]{:S(2)}, u32[]{:S(2)}) %collective-permute-start.11) | collective-permute-done | bytes 16416 | tf_op jit(solution)/shard_map/ppermute | solution.py:44
  (188 shorter events, 130.8 us)
Async XLA Ops:
  3.7 14.2 %collective-permute-start = (bf16[48,2048]{1,0:T(8,128)(2,1)}, bf16[48,2048]{1,0:T(8,128)(2,1)S(1)}, u32[]{:S(2)}, u32[]{:S(2)}) collective-permute-start(bf16[48,2048]{1,0:T(8,128)(2,1)} %get-tuple-element.32.mine_ref), channel_id=1, source_target_pairs={{0,1},{1,0},{2,3},{3,2},{4,5},{5,4},{6,7},{7,6},{8,9},{9,8},{10,11... | collective-permute-start | bytes 589832 | tf_op jit(solution)/shard_map/ppermute | solution.py:30
  8.5 58.5 %collective-permute-start.2 = (bf16[288,2048]{1,0:T(8,128)(2,1)}, bf16[288,2048]{1,0:T(8,128)(2,1)}, u32[]{:S(2)}, u32[]{:S(2)}) collective-permute-start(bf16[288,2048]{1,0:T(8,128)(2,1)} %get-tuple-element.41), channel_id=1, source_target_pairs={{0,1},{1,0},{2,3},{3,2},{4,5},{5,4},{6,7},{7,6},{8,9},{9,8},{10,11... | collective-permute-start | bytes 3538952 | tf_op jit(solution)/shard_map/ppermute | solution.py:30
  16.3 52.1 %copy-start.25 = (bf16[64,1024]{1,0:T(8,128)(2,1)}, bf16[64,1024]{1,0:T(8,128)(2,1)S(1)}, u32[]{:S(2)}) copy-start(bf16[64,1024]{1,0:T(8,128)(2,1)S(1)} %get-tuple-element.55.mask_ref) | copy-start | bytes 393220
  16.3 52.1 %copy-start.27 = (bf16[64,1024]{1,0:T(8,128)(2,1)}, bf16[64,1024]{1,0:T(8,128)(2,1)S(1)}, u32[]{:S(2)}) copy-start(bf16[64,1024]{1,0:T(8,128)(2,1)S(1)} %get-tuple-element.39.mask_ref) | copy-start | bytes 393220
  16.3 52.1 %copy-start.31 = (f32[64,128]{1,0:T(8,128)}, f32[64,128]{1,0:T(8,128)S(1)}, u32[]{:S(2)}) copy-start(f32[64,128]{1,0:T(8,128)S(1)} %get-tuple-element.54.hot_ref) | copy-start | bytes 98308
  16.3 52.1 %copy-start.33 = (f32[64,128]{1,0:T(8,128)}, f32[64,128]{1,0:T(8,128)S(1)}, u32[]{:S(2)}) copy-start(f32[64,128]{1,0:T(8,128)S(1)} %get-tuple-element.45.hot_ref) | copy-start | bytes 98308
  16.3 52.1 %copy-start.35 = (f32[64,128]{1,0:T(8,128)}, f32[64,128]{1,0:T(8,128)S(1)}, u32[]{:S(2)}) copy-start(f32[64,128]{1,0:T(8,128)S(1)} %get-tuple-element.37.hot_ref) | copy-start | bytes 98308
  20.5 82.5 %all-to-all-start = ((bf16[128,8,512]{2,1,0:T(8,128)(2,1)}), bf16[128,8,512]{2,1,0:T(8,128)(2,1)}, u32[]{:S(2)}, u32[]{:S(2)}) async-start(bf16[128,8,512]{2,1,0:T(8,128)(2,1)} %bitcast.68), calls=%async_computation | async-start | bytes 2097152 | tf_op jit(solution)/shard_map/all_to_all | solution.py:485
  109.5 42.3 %all-to-all-start.1 = ((bf16[128,8,512]{2,1,0:T(8,128)(2,1)}), bf16[128,8,512]{2,1,0:T(8,128)(2,1)}, u32[]{:S(2)}, u32[]{:S(2)}) async-start(bf16[128,8,512]{2,1,0:T(8,128)(2,1)} %bitcast.60), calls=%async_computation.1 | async-start | bytes 2097152 | tf_op jit(solution)/shard_map/all_to_all | solution.py:525
  121.2 20.9 %collective-permute-start.1 = (bf16[512,128]{1,0:T(8,128)(2,1)}, bf16[512,128]{1,0:T(8,128)(2,1)}, u32[]{:S(2)}, u32[]{:S(2)}) collective-permute-start(bf16[512,128]{1,0:T(8,128)(2,1)} %constant_dynamic-slice_fusion.2), channel_id=1, source_target_pairs={{0,1},{1,0},{2,3},{3,2},{4,5},{5,4},{6,7},{7,6},{8,9},{9,8},{10,11... | collective-permute-start | bytes 393224 | tf_op jit(solution)/shard_map/ppermute | solution.py:30
  174.9 39.1 %all-to-all-start.2 = ((bf16[128,8,512]{2,1,0:T(8,128)(2,1)}), bf16[128,8,512]{2,1,0:T(8,128)(2,1)}, u32[]{:S(2)}, u32[]{:S(2)}) async-start(bf16[128,8,512]{2,1,0:T(8,128)(2,1)} %bitcast.67), calls=%async_computation.2 | async-start | bytes 2097152 | tf_op jit(solution)/shard_map/all_to_all | solution.py:485
  190.8 18.7 %collective-permute-start.5 = (bf16[64,512]{1,0:T(8,128)(2,1)S(1)}, bf16[64,512]{1,0:T(8,128)(2,1)S(1)}, u32[]{:S(2)}, u32[]{:S(2)}) collective-permute-start(bf16[64,512]{1,0:T(8,128)(2,1)S(1)} %fusion), channel_id=1, source_target_pairs={{256,257},{257,256},{258,259},{259,258},{260,261},{261,260},{262,2... | collective-permute-start | bytes 196616 | tf_op jit(solution)/shard_map/ppermute | solution.py:34
  196.6 6.5 %collective-permute-start.3 = (bf16[16,512]{1,0:T(8,128)(2,1)S(1)}, bf16[16,512]{1,0:T(8,128)(2,1)S(1)}, u32[]{:S(2)}, u32[]{:S(2)}) collective-permute-start(bf16[16,512]{1,0:T(8,128)(2,1)S(1)} %slice.163), channel_id=1, source_target_pairs={{256,258},{257,259},{258,260},{259,261},{260,262},{261,263},{262,2... | collective-permute-start | bytes 49160 | tf_op jit(solution)/shard_map/ppermute | solution.py:44
  199.7 9.7 %collective-permute-start.4 = (bf16[16,512]{1,0:T(8,128)(2,1)S(1)}, bf16[16,512]{1,0:T(8,128)(2,1)S(1)}, u32[]{:S(2)}, u32[]{:S(2)}) collective-permute-start(bf16[16,512]{1,0:T(8,128)(2,1)S(1)} %slice.163), channel_id=1, source_target_pairs={{256,259},{257,258},{258,261},{259,260},{260,263},{261,262},{262,2... | collective-permute-start | bytes 49160 | tf_op jit(solution)/shard_map/ppermute | solution.py:44
  220.5 40.7 %all-to-all-start.3 = ((bf16[128,8,512]{2,1,0:T(8,128)(2,1)}), bf16[128,8,512]{2,1,0:T(8,128)(2,1)}, u32[]{:S(2)}, u32[]{:S(2)}) async-start(bf16[128,8,512]{2,1,0:T(8,128)(2,1)} %bitcast.61), calls=%async_computation.3 | async-start | bytes 2097152 | tf_op jit(solution)/shard_map/all_to_all | solution.py:525
  233.2 17.5 %collective-permute-start.6 = (f32[23,512]{1,0:T(8,128)S(1)}, f32[23,512]{1,0:T(8,128)}, u32[]{:S(2)}, u32[]{:S(2)}) collective-permute-start(f32[23,512]{1,0:T(8,128)S(1)} %concatenate.58), channel_id=1, source_target_pairs={{256,257},{257,256},{258,259},{259,258},{260,261},{261,260},{262,2... | collective-permute-start | bytes 141320 | tf_op jit(solution)/shard_map/ppermute | solution.py:34
  284.0 39.2 %all-to-all-start.4 = ((bf16[128,8,512]{2,1,0:T(8,128)(2,1)}), bf16[128,8,512]{2,1,0:T(8,128)(2,1)}, u32[]{:S(2)}, u32[]{:S(2)}) async-start(bf16[128,8,512]{2,1,0:T(8,128)(2,1)} %bitcast.66), calls=%async_computation.4 | async-start | bytes 2097152 | tf_op jit(solution)/shard_map/all_to_all | solution.py:485
  299.9 17.3 %collective-permute-start.9 = (bf16[64,512]{1,0:T(8,128)(2,1)S(1)}, bf16[64,512]{1,0:T(8,128)(2,1)S(1)}, u32[]{:S(2)}, u32[]{:S(2)}) collective-permute-start(bf16[64,512]{1,0:T(8,128)(2,1)S(1)} %fusion.1), channel_id=1, source_target_pairs={{256,257},{257,256},{258,259},{259,258},{260,261},{261,260},{262,2... | collective-permute-start | bytes 196616 | tf_op jit(solution)/shard_map/ppermute | solution.py:34
  304.4 8.1 %collective-permute-start.7 = (bf16[16,512]{1,0:T(8,128)(2,1)S(1)}, bf16[16,512]{1,0:T(8,128)(2,1)S(1)}, u32[]{:S(2)}, u32[]{:S(2)}) collective-permute-start(bf16[16,512]{1,0:T(8,128)(2,1)S(1)} %slice.172), channel_id=1, source_target_pairs={{256,258},{257,259},{258,260},{259,261},{260,262},{261,263},{262,2... | collective-permute-start | bytes 49160 | tf_op jit(solution)/shard_map/ppermute | solution.py:44
  307.5 9.7 %collective-permute-start.8 = (bf16[16,512]{1,0:T(8,128)(2,1)S(1)}, bf16[16,512]{1,0:T(8,128)(2,1)S(1)}, u32[]{:S(2)}, u32[]{:S(2)}) collective-permute-start(bf16[16,512]{1,0:T(8,128)(2,1)S(1)} %slice.172), channel_id=1, source_target_pairs={{256,259},{257,258},{258,261},{259,260},{260,263},{261,262},{262,2... | collective-permute-start | bytes 49160 | tf_op jit(solution)/shard_map/ppermute | solution.py:44
  329.7 38.2 %all-to-all-start.5 = ((bf16[128,8,512]{2,1,0:T(8,128)(2,1)}), bf16[128,8,512]{2,1,0:T(8,128)(2,1)S(1)}, u32[]{:S(2)}, u32[]{:S(2)}) async-start(bf16[128,8,512]{2,1,0:T(8,128)(2,1)} %bitcast.62), calls=%async_computation.5 | async-start | bytes 2097152 | tf_op jit(solution)/shard_map/all_to_all | solution.py:525
  388.2 19.5 %collective-permute-start.12 = (bf16[64,512]{1,0:T(8,128)(2,1)S(1)}, bf16[64,512]{1,0:T(8,128)(2,1)S(1)}, u32[]{:S(2)}, u32[]{:S(2)}) collective-permute-start(bf16[64,512]{1,0:T(8,128)(2,1)S(1)} %fusion.2), channel_id=1, source_target_pairs={{256,257},{257,256},{258,259},{259,258},{260,261},{261,260},{262,2... | collective-permute-start | bytes 196616 | tf_op jit(solution)/shard_map/ppermute | solution.py:34
  392.7 8.6 %collective-permute-start.10 = (bf16[16,512]{1,0:T(8,128)(2,1)S(1)}, bf16[16,512]{1,0:T(8,128)(2,1)S(1)}, u32[]{:S(2)}, u32[]{:S(2)}) collective-permute-start(bf16[16,512]{1,0:T(8,128)(2,1)S(1)} %slice.181), channel_id=1, source_target_pairs={{256,258},{257,259},{258,260},{259,261},{260,262},{261,263},{262,2... | collective-permute-start | bytes 49160 | tf_op jit(solution)/shard_map/ppermute | solution.py:44
  398.5 9.3 %collective-permute-start.11 = (bf16[16,512]{1,0:T(8,128)(2,1)S(1)}, bf16[16,512]{1,0:T(8,128)(2,1)S(1)}, u32[]{:S(2)}, u32[]{:S(2)}) collective-permute-start(bf16[16,512]{1,0:T(8,128)(2,1)S(1)} %slice.181), channel_id=1, source_target_pairs={{256,259},{257,258},{258,261},{259,260},{260,263},{261,262},{262,2... | collective-permute-start | bytes 49160 | tf_op jit(solution)/shard_map/ppermute | solution.py:44
  (44 other events, 426.3 us)

commit v7 on v6

--- a/solution.py
+++ b/solution.py
@@ -142,8 +142,12 @@
             gain_ref[2 * h + q : 2 * h + q + 1, :] = (terms[0:1] + terms[1:2]) + terms[2:3]
 
 
-def norm_kernel(depth, x_ref, gain_ref, pick_ref, out_ref, normed_out, normed_ref, held_ref, sems):
+def norm_kernel(
+    depth, x_ref, gain_ref, pick_ref, out_ref, normed_out, x_out, normed_ref, held_ref, sems
+):
     rows = x_ref.shape[0] // QUARTERS
+    keep = pltpu.make_async_copy(x_ref, x_out, sems.at[QUARTERS + 1])
+    keep.start()
     total = jnp.zeros((rows, 1), F32)
     for q in range(QUARTERS):
         part = x_ref[q * rows : (q + 1) * rows, :].astype(F32)
@@ -154,8 +158,8 @@
         normed_ref[q * rows : (q + 1) * rows, :] = (
             part * scale * gain_ref[q : q + 1, :]
         ).astype(BF16)
-    copies = [pltpu.make_async_copy(normed_ref, normed_out, sems.at[QUARTERS])]
-    copies[0].start()
+    copies = [keep, pltpu.make_async_copy(normed_ref, normed_out, sems.at[QUARTERS])]
+    copies[1].start()
     normed = normed_ref[...]
     size = pick_ref.shape[0] // QUARTERS
     for i in range(QUARTERS):
@@ -453,6 +457,16 @@
     frames = None
     voiced = []
 
+    def rendered_frames(x):
+        own = sum(
+            dot(x[q * rows : (q + 1) * rows], w_in[q * width : (q + 1) * width])
+            for q in range(QUARTERS)
+        ).astype(BF16)
+        last = own[-BACK:]
+        near = jnp.concatenate([voiced_pass(last, 0), own], axis=0)
+        far = jnp.concatenate([voiced_pass(last, 1), voiced_swap(own)], axis=0)
+        return jnp.concatenate([near, far], axis=1)
+
     def voice(frames):
         return call(
             functools.partial(vocoder_kernel, layers, kernel),
@@ -469,19 +483,25 @@
 
     for step in range(steps):
         hot, mask, pick = hots[step], masks[step], picks[step]
-        outgoing, normed = call(
+        outgoing, normed, x = call(
             functools.partial(norm_kernel, depth),
-            (HBM((slots * QUARTERS, width), BF16), HBM((QUARTERS * rows, width), BF16)),
+            (
+                HBM((slots * QUARTERS, width), BF16),
+                HBM((QUARTERS * rows, width), BF16),
+                HBM((QUARTERS * rows, width), BF16),
+            ),
             x,
             gain,
             pick,
             scratch=[
                 pltpu.VMEM((QUARTERS * rows, width), BF16),
                 pltpu.VMEM((QUARTERS, slots, width), BF16),
-                pltpu.SemaphoreType.DMA((QUARTERS + 1,)),
+                pltpu.SemaphoreType.DMA((QUARTERS + 2,)),
             ],
             flops=2 * slots * QUARTERS * QUARTERS * rows * width,
         )
+        if step > 0:
+            frames = rendered_frames(x)
         received = lax.all_to_all(
             outgoing.reshape(experts, per_device * QUARTERS, width),
             "rows",
@@ -548,14 +568,7 @@
         fresh = (mine + (total[0] + total[1])).astype(BF16)
         x = lax.all_gather(fresh, "segment", axis=0, tiled=True)
 
-        own = sum(
-            dot(x[q * rows : (q + 1) * rows], w_in[q * width : (q + 1) * width])
-            for q in range(QUARTERS)
-        ).astype(BF16)
-        last = own[-BACK:]
-        near = jnp.concatenate([voiced_pass(last, 0), own], axis=0)
-        far = jnp.concatenate([voiced_pass(last, 1), voiced_swap(own)], axis=0)
-        frames = jnp.concatenate([near, far], axis=1)
+    frames = rendered_frames(x)
     voiced.append(voice(frames))
     audio = jnp.stack([v.reshape(2 * rows) for v in voiced], axis=0)
     audio = jnp.where(seg == 0, jnp.zeros_like(audio), audio)[None]

time: 412 us -> 411 us (level)
    unnamed x100 -> x94, local copies, waits for them, and re-layouts: 19.7 us -> 17.6 us
where the time goes in v7:
time: 411 us; the launch traced here: 409 us
  waiting for transfers between devices  146 us (36%)
  starting transfers between devices  124 us (30%)
  blocking collectives  67.4 us (16%)
  Pallas kernels  32.6 us (8%)
  local copies, waits for them, and re-layouts  21.1 us (5%)
  matrix products  11.2 us (3%)
    ppermute x3, waiting for transfers between devices, swapped(): return lax.ppermute(block, axis, [(0, 1), (1, 0)])  46.1 us
    all_to_all x3, starting transfers between devices, on_device(): lax.all_to_all(outgoing.reshape(experts, per_device * QUARTERS, width), '...  41.8 us
    all_gather x3, blocking collectives, on_device(): total = lax.all_gather(chip, 'mp', axis=0).astype(F32)  38.3 us
    all_to_all x3, waiting for transfers between devices, on_device(): lax.all_to_all(outgoing.reshape(experts, per_device * QUARTERS, width), '...  34.9 us
    all_to_all x3, waiting for transfers between devices, on_device(): lax.all_to_all(answer.reshape(experts, per_device * QUARTERS, width), 'ro...  33.4 us
    all_to_all x3, starting transfers between devices, on_device(): lax.all_to_all(answer.reshape(experts, per_device * QUARTERS, width), 'ro...  32.7 us
    pallas_call x18, Pallas kernels, call(): pl.pallas_call(kernel, out_shape=outs, in_specs=specs, out_specs=out_spec...  32.6 us
    ppermute x6, starting transfers between devices, voiced_pass(): return lax.ppermute(block, ('segment', 'rows', 'mp'), route)  19 us
  transfers between devices with their start and end apart: 19, of which 14 were waited for; matrix products, arithmetic and copies ran while one was open for 4% of the time, Pallas kernels for 2%

profile of v7, /device:TPU:31, one launch (start us, length us, event | category | flops | bytes accessed | tf_op | source)
XLA Modules:
  0.0 408.9 jit_solution(5137291292385686865)
XLA Ops:
  3.7 4.8 %collective-permute-start = (bf16[48,2048]{1,0:T(8,128)(2,1)}, bf16[48,2048]{1,0:T(8,128)(2,1)S(1)}, u32[]{:S(2)}, u32[]{:S(2)}) collective-permute-start(bf16[48,2048]{1,0:T(8,128)(2,1)} %get-tuple-element.35.mine_ref), channel_id=1, source_target_pairs={{0,1},{1,0},{2,3},{3,2},{4,5},{5,4},{6,7},{7,6},{8,9},{9,8},{10,11... | collective-permute-start | bytes 589832 | tf_op jit(solution)/shard_map/ppermute | solution.py:30
  20.4 20.4 %all-to-all-start = ((bf16[128,8,512]{2,1,0:T(8,128)(2,1)}), bf16[128,8,512]{2,1,0:T(8,128)(2,1)}, u32[]{:S(2)}, u32[]{:S(2)}) async-start(bf16[128,8,512]{2,1,0:T(8,128)(2,1)} %bitcast.68), calls=%async_computation | async-start | bytes 2097152 | tf_op jit(solution)/shard_map/all_to_all | solution.py:505
  40.9 26.1 %collective-permute-done.2 = bf16[288,2048]{1,0:T(8,128)(2,1)} collective-permute-done((bf16[288,2048]{1,0:T(8,128)(2,1)}, bf16[288,2048]{1,0:T(8,128)(2,1)}, u32[]{:S(2)}, u32[]{:S(2)}) %collective-permute-start.2) | collective-permute-done | bytes 1179680 | tf_op jit(solution)/shard_map/ppermute | solution.py:30
  68.4 4.8 %all_gather.52.gate2_ref = bf16[192,2048]{1,0:T(8,128)(2,1)S(1)} all-gather(bf16[96,2048]{1,0:T(8,128)(2,1)S(1)} %get-tuple-element.76), channel_id=1, replica_groups=mesh['segment'=2,'rows'=128,'mp'=2] {'segment'}, dimensions={0}, use_global_device_ids=true | all-gather | bytes 1179648 | tf_op jit(solution)/shard_map/all_gather | solution.py:320
  77.9 25.0 %all-to-all-done = bf16[128,8,512]{2,1,0:T(8,128)(2,1)} async-done(((bf16[128,8,512]{2,1,0:T(8,128)(2,1)}), bf16[128,8,512]{2,1,0:T(8,128)(2,1)}, u32[]{:S(2)}, u32[]{:S(2)}) %all-to-all-start) | async-done | bytes 1048608 | tf_op jit(solution)/shard_map/all_to_all | solution.py:505
  109.4 10.2 %all-to-all-start.1 = ((bf16[128,8,512]{2,1,0:T(8,128)(2,1)}), bf16[128,8,512]{2,1,0:T(8,128)(2,1)}, u32[]{:S(2)}, u32[]{:S(2)}) async-start(bf16[128,8,512]{2,1,0:T(8,128)(2,1)} %bitcast.60), calls=%async_computation.1 | async-start | bytes 2097152 | tf_op jit(solution)/shard_map/all_to_all | solution.py:545
  124.5 17.5 %collective-permute-done.1 = bf16[512,128]{1,0:T(8,128)(2,1)} collective-permute-done((bf16[512,128]{1,0:T(8,128)(2,1)}, bf16[512,128]{1,0:T(8,128)(2,1)}, u32[]{:S(2)}, u32[]{:S(2)}) %collective-permute-start.1) | collective-permute-done | bytes 131104 | tf_op jit(solution)/shard_map/ppermute | solution.py:30
  157.9 12.6 %all_gather.57 = bf16[2,128,512]{2,1,0:T(8,128)(2,1)S(1)} all-gather(bf16[1,128,512]{2,1,0:T(8,128)(2,1)S(1)} %fusion.29), channel_id=1, replica_groups=mesh['segment'=2,'rows'=128,'mp'=2] {'mp'}, dimensions={0}, use_global_device_ids=true | all-gather | bytes 393216 | tf_op jit(solution)/shard_map/all_gather | solution.py:566
  174.2 10.7 %all-to-all-start.2 = ((bf16[128,8,512]{2,1,0:T(8,128)(2,1)}), bf16[128,8,512]{2,1,0:T(8,128)(2,1)}, u32[]{:S(2)}, u32[]{:S(2)}) async-start(bf16[128,8,512]{2,1,0:T(8,128)(2,1)} %bitcast.67), calls=%async_computation.2 | async-start | bytes 2097152 | tf_op jit(solution)/shard_map/all_to_all | solution.py:505
  190.1 5.9 %collective-permute-start.5 = (bf16[64,512]{1,0:T(8,128)(2,1)S(1)}, bf16[64,512]{1,0:T(8,128)(2,1)S(1)}, u32[]{:S(2)}, u32[]{:S(2)}) collective-permute-start(bf16[64,512]{1,0:T(8,128)(2,1)S(1)} %fusion), channel_id=1, source_target_pairs={{256,257},{257,256},{258,259},{259,258},{260,261},{261,260},{262,2... | collective-permute-start | bytes 196616 | tf_op jit(solution)/shard_map/ppermute | solution.py:34
  202.5 6.3 %collective-permute-done.4 = bf16[16,512]{1,0:T(8,128)(2,1)S(1)} collective-permute-done((bf16[16,512]{1,0:T(8,128)(2,1)S(1)}, bf16[16,512]{1,0:T(8,128)(2,1)S(1)}, u32[]{:S(2)}, u32[]{:S(2)}) %collective-permute-start.4) | collective-permute-done | bytes 16416 | tf_op jit(solution)/shard_map/ppermute | solution.py:44
  219.9 12.5 %all-to-all-start.3 = ((bf16[128,8,512]{2,1,0:T(8,128)(2,1)}), bf16[128,8,512]{2,1,0:T(8,128)(2,1)}, u32[]{:S(2)}, u32[]{:S(2)}) async-start(bf16[128,8,512]{2,1,0:T(8,128)(2,1)} %bitcast.61), calls=%async_computation.3 | async-start | bytes 2097152 | tf_op jit(solution)/shard_map/all_to_all | solution.py:545
  236.4 13.7 %collective-permute-done.6 = f32[23,512]{1,0:T(8,128)} collective-permute-done((f32[23,512]{1,0:T(8,128)S(1)}, f32[23,512]{1,0:T(8,128)}, u32[]{:S(2)}, u32[]{:S(2)}) %collective-permute-start.6) | collective-permute-done | bytes 47136 | tf_op jit(solution)/shard_map/ppermute | solution.py:34
  253.5 7.1 %all-to-all-done.3 = bf16[128,8,512]{2,1,0:T(8,128)(2,1)} async-done(((bf16[128,8,512]{2,1,0:T(8,128)(2,1)}), bf16[128,8,512]{2,1,0:T(8,128)(2,1)}, u32[]{:S(2)}, u32[]{:S(2)}) %all-to-all-start.3) | async-done | bytes 1048608 | tf_op jit(solution)/shard_map/all_to_all | solution.py:545
  266.1 12.8 %all_gather.61 = bf16[2,128,512]{2,1,0:T(8,128)(2,1)S(1)} all-gather(bf16[1,128,512]{2,1,0:T(8,128)(2,1)S(1)} %fusion.25), channel_id=1, replica_groups=mesh['segment'=2,'rows'=128,'mp'=2] {'mp'}, dimensions={0}, use_global_device_ids=true | all-gather | bytes 393216 | tf_op jit(solution)/shard_map/all_gather | solution.py:566
  282.7 10.7 %all-to-all-start.4 = ((bf16[128,8,512]{2,1,0:T(8,128)(2,1)}), bf16[128,8,512]{2,1,0:T(8,128)(2,1)}, u32[]{:S(2)}, u32[]{:S(2)}) async-start(bf16[128,8,512]{2,1,0:T(8,128)(2,1)} %bitcast.66), calls=%async_computation.4 | async-start | bytes 2097152 | tf_op jit(solution)/shard_map/all_to_all | solution.py:505
  298.6 4.5 %collective-permute-start.9 = (bf16[64,512]{1,0:T(8,128)(2,1)S(1)}, bf16[64,512]{1,0:T(8,128)(2,1)S(1)}, u32[]{:S(2)}, u32[]{:S(2)}) collective-permute-start(bf16[64,512]{1,0:T(8,128)(2,1)S(1)} %fusion.1), channel_id=1, source_target_pairs={{256,257},{257,256},{258,259},{259,258},{260,261},{261,260},{262,2... | collective-permute-start | bytes 196616 | tf_op jit(solution)/shard_map/ppermute | solution.py:34
  311.2 4.7 %collective-permute-done.8 = bf16[16,512]{1,0:T(8,128)(2,1)S(1)} collective-permute-done((bf16[16,512]{1,0:T(8,128)(2,1)S(1)}, bf16[16,512]{1,0:T(8,128)(2,1)S(1)}, u32[]{:S(2)}, u32[]{:S(2)}) %collective-permute-start.8) | collective-permute-done | bytes 16416 | tf_op jit(solution)/shard_map/ppermute | solution.py:44
  315.9 6.0 %all-to-all-done.4 = bf16[128,8,512]{2,1,0:T(8,128)(2,1)} async-done(((bf16[128,8,512]{2,1,0:T(8,128)(2,1)}), bf16[128,8,512]{2,1,0:T(8,128)(2,1)}, u32[]{:S(2)}, u32[]{:S(2)}) %all-to-all-start.4) | async-done | bytes 1048608 | tf_op jit(solution)/shard_map/all_to_all | solution.py:505
  328.4 10.1 %all-to-all-start.5 = ((bf16[128,8,512]{2,1,0:T(8,128)(2,1)}), bf16[128,8,512]{2,1,0:T(8,128)(2,1)S(1)}, u32[]{:S(2)}, u32[]{:S(2)}) async-start(bf16[128,8,512]{2,1,0:T(8,128)(2,1)} %bitcast.62), calls=%async_computation.5 | async-start | bytes 2097152 | tf_op jit(solution)/shard_map/all_to_all | solution.py:545
  340.3 26.3 %all-to-all-done.5 = bf16[128,8,512]{2,1,0:T(8,128)(2,1)S(1)} async-done(((bf16[128,8,512]{2,1,0:T(8,128)(2,1)}), bf16[128,8,512]{2,1,0:T(8,128)(2,1)S(1)}, u32[]{:S(2)}, u32[]{:S(2)}) %all-to-all-start.5) | async-done | bytes 1048608 | tf_op jit(solution)/shard_map/all_to_all | solution.py:545
  371.0 12.9 %all_gather.65 = bf16[2,128,512]{2,1,0:T(8,128)(2,1)S(1)} all-gather(bf16[1,128,512]{2,1,0:T(8,128)(2,1)S(1)} %fusion.21), channel_id=1, replica_groups=mesh['segment'=2,'rows'=128,'mp'=2] {'mp'}, dimensions={0}, use_global_device_ids=true | all-gather | bytes 393216 | tf_op jit(solution)/shard_map/all_gather | solution.py:566
  391.4 5.8 %collective-permute-start.10 = (bf16[16,512]{1,0:T(8,128)(2,1)S(1)}, bf16[16,512]{1,0:T(8,128)(2,1)S(1)}, u32[]{:S(2)}, u32[]{:S(2)}) collective-permute-start(bf16[16,512]{1,0:T(8,128)(2,1)S(1)} %slice.173), channel_id=1, source_target_pairs={{256,258},{257,259},{258,260},{259,261},{260,262},{261,263},{262,2... | collective-permute-start | bytes 49160 | tf_op jit(solution)/shard_map/ppermute | solution.py:44
  400.0 6.5 %collective-permute-done.11 = bf16[16,512]{1,0:T(8,128)(2,1)S(1)} collective-permute-done((bf16[16,512]{1,0:T(8,128)(2,1)S(1)}, bf16[16,512]{1,0:T(8,128)(2,1)S(1)}, u32[]{:S(2)}, u32[]{:S(2)}) %collective-permute-start.11) | collective-permute-done | bytes 16416 | tf_op jit(solution)/shard_map/ppermute | solution.py:44
  (182 shorter events, 129.4 us)
Async XLA Ops:
  3.7 14.2 %collective-permute-start = (bf16[48,2048]{1,0:T(8,128)(2,1)}, bf16[48,2048]{1,0:T(8,128)(2,1)S(1)}, u32[]{:S(2)}, u32[]{:S(2)}) collective-permute-start(bf16[48,2048]{1,0:T(8,128)(2,1)} %get-tuple-element.35.mine_ref), channel_id=1, source_target_pairs={{0,1},{1,0},{2,3},{3,2},{4,5},{5,4},{6,7},{7,6},{8,9},{9,8},{10,11... | collective-permute-start | bytes 589832 | tf_op jit(solution)/shard_map/ppermute | solution.py:30
  8.5 58.5 %collective-permute-start.2 = (bf16[288,2048]{1,0:T(8,128)(2,1)}, bf16[288,2048]{1,0:T(8,128)(2,1)}, u32[]{:S(2)}, u32[]{:S(2)}) collective-permute-start(bf16[288,2048]{1,0:T(8,128)(2,1)} %get-tuple-element.45), channel_id=1, source_target_pairs={{0,1},{1,0},{2,3},{3,2},{4,5},{5,4},{6,7},{7,6},{8,9},{9,8},{10,11... | collective-permute-start | bytes 3538952 | tf_op jit(solution)/shard_map/ppermute | solution.py:30
  15.5 52.9 %copy-start.31 = (bf16[1024,256]{1,0:T(8,128)(2,1)}, bf16[1024,256]{1,0:T(8,128)(2,1)S(1)}, u32[]{:S(2)}) copy-start(bf16[1024,256]{1,0:T(8,128)(2,1)S(1)} %get-tuple-element.56.pick_ref) | copy-start | bytes 1572868
  20.4 82.5 %all-to-all-start = ((bf16[128,8,512]{2,1,0:T(8,128)(2,1)}), bf16[128,8,512]{2,1,0:T(8,128)(2,1)}, u32[]{:S(2)}, u32[]{:S(2)}) async-start(bf16[128,8,512]{2,1,0:T(8,128)(2,1)} %bitcast.68), calls=%async_computation | async-start | bytes 2097152 | tf_op jit(solution)/shard_map/all_to_all | solution.py:505
  68.3 34.6 %copy-start = (bf16[1,2048,192]{1,2,0:T(8,128)(2,1)S(1)}, bf16[1,2048,192]{1,2,0:T(8,128)(2,1)}, u32[]{:S(2)}) copy-start(bf16[1,2048,192]{1,2,0:T(8,128)(2,1)} %param.17) | copy-start | bytes 2359300
  109.4 42.3 %all-to-all-start.1 = ((bf16[128,8,512]{2,1,0:T(8,128)(2,1)}), bf16[128,8,512]{2,1,0:T(8,128)(2,1)}, u32[]{:S(2)}, u32[]{:S(2)}) async-start(bf16[128,8,512]{2,1,0:T(8,128)(2,1)} %bitcast.60), calls=%async_computation.1 | async-start | bytes 2097152 | tf_op jit(solution)/shard_map/all_to_all | solution.py:545
  121.2 20.9 %collective-permute-start.1 = (bf16[512,128]{1,0:T(8,128)(2,1)}, bf16[512,128]{1,0:T(8,128)(2,1)}, u32[]{:S(2)}, u32[]{:S(2)}) collective-permute-start(bf16[512,128]{1,0:T(8,128)(2,1)} %constant_dynamic-slice_fusion.2), channel_id=1, source_target_pairs={{0,1},{1,0},{2,3},{3,2},{4,5},{5,4},{6,7},{7,6},{8,9},{9,8},{10,11... | collective-permute-start | bytes 393224 | tf_op jit(solution)/shard_map/ppermute | solution.py:30
  174.2 39.1 %all-to-all-start.2 = ((bf16[128,8,512]{2,1,0:T(8,128)(2,1)}), bf16[128,8,512]{2,1,0:T(8,128)(2,1)}, u32[]{:S(2)}, u32[]{:S(2)}) async-start(bf16[128,8,512]{2,1,0:T(8,128)(2,1)} %bitcast.67), calls=%async_computation.2 | async-start | bytes 2097152 | tf_op jit(solution)/shard_map/all_to_all | solution.py:505
  184.9 16.2 %copy-start.8 = (bf16[2048,128]{1,0:T(8,128)(2,1)S(1)}, bf16[2048,128]{1,0:T(8,128)(2,1)}, u32[]{:S(2)}) copy-start(bf16[2048,128]{1,0:T(8,128)(2,1)} %copy-done.7) | copy-start | bytes 1572868
  190.1 18.7 %collective-permute-start.5 = (bf16[64,512]{1,0:T(8,128)(2,1)S(1)}, bf16[64,512]{1,0:T(8,128)(2,1)S(1)}, u32[]{:S(2)}, u32[]{:S(2)}) collective-permute-start(bf16[64,512]{1,0:T(8,128)(2,1)S(1)} %fusion), channel_id=1, source_target_pairs={{256,257},{257,256},{258,259},{259,258},{260,261},{261,260},{262,2... | collective-permute-start | bytes 196616 | tf_op jit(solution)/shard_map/ppermute | solution.py:34
  196.0 6.4 %collective-permute-start.3 = (bf16[16,512]{1,0:T(8,128)(2,1)S(1)}, bf16[16,512]{1,0:T(8,128)(2,1)S(1)}, u32[]{:S(2)}, u32[]{:S(2)}) collective-permute-start(bf16[16,512]{1,0:T(8,128)(2,1)S(1)} %slice.159), channel_id=1, source_target_pairs={{256,258},{257,259},{258,260},{259,261},{260,262},{261,263},{262,2... | collective-permute-start | bytes 49160 | tf_op jit(solution)/shard_map/ppermute | solution.py:44
  199.1 9.7 %collective-permute-start.4 = (bf16[16,512]{1,0:T(8,128)(2,1)S(1)}, bf16[16,512]{1,0:T(8,128)(2,1)S(1)}, u32[]{:S(2)}, u32[]{:S(2)}) collective-permute-start(bf16[16,512]{1,0:T(8,128)(2,1)S(1)} %slice.159), channel_id=1, source_target_pairs={{256,259},{257,258},{258,261},{259,260},{260,263},{261,262},{262,2... | collective-permute-start | bytes 49160 | tf_op jit(solution)/shard_map/ppermute | solution.py:44
  219.9 40.7 %all-to-all-start.3 = ((bf16[128,8,512]{2,1,0:T(8,128)(2,1)}), bf16[128,8,512]{2,1,0:T(8,128)(2,1)}, u32[]{:S(2)}, u32[]{:S(2)}) async-start(bf16[128,8,512]{2,1,0:T(8,128)(2,1)} %bitcast.61), calls=%async_computation.3 | async-start | bytes 2097152 | tf_op jit(solution)/shard_map/all_to_all | solution.py:545
  232.6 17.5 %collective-permute-start.6 = (f32[23,512]{1,0:T(8,128)S(1)}, f32[23,512]{1,0:T(8,128)}, u32[]{:S(2)}, u32[]{:S(2)}) collective-permute-start(f32[23,512]{1,0:T(8,128)S(1)} %concatenate.58), channel_id=1, source_target_pairs={{256,257},{257,256},{258,259},{259,258},{260,261},{261,260},{262,2... | collective-permute-start | bytes 141320 | tf_op jit(solution)/shard_map/ppermute | solution.py:34
  282.7 39.2 %all-to-all-start.4 = ((bf16[128,8,512]{2,1,0:T(8,128)(2,1)}), bf16[128,8,512]{2,1,0:T(8,128)(2,1)}, u32[]{:S(2)}, u32[]{:S(2)}) async-start(bf16[128,8,512]{2,1,0:T(8,128)(2,1)} %bitcast.66), calls=%async_computation.4 | async-start | bytes 2097152 | tf_op jit(solution)/shard_map/all_to_all | solution.py:505
  298.6 17.3 %collective-permute-start.9 = (bf16[64,512]{1,0:T(8,128)(2,1)S(1)}, bf16[64,512]{1,0:T(8,128)(2,1)S(1)}, u32[]{:S(2)}, u32[]{:S(2)}) collective-permute-start(bf16[64,512]{1,0:T(8,128)(2,1)S(1)} %fusion.1), channel_id=1, source_target_pairs={{256,257},{257,256},{258,259},{259,258},{260,261},{261,260},{262,2... | collective-permute-start | bytes 196616 | tf_op jit(solution)/shard_map/ppermute | solution.py:34
  303.1 8.1 %collective-permute-start.7 = (bf16[16,512]{1,0:T(8,128)(2,1)S(1)}, bf16[16,512]{1,0:T(8,128)(2,1)S(1)}, u32[]{:S(2)}, u32[]{:S(2)}) collective-permute-start(bf16[16,512]{1,0:T(8,128)(2,1)S(1)} %slice.164), channel_id=1, source_target_pairs={{256,258},{257,259},{258,260},{259,261},{260,262},{261,263},{262,2... | collective-permute-start | bytes 49160 | tf_op jit(solution)/shard_map/ppermute | solution.py:44
  306.2 9.7 %collective-permute-start.8 = (bf16[16,512]{1,0:T(8,128)(2,1)S(1)}, bf16[16,512]{1,0:T(8,128)(2,1)S(1)}, u32[]{:S(2)}, u32[]{:S(2)}) collective-permute-start(bf16[16,512]{1,0:T(8,128)(2,1)S(1)} %slice.164), channel_id=1, source_target_pairs={{256,259},{257,258},{258,261},{259,260},{260,263},{261,262},{262,2... | collective-permute-start | bytes 49160 | tf_op jit(solution)/shard_map/ppermute | solution.py:44
  328.4 38.3 %copy-start.15 = (bf16[128,1024]{1,0:T(8,128)(2,1)S(1)}, bf16[128,1024]{1,0:T(8,128)(2,1)}, u32[]{:S(2)}) copy-start(bf16[128,1024]{1,0:T(8,128)(2,1)} %copy-done.14) | copy-start | bytes 786436
  328.4 38.2 %all-to-all-start.5 = ((bf16[128,8,512]{2,1,0:T(8,128)(2,1)}), bf16[128,8,512]{2,1,0:T(8,128)(2,1)S(1)}, u32[]{:S(2)}, u32[]{:S(2)}) async-start(bf16[128,8,512]{2,1,0:T(8,128)(2,1)} %bitcast.62), calls=%async_computation.5 | async-start | bytes 2097152 | tf_op jit(solution)/shard_map/all_to_all | solution.py:545
  367.4 16.6 %copy-start.37 = (bf16[256,512]{1,0:T(8,128)(2,1)S(1)}, bf16[256,512]{1,0:T(8,128)(2,1)}, u32[]{:S(2)}) copy-start(bf16[256,512]{1,0:T(8,128)(2,1)} %get-tuple-element.57) | copy-start | bytes 786436
  387.0 19.5 %collective-permute-start.12 = (bf16[64,512]{1,0:T(8,128)(2,1)S(1)}, bf16[64,512]{1,0:T(8,128)(2,1)S(1)}, u32[]{:S(2)}, u32[]{:S(2)}) collective-permute-start(bf16[64,512]{1,0:T(8,128)(2,1)S(1)} %fusion.2), channel_id=1, source_target_pairs={{256,257},{257,256},{258,259},{259,258},{260,261},{261,260},{262,2... | collective-permute-start | bytes 196616 | tf_op jit(solution)/shard_map/ppermute | solution.py:34
  391.4 8.6 %collective-permute-start.10 = (bf16[16,512]{1,0:T(8,128)(2,1)S(1)}, bf16[16,512]{1,0:T(8,128)(2,1)S(1)}, u32[]{:S(2)}, u32[]{:S(2)}) collective-permute-start(bf16[16,512]{1,0:T(8,128)(2,1)S(1)} %slice.173), channel_id=1, source_target_pairs={{256,258},{257,259},{258,260},{259,261},{260,262},{261,263},{262,2... | collective-permute-start | bytes 49160 | tf_op jit(solution)/shard_map/ppermute | solution.py:44
  397.2 9.3 %collective-permute-start.11 = (bf16[16,512]{1,0:T(8,128)(2,1)S(1)}, bf16[16,512]{1,0:T(8,128)(2,1)S(1)}, u32[]{:S(2)}, u32[]{:S(2)}) collective-permute-start(bf16[16,512]{1,0:T(8,128)(2,1)S(1)} %slice.173), channel_id=1, source_target_pairs={{256,259},{257,258},{258,261},{259,260},{260,263},{261,262},{262,2... | collective-permute-start | bytes 49160 | tf_op jit(solution)/shard_map/ppermute | solution.py:44
  (41 other events, 288.1 us)
